TPU v7x, 512 devices: a whole 4x4x16 slice. The times are simulated.
512 devices in a mesh: dp: 4 (over z_hi), tm: 4 (over x), space: 32 (over z_lo, y, core).
Axes of the slice: x: 4, y: 4, z: 16 (z_hi: 4, z_lo: 4; z = z_hi * 4 + z_lo), core: 2. Of those that a mesh axis runs over, the one named last changes fastest.
Arguments:
- q_spatial: bfloat16 [4, 8, 2048, 1152], P('dp', 'tm', 'space'), may hold values from -6 to 6
- k_spatial: bfloat16 [4, 8, 2048, 1152], P('dp', 'tm', 'space'), may hold values from -6 to 6
- v_spatial: bfloat16 [4, 8, 2048, 1152], P('dp', 'tm', 'space'), may hold values from -6 to 6
- grad_spatial: bfloat16 [4, 8, 2048, 1152], P('dp', 'tm', 'space'), may hold values from -6 to 6
- q_temporal: bfloat16 [4, 8, 2048, 1152], P('dp', 'tm', 'space'), may hold values from -6 to 6
- k_temporal: bfloat16 [4, 8, 2048, 1152], P('dp', 'tm', 'space'), may hold values from -6 to 6
- v_temporal: bfloat16 [4, 8, 2048, 1152], P('dp', 'tm', 'space'), may hold values from -6 to 6
- grad_out: bfloat16 [4, 8, 2048, 1152], P('dp', 'tm', 'space'), may hold values from -6 to 6
- w_tout: bfloat16 [1152, 1152], P('dp', 'tm'), may hold values from -0.1875 to 0.1875
Outputs:
- dq_spatial: bfloat16 [4, 8, 2048, 1152], P('dp', 'tm', 'space')
- dk_spatial: bfloat16 [4, 8, 2048, 1152], P('dp', 'tm', 'space')
- dv_spatial: bfloat16 [4, 8, 2048, 1152], P('dp', 'tm', 'space')
- dq_temporal: bfloat16 [4, 8, 2048, 1152], P('dp', 'tm', 'space')
- dk_temporal: bfloat16 [4, 8, 2048, 1152], P('dp', 'tm', 'space')
- dv_temporal: bfloat16 [4, 8, 2048, 1152], P('dp', 'tm', 'space')
- d_w_tout: float32 [1152, 1152], P('dp', 'tm')
All inputs are finite; a program needn't handle non-finite values.
Results may differ from a plain program's by a relative error of at most 0.015.
Values may be sent and summed in bfloat16 or wider, within the bound.
No kernel may reach another device: no remote copies, remote signals or barrier semaphores. Data moves between devices by JAX's collectives and lax.ppermute only.
A program may use at most 64 MiB of HBM per device.

v0:
```python
import math

import jax
import jax.numpy as jnp
from jax import lax
from jax.sharding import PartitionSpec as P

HEADS = 16
HDIM = 72


def item_back(queries, keys_in, values, out_grad):
    length, head_dim = queries.shape
    block_rows = min(512, length)
    blocks = length // block_rows
    scale = 1.0 / math.sqrt(head_dim)
    query_blocks = queries.reshape(blocks, block_rows, head_dim)
    grad_blocks = out_grad.reshape(blocks, block_rows, head_dim)
    contract_last = (((1,), (1,)), ((), ()))
    contract_first = (((0,), (0,)), ((), ()))

    def step(carry, pair):
        key_total, value_total = carry
        query_block, grad_block = pair
        scores = (
            lax.dot_general(query_block, keys_in, contract_last, preferred_element_type=jnp.float32)
            * scale
        )
        peak = jnp.max(scores, axis=1, keepdims=True)
        raised = jnp.exp(scores - peak)
        weights = raised / jnp.sum(raised, axis=1, keepdims=True)
        prob_grad = lax.dot_general(
            grad_block, values, contract_last, preferred_element_type=jnp.float32
        )
        inner = jnp.sum(weights * prob_grad, axis=1, keepdims=True)
        score_low = (weights * (prob_grad - inner)).astype(jnp.bfloat16)
        weight_low = weights.astype(jnp.bfloat16)
        value_total = value_total + lax.dot_general(
            weight_low, grad_block, contract_first, preferred_element_type=jnp.float32
        )
        key_total = key_total + lax.dot_general(
            score_low, query_block, contract_first, preferred_element_type=jnp.float32
        )
        query_grad = (
            jnp.dot(score_low, keys_in, preferred_element_type=jnp.float32) * scale
        ).astype(jnp.bfloat16)
        return ((key_total, value_total), query_grad)

    zeros = jnp.zeros((length, head_dim), jnp.float32)
    totals, query_grad = lax.scan(step, (zeros, zeros), (query_blocks, grad_blocks))
    return (
        query_grad.reshape(length, head_dim),
        (totals[0] * scale).astype(jnp.bfloat16),
        totals[1].astype(jnp.bfloat16),
    )


def spatial_work(parts):
    results = jax.vmap(item_back)(parts[0][0], parts[1][0], parts[2][0], parts[3][0])
    return (results[0][None], results[1][None], results[2][None])


def frames_back(queries, keys_in, values, out_grad):
    scale = 1.0 / math.sqrt(queries.shape[-1])
    scores = (
        jnp.einsum("fthd,gthd->thfg", queries, keys_in, preferred_element_type=jnp.float32) * scale
    )
    peak = jnp.max(scores, axis=-1, keepdims=True)
    raised = jnp.exp(scores - peak)
    weights = raised / jnp.sum(raised, axis=-1, keepdims=True)
    prob_grad = jnp.einsum("fthd,gthd->thfg", out_grad, values, preferred_element_type=jnp.float32)
    inner = jnp.sum(weights * prob_grad, axis=-1, keepdims=True)
    score_low = (weights * (prob_grad - inner)).astype(jnp.bfloat16)
    weight_low = weights.astype(jnp.bfloat16)
    query_grad = (
        jnp.einsum("thfg,gthd->fthd", score_low, keys_in, preferred_element_type=jnp.float32)
        * scale
    )
    key_grad = (
        jnp.einsum("thfg,fthd->gthd", score_low, queries, preferred_element_type=jnp.float32)
        * scale
    )
    value_grad = jnp.einsum(
        "thfg,fthd->gthd", weight_low, out_grad, preferred_element_type=jnp.float32
    )
    output = jnp.einsum("thfg,gthd->fthd", weight_low, values, preferred_element_type=jnp.float32)
    return (
        query_grad.astype(jnp.bfloat16),
        key_grad.astype(jnp.bfloat16),
        value_grad.astype(jnp.bfloat16),
        output.astype(jnp.bfloat16),
    )


def to_items(field, groups):
    frames_here, tokens = (field.shape[1], field.shape[2])
    items = field.reshape(frames_here, tokens, HEADS, HDIM).transpose(0, 2, 1, 3)
    return items.reshape(groups, frames_here * HEADS // groups, tokens, HDIM)


def from_items(field, frames_here):
    tokens = field.shape[2]
    return (
        field.reshape(frames_here, HEADS, tokens, HDIM)
        .transpose(0, 2, 1, 3)
        .reshape(1, frames_here, tokens, HEADS * HDIM)
    )


def shards(
    q_spatial,
    k_spatial,
    v_spatial,
    grad_spatial,
    q_temporal,
    k_temporal,
    v_temporal,
    grad_out,
    w_tout,
):
    frames_here = q_spatial.shape[1]
    groups = lax.axis_size("space")
    spatial = spatial_work(
        (
            lax.all_to_all(
                to_items(q_spatial, groups), "space", split_axis=0, concat_axis=2, tiled=True
            ),
            lax.all_to_all(
                to_items(k_spatial, groups), "space", split_axis=0, concat_axis=2, tiled=True
            ),
            lax.all_to_all(
                to_items(v_spatial, groups), "space", split_axis=0, concat_axis=2, tiled=True
            ),
            lax.all_to_all(
                to_items(grad_spatial, groups), "space", split_axis=0, concat_axis=2, tiled=True
            ),
        )
    )
    returned = (
        lax.all_to_all(spatial[0], "space", split_axis=2, concat_axis=0, tiled=True),
        lax.all_to_all(spatial[1], "space", split_axis=2, concat_axis=0, tiled=True),
        lax.all_to_all(spatial[2], "space", split_axis=2, concat_axis=0, tiled=True),
    )
    heads_in = (
        lax.all_to_all(q_temporal, "tm", split_axis=3, concat_axis=1, tiled=True),
        lax.all_to_all(k_temporal, "tm", split_axis=3, concat_axis=1, tiled=True),
        lax.all_to_all(v_temporal, "tm", split_axis=3, concat_axis=1, tiled=True),
    )
    grad_all = lax.all_gather(grad_out, "tm", axis=1, tiled=True)
    width = grad_out.shape[3]
    all_frames = grad_all.shape[1]
    tokens = grad_all.shape[2]
    grad_rows = grad_all.reshape(all_frames * tokens, width)
    local_width = w_tout.shape[1]
    local_heads = local_width // HDIM
    columns = grad_rows
    head_grad = jnp.dot(
        columns,
        lax.all_gather(w_tout, "dp", axis=0, tiled=True),
        preferred_element_type=jnp.float32,
    )

    def head_split(field):
        return field.reshape(all_frames, tokens, local_heads, HDIM)

    def head_join(field):
        return field.reshape(1, all_frames, tokens, local_width)

    results = frames_back(
        head_split(heads_in[0]),
        head_split(heads_in[1]),
        head_split(heads_in[2]),
        head_split(head_grad.astype(jnp.bfloat16)),
    )
    back = (
        lax.all_to_all(head_join(results[0]), "tm", split_axis=1, concat_axis=3, tiled=True),
        lax.all_to_all(head_join(results[1]), "tm", split_axis=1, concat_axis=3, tiled=True),
        lax.all_to_all(head_join(results[2]), "tm", split_axis=1, concat_axis=3, tiled=True),
    )
    output_rows = results[3].reshape(all_frames * tokens, local_width)
    weight_scale = 1.0 / math.sqrt(
        grad_out.shape[0] * lax.axis_size("dp") * all_frames * tokens * lax.axis_size("space")
    )
    contract_first = (((0,), (0,)), ((), ()))
    own_rows = w_tout.shape[0]
    columns = grad_rows
    whole = lax.psum(
        lax.dot_general(columns, output_rows, contract_first, preferred_element_type=jnp.float32)
        * weight_scale,
        ("dp", "space"),
    )
    weight_grad = lax.dynamic_slice_in_dim(whole, lax.axis_index("dp") * own_rows, own_rows, 0)
    return (
        from_items(returned[0], frames_here),
        from_items(returned[1], frames_here),
        from_items(returned[2], frames_here),
        back[0],
        back[1],
        back[2],
        weight_grad,
    )


def solution(mesh):
    return jax.shard_map(
        shards,
        mesh=mesh,
        in_specs=(
            P("dp", "tm", "space", None),
            P("dp", "tm", "space", None),
            P("dp", "tm", "space", None),
            P("dp", "tm", "space", None),
            P("dp", "tm", "space", None),
            P("dp", "tm", "space", None),
            P("dp", "tm", "space", None),
            P("dp", "tm", "space", None),
            P("dp", "tm"),
        ),
        out_specs=(
            P("dp", "tm", "space", None),
            P("dp", "tm", "space", None),
            P("dp", "tm", "space", None),
            P("dp", "tm", "space", None),
            P("dp", "tm", "space", None),
            P("dp", "tm", "space", None),
            P("dp", "tm"),
        ),
        check_vma=False,
    )
```

profile of v0, /device:TPU:1, one launch (start us, length us, event | category | flops | bytes accessed | tf_op | source)
XLA Modules:
  0.0 686.2 jit_solution(4775447620865652827)
XLA Ops:
  7.2 1.6 copy.141
  9.9 5.0 all-to-all-start.8
  14.9 1.5 copy.139
  17.6 3.0 all-to-all-done.8
  20.6 3.5 all-to-all-start.7
  26.0 3.8 all-to-all-done.7
  29.8 3.5 all-to-all-start.9
  35.1 3.7 all-to-all-done.9
  38.9 13.3 %all-to-all-start = ((bf16[32,1,64,72]{3,2,1,0:T(8,128)(2,1)}), bf16[32,1,64,72]{3,2,1,0:T(8,128)(2,1)}, u32[]{:S(2)}, u32[]{:S(2)}) async-start(bf16[32,1,64,72]{3,2,1,0:T(8,128)(2,1)} %bitcast.1), calls=%async_computation | async-start | bytes 1048576 | tf_op jit(solution)/shard_map/all_to_all | solution.py:125
  54.1 14.5 %all-to-all-done = bf16[32,1,64,72]{3,2,1,0:T(8,128)(2,1)} async-done(((bf16[32,1,64,72]{3,2,1,0:T(8,128)(2,1)}), bf16[32,1,64,72]{3,2,1,0:T(8,128)(2,1)}, u32[]{:S(2)}, u32[]{:S(2)}) %all-to-all-start) | async-done | bytes 294944 | tf_op jit(solution)/shard_map/all_to_all | solution.py:125
  68.7 4.1 all-to-all-start.1
  75.5 13.7 %all-to-all-done.1 = bf16[32,1,64,72]{3,2,1,0:T(8,128)(2,1)S(1)} async-done(((bf16[32,1,64,72]{3,2,1,0:T(8,128)(2,1)}), bf16[32,1,64,72]{3,2,1,0:T(8,128)(2,1)S(1)}, u32[]{:S(2)}, u32[]{:S(2)}) %all-to-all-start.1) | async-done | bytes 294944 | tf_op jit(solution)/shard_map/all_to_all | solution.py:128
  89.2 4.4 all-to-all-start.2
  95.6 35.7 %all_gather.7 = bf16[1152,288]{1,0:T(8,128)(2,1)S(1)} all-gather(bf16[288,288]{1,0:T(8,128)(2,1)S(1)} %copy-done.18), channel_id=1, replica_groups=mesh['dp'=4,'tm'=4,'space'=32] {'dp'}, dimensions={0}, use_global_device_ids=true | all-gather | bytes 829440 | tf_op jit(solution)/shard_map/all_gather | solution.py:159
  135.5 1.4 reshape.209
  137.7 4.0 fusion.56
  141.7 22.8 %all-to-all-start.3 = ((bf16[32,1,64,72]{3,2,1,0:T(8,128)(2,1)}), bf16[32,1,64,72]{3,2,1,0:T(8,128)(2,1)}, u32[]{:S(2)}, u32[]{:S(2)}) async-start(bf16[32,1,64,72]{3,2,1,0:T(8,128)(2,1)} %bitcast.12), calls=%async_computation.3 | async-start | bytes 1048576 | tf_op jit(solution)/shard_map/all_to_all | solution.py:131
  164.6 1.9 convolution_convert_fusion.2
  166.7 1.8 copy.148
  168.5 2.2 multiply_reduce_fusion.2
  173.1 7.7 %all-to-all-done.3 = bf16[32,1,64,72]{3,2,1,0:T(8,128)(2,1)} async-done(((bf16[32,1,64,72]{3,2,1,0:T(8,128)(2,1)}), bf16[32,1,64,72]{3,2,1,0:T(8,128)(2,1)}, u32[]{:S(2)}, u32[]{:S(2)}) %all-to-all-start.3) | async-done | bytes 294944 | tf_op jit(solution)/shard_map/all_to_all | solution.py:131
  180.8 3.5 all-to-all-start.10
  186.1 6.6 all-to-all-done.10
  192.7 3.5 all-to-all-start.11
  196.2 1.8 fusion.34
  199.4 4.4 all-to-all-done.11
  203.8 4.1 all-to-all-start.12
  207.9 53.5 %while.15 = (s32[]{:T(128)}, f32[1,2048,72]{1,2,0:T(8,128)S(1)}, f32[1,2048,72]{1,2,0:T(8,128)}, bf16[4,1,512,72]{2,3,1,0:T(8,128)(2,1)S(1)}, bf16[4,1,512,72]{3...) while((s32[]{:T(128)}, f32[1,2048,72]{1,2,0:T(8,128)S(1)}, ...), condition=%wide.region_4.5_spmd.clone, body=%wide.region_0.4_spmd.clone.sunk | while | flops 776608256 | bytes 56752292 | solution.py:50
  207.9 1.7 multiply_reduce_fusion.5
  210.5 3.0 multiply_reduce_fusion.6
  213.4 1.4 multiply_convert_fusion.4
  214.8 1.5 fusion.88
  216.3 4.1 fusion.89
  221.2 1.7 multiply_reduce_fusion.5
  223.7 3.0 multiply_reduce_fusion.6
  226.7 1.4 multiply_convert_fusion.4
  228.1 1.5 fusion.88
  229.6 4.3 fusion.89
  234.6 1.7 multiply_reduce_fusion.5
  237.1 3.0 multiply_reduce_fusion.6
  240.1 1.4 multiply_convert_fusion.4
  241.5 1.5 fusion.88
  243.0 4.3 fusion.89
  248.0 1.7 multiply_reduce_fusion.5
  250.5 3.0 multiply_reduce_fusion.6
  253.5 1.4 multiply_convert_fusion.4
  254.9 1.5 fusion.88
  256.4 4.3 fusion.89
  262.5 11.5 %reduce.6 = bf16[2048,72]{1,0:T(8,128)(2,1)S(1)} reduce(bf16[2048,1,1,72]{3,2,1,0:T(2,128)(2,1)S(1)} %bitcast.186, bf16[]{:T(256)} %broadcast.60), dimensions={1,2}, to_apply=%bitcast.129.reduce_sub_computation | reduce | bytes 589826
  274.1 1.8 reshape.202
  275.9 15.4 %all-to-all-start.4 = ((bf16[32,2,2304]{2,1,0:T(2,128)(2,1)}), bf16[32,2,2304]{2,1,0:T(2,128)(2,1)S(1)}, u32[]{:S(2)}, u32[]{:S(2)}) async-start(bf16[32,2,2304]{2,1,0:T(2,128)(2,1)} %reshape.202), calls=%async_computation.4 | async-start | bytes 589824 | tf_op jit(solution)/shard_map/all_to_all | solution.py:140
  292.1 11.5 %reduce.7 = bf16[2048,72]{1,0:T(8,128)(2,1)S(1)} reduce(bf16[2048,1,1,72]{3,2,1,0:T(2,128)(2,1)S(1)} %bitcast.188, bf16[]{:T(256)} %broadcast.60), dimensions={1,2}, to_apply=%bitcast.131.reduce_sub_computation | reduce | bytes 589826
  303.7 1.8 reshape.204
  305.5 7.7 %all-to-all-start.5 = ((bf16[32,2,2304]{2,1,0:T(2,128)(2,1)}), bf16[32,2,2304]{2,1,0:T(2,128)(2,1)S(1)}, u32[]{:S(2)}, u32[]{:S(2)}) async-start(bf16[32,2,2304]{2,1,0:T(2,128)(2,1)} %reshape.204), calls=%async_computation.5 | async-start | bytes 589824 | tf_op jit(solution)/shard_map/all_to_all | solution.py:141
  313.9 11.5 %reduce.8 = bf16[2048,72]{1,0:T(8,128)(2,1)S(1)} reduce(bf16[2048,1,1,72]{3,2,1,0:T(2,128)(2,1)S(1)} %bitcast.187, bf16[]{:T(256)} %broadcast.60), dimensions={1,2}, to_apply=%bitcast.133.reduce_sub_computation | reduce | bytes 589826
  325.5 1.8 reshape.206
  327.3 7.8 %all-to-all-start.6 = ((bf16[32,2,2304]{2,1,0:T(2,128)(2,1)}), bf16[32,2,2304]{2,1,0:T(2,128)(2,1)}, u32[]{:S(2)}, u32[]{:S(2)}) async-start(bf16[32,2,2304]{2,1,0:T(2,128)(2,1)} %reshape.206), calls=%async_computation.6 | async-start | bytes 589824 | tf_op jit(solution)/shard_map/all_to_all | solution.py:142
  335.4 2.7 fusion.35
  338.1 1.9 copy.165
  340.4 1.6 fusion.27
  347.0 1.8 reshape.203
  352.2 1.8 reshape.205
  357.4 3.2 reshape.207
  364.1 312.7 %all-reduce.2.cloned.1.call-done = f32[1152,288]{0,1:T(8,128)} async-done(((f32[1152,288]{0,1:T(8,128)}), f32[1152,288]{0,1:T(8,128)}) %all-reduce.2.cloned.1.call-update) | async-done | bytes 1327120 | tf_op jit(solution)/shard_map/psum | solution.py:187
  (128 shorter events, 50.1 us)
Async XLA Ops:
  7.2 16.9 %copy-start.12 = (bf16[1,2,64,1152]{3,2,1,0:T(8,128)(2,1)S(1)}, bf16[1,2,64,1152]{3,2,1,0:T(8,128)(2,1)}, u32[]{:S(2)}) copy-start(bf16[1,2,64,1152]{3,2,1,0:T(8,128)(2,1)} %param.17) | copy-start | bytes 884740
  7.2 26.0 %copy-start.13 = (bf16[1,2,64,1152]{3,2,1,0:T(8,128)(2,1)S(1)}, bf16[1,2,64,1152]{3,2,1,0:T(8,128)(2,1)}, u32[]{:S(2)}) copy-start(bf16[1,2,64,1152]{3,2,1,0:T(8,128)(2,1)} %param.11) | copy-start | bytes 884740
  9.9 42.3 %copy-start.14 = (bf16[1,2,64,1152]{3,2,1,0:T(8,128)(2,1)S(1)}, bf16[1,2,64,1152]{3,2,1,0:T(8,128)(2,1)}, u32[]{:S(2)}) copy-start(bf16[1,2,64,1152]{3,2,1,0:T(8,128)(2,1)} %param.12) | copy-start | bytes 884740
  9.9 10.7 %all-to-all-start.8 = ((bf16[4,2,18432]{2,1,0:T(2,128)(2,1)}), bf16[4,2,18432]{2,1,0:T(2,128)(2,1)S(1)}, u32[]{:S(2)}, u32[]{:S(2)}) async-start(bf16[4,2,18432]{2,1,0:T(2,128)(2,1)} %reshape.210), calls=%async_computation.8 | async-start | bytes 589824 | tf_op jit(solution)/shard_map/all_to_all | solution.py:146
  20.6 9.1 %all-to-all-start.7 = ((bf16[4,2,18432]{2,1,0:T(2,128)(2,1)}), bf16[4,2,18432]{2,1,0:T(2,128)(2,1)S(1)}, u32[]{:S(2)}, u32[]{:S(2)}) async-start(bf16[4,2,18432]{2,1,0:T(2,128)(2,1)} %reshape.212), calls=%async_computation.7 | async-start | bytes 589824 | tf_op jit(solution)/shard_map/all_to_all | solution.py:145
  24.1 49.5 %copy-start.15 = (bf16[1,2,64,1152]{3,2,1,0:T(8,128)(2,1)S(1)}, bf16[1,2,64,1152]{3,2,1,0:T(8,128)(2,1)}, u32[]{:S(2)}) copy-start(bf16[1,2,64,1152]{3,2,1,0:T(8,128)(2,1)} %param.14) | copy-start | bytes 884740
  29.8 43.1 %copy-start.7 = (bf16[4,2,18432]{2,1,0:T(2,128)(2,1)}, bf16[4,2,18432]{2,1,0:T(2,128)(2,1)S(1)}, u32[]{:S(2)}) copy-start(bf16[4,2,18432]{2,1,0:T(2,128)(2,1)S(1)} %all-to-all-done.7) | copy-start | bytes 884740
  29.8 9.1 %all-to-all-start.9 = ((bf16[4,2,18432]{2,1,0:T(2,128)(2,1)}), bf16[4,2,18432]{2,1,0:T(2,128)(2,1)S(1)}, u32[]{:S(2)}, u32[]{:S(2)}) async-start(bf16[4,2,18432]{2,1,0:T(2,128)(2,1)} %reshape.208), calls=%async_computation.9 | async-start | bytes 589824 | tf_op jit(solution)/shard_map/all_to_all | solution.py:147
  34.2 59.5 %copy-start.16 = (bf16[1,2,64,1152]{3,2,1,0:T(8,128)(2,1)S(1)}, bf16[1,2,64,1152]{3,2,1,0:T(8,128)(2,1)}, u32[]{:S(2)}) copy-start(bf16[1,2,64,1152]{3,2,1,0:T(8,128)(2,1)} %param.13) | copy-start | bytes 884740
  38.9 34.0 %copy-start.8 = (bf16[4,2,18432]{2,1,0:T(2,128)(2,1)}, bf16[4,2,18432]{2,1,0:T(2,128)(2,1)S(1)}, u32[]{:S(2)}) copy-start(bf16[4,2,18432]{2,1,0:T(2,128)(2,1)S(1)} %all-to-all-done.9) | copy-start | bytes 884740
  38.9 29.8 %all-to-all-start = ((bf16[32,1,64,72]{3,2,1,0:T(8,128)(2,1)}), bf16[32,1,64,72]{3,2,1,0:T(8,128)(2,1)}, u32[]{:S(2)}, u32[]{:S(2)}) async-start(bf16[32,1,64,72]{3,2,1,0:T(8,128)(2,1)} %bitcast.1), calls=%async_computation | async-start | bytes 1048576 | tf_op jit(solution)/shard_map/all_to_all | solution.py:125
  52.2 43.3 %copy-start.18 = (bf16[288,288]{1,0:T(8,128)(2,1)S(1)}, bf16[288,288]{1,0:T(8,128)(2,1)}, u32[]{:S(2)}) copy-start(bf16[288,288]{1,0:T(8,128)(2,1)} %param.19) | copy-start | bytes 497668
  68.7 20.6 %all-to-all-start.1 = ((bf16[32,1,64,72]{3,2,1,0:T(8,128)(2,1)}), bf16[32,1,64,72]{3,2,1,0:T(8,128)(2,1)S(1)}, u32[]{:S(2)}, u32[]{:S(2)}) async-start(bf16[32,1,64,72]{3,2,1,0:T(8,128)(2,1)} %bitcast.5), calls=%async_computation.1 | async-start | bytes 1048576 | tf_op jit(solution)/shard_map/all_to_all | solution.py:128
  72.8 91.7 %all-gather.2.cloned.1.call-start = ((), (), s32[]{:S(2)}) async-start(), calls=%async_computation.13 | async-start | bytes 1474560 | tf_op jit(solution)/shard_map/all_gather | solution.py:149
  89.2 52.5 %all-to-all-start.2 = ((bf16[32,1,64,72]{3,2,1,0:T(8,128)(2,1)}), bf16[32,1,64,72]{3,2,1,0:T(8,128)(2,1)}, u32[]{:S(2)}, u32[]{:S(2)}) async-start(bf16[32,1,64,72]{3,2,1,0:T(8,128)(2,1)} %bitcast.8), calls=%async_computation.2 | async-start | bytes 1048576 | tf_op jit(solution)/shard_map/all_to_all | solution.py:134
  137.7 30.8 %copy-start.11 = (bf16[8,64,4,72]{3,2,1,0:T(4,128)(2,1)}, bf16[8,64,4,72]{3,2,1,0:T(4,128)(2,1)S(1)}, u32[]{:S(2)}) copy-start(bf16[8,64,4,72]{3,2,1,0:T(4,128)(2,1)S(1)} %reshape.192) | copy-start | bytes 884740
  141.7 39.1 %all-to-all-start.3 = ((bf16[32,1,64,72]{3,2,1,0:T(8,128)(2,1)}), bf16[32,1,64,72]{3,2,1,0:T(8,128)(2,1)}, u32[]{:S(2)}, u32[]{:S(2)}) async-start(bf16[32,1,64,72]{3,2,1,0:T(8,128)(2,1)} %bitcast.12), calls=%async_computation.3 | async-start | bytes 1048576 | tf_op jit(solution)/shard_map/all_to_all | solution.py:131
  166.4 4.4 copy-start.19
  168.5 2.3 copy-start.9
  168.5 2.6 copy-start.2
  171.2 25.0 %copy-start.20 = (f32[64,4,8]{2,1,0:T(4,128)S(1)}, f32[64,4,8]{2,1,0:T(4,128)}, u32[]{:S(2)}) copy-start(f32[64,4,8]{2,1,0:T(4,128)} %get-tuple-element.152) | copy-start | bytes 24580
  180.8 11.9 %all-to-all-start.10 = ((bf16[1,8,64,288]{3,2,0,1:T(8,128)(2,1)}), bf16[1,8,64,288]{3,2,0,1:T(8,128)(2,1)S(1)}, u32[]{:S(2)}, u32[]{:S(2)}) async-start(bf16[1,8,64,288]{3,2,0,1:T(8,128)(2,1)} %bitcast.28), calls=%async_computation.10 | async-start | bytes 786432 | tf_op jit(solution)/shard_map/all_to_all | solution.py:176
  185.0 22.9 %copy-start.17 = (bf16[4,1,512,72]{2,3,1,0:T(8,128)(2,1)S(1)}, bf16[4,1,512,72]{2,3,1,0:T(8,128)(2,1)}, u32[]{:S(2)}) copy-start(bf16[4,1,512,72]{2,3,1,0:T(8,128)(2,1)} %custom-call.2) | copy-start | bytes 884740
  192.7 15.2 %copy-start.3 = (bf16[1,8,64,288]{3,2,0,1:T(8,128)(2,1)}, bf16[1,8,64,288]{3,2,0,1:T(8,128)(2,1)S(1)}, u32[]{:S(2)}) copy-start(bf16[1,8,64,288]{3,2,0,1:T(8,128)(2,1)S(1)} %all-to-all-done.10) | copy-start | bytes 884740
  192.7 11.0 %all-to-all-start.11 = ((bf16[1,8,64,288]{3,2,0,1:T(8,128)(2,1)}), bf16[1,8,64,288]{3,2,0,1:T(8,128)(2,1)S(1)}, u32[]{:S(2)}, u32[]{:S(2)}) async-start(bf16[1,8,64,288]{3,2,0,1:T(8,128)(2,1)} %bitcast.32), calls=%async_computation.11 | async-start | bytes 786432 | tf_op jit(solution)/shard_map/all_to_all | solution.py:177
  203.8 4.1 copy-start.5
  203.8 72.1 %all-to-all-start.12 = ((bf16[1,8,64,288]{3,2,0,1:T(8,128)(2,1)}), bf16[1,8,64,288]{3,2,0,1:T(8,128)(2,1)}, u32[]{:S(2)}, u32[]{:S(2)}) async-start(bf16[1,8,64,288]{3,2,0,1:T(8,128)(2,1)} %bitcast.36), calls=%async_computation.12 | async-start | bytes 786432 | tf_op jit(solution)/shard_map/all_to_all | solution.py:178
  209.6 3.8 copy-start
  222.9 3.8 copy-start
  236.3 3.8 copy-start
  249.7 3.8 copy-start
  261.4 29.8 %copy-start.10 = (f32[1,2048,72]{1,2,0:T(8,128)S(1)}, f32[1,2048,72]{1,2,0:T(8,128)}, u32[]{:S(2)}) copy-start(f32[1,2048,72]{1,2,0:T(8,128)} %get-tuple-element.53) | copy-start | bytes 1769476
  275.9 29.6 %all-to-all-start.4 = ((bf16[32,2,2304]{2,1,0:T(2,128)(2,1)}), bf16[32,2,2304]{2,1,0:T(2,128)(2,1)S(1)}, u32[]{:S(2)}, u32[]{:S(2)}) async-start(bf16[32,2,2304]{2,1,0:T(2,128)(2,1)} %reshape.202), calls=%async_computation.4 | async-start | bytes 589824 | tf_op jit(solution)/shard_map/all_to_all | solution.py:140
  291.4 44.0 %copy-start.21 = (f32[64,4,8]{2,1,0:T(4,128)S(1)}, f32[64,4,8]{2,1,0:T(4,128)}, u32[]{:S(2)}) copy-start(f32[64,4,8]{2,1,0:T(4,128)} %get-tuple-element.152) | copy-start | bytes 24580
  305.5 21.8 %all-to-all-start.5 = ((bf16[32,2,2304]{2,1,0:T(2,128)(2,1)}), bf16[32,2,2304]{2,1,0:T(2,128)(2,1)S(1)}, u32[]{:S(2)}, u32[]{:S(2)}) async-start(bf16[32,2,2304]{2,1,0:T(2,128)(2,1)} %reshape.204), calls=%async_computation.5 | async-start | bytes 589824 | tf_op jit(solution)/shard_map/all_to_all | solution.py:141
  325.5 14.9 %copy-start.1 = (bf16[1,8,64,1152]{3,2,0,1:T(8,128)(2,1)S(1)}, bf16[1,8,64,1152]{3,2,0,1:T(8,128)(2,1)}, u32[]{:S(2)}) copy-start(bf16[1,8,64,1152]{3,2,0,1:T(8,128)(2,1)} %all-gather.2.cloned.1.call-done) | copy-start | bytes 3538948
  327.3 30.1 %all-to-all-start.6 = ((bf16[32,2,2304]{2,1,0:T(2,128)(2,1)}), bf16[32,2,2304]{2,1,0:T(2,128)(2,1)}, u32[]{:S(2)}, u32[]{:S(2)}) async-start(bf16[32,2,2304]{2,1,0:T(2,128)(2,1)} %reshape.206), calls=%async_computation.6 | async-start | bytes 589824 | tf_op jit(solution)/shard_map/all_to_all | solution.py:142
  335.1 6.9 %copy-start.4 = (bf16[1,8,64,288]{3,2,0,1:T(8,128)(2,1)S(1)}, bf16[1,8,64,288]{3,2,0,1:T(8,128)(2,1)}, u32[]{:S(2)}) copy-start(bf16[1,8,64,288]{3,2,0,1:T(8,128)(2,1)} %copy-done.3) | copy-start | bytes 884740
  335.1 341.7 %all-reduce.2.cloned.1.call-start = ((), (), s32[]{:S(2)}) async-start(), calls=%async_computation.14 | async-start | bytes 2654208 | tf_op jit(solution)/shard_map/psum | solution.py:187
  338.1 5.3 copy-start.6
Sparse Core Ops, SparseCore 0:
  75.8 30.7 all-gather.1
  342.1 334.5 all-reduce.1
where the time goes:
time: 696 us; the launch traced here: 686 us
  waiting for transfers between devices  371 us (53%)
  starting transfers between devices  98.8 us (14%)
  local copies, waits for them, and re-layouts  61.7 us (9%)
  matrix products  59.8 us (9%)
  other arithmetic  43.9 us (6%)
  blocking collectives  35.7 us (5%)
  between operations  15.2 us (2%)
    psum x1, waiting for transfers between devices, shards(): lax.psum(lax.dot_general(columns, output_rows, contract_first, preferred_...  313 us
    all_gather x1, blocking collectives, shards(): lax.all_gather(w_tout, 'dp', axis=0, tiled=True)  35.7 us
    unnamed x5, other arithmetic  34.6 us
    unnamed x59, local copies, waits for them, and re-layouts  24.3 us
    all_to_all x1, starting transfers between devices, shards(): lax.all_to_all(to_items(v_spatial, groups), 'space', split_axis=0, concat...  22.8 us
    dot_general x4, matrix products, step(): lax.dot_general(weight_low, grad_block, contract_first, preferred_element...  16.9 us
    all_to_all x1, starting transfers between devices, shards(): lax.all_to_all(spatial[0], 'space', split_axis=2, concat_axis=0, tiled=True)  15.4 us
    all_to_all x1, waiting for transfers between devices, shards(): lax.all_to_all(to_items(q_spatial, groups), 'space', split_axis=0, concat...  14.5 us
  transfers between devices with their start and end apart: 15, of which 9 were waited for; matrix products, arithmetic and copies ran while one was open for 23% of the time, Pallas kernels for 0%

commit v1 on v0

v1 whole, which is shorter than its diff:
```python
import math
import functools
import jax
import jax.numpy as jnp
from jax import lax
from jax.experimental import pallas as pl
from jax.experimental.pallas import tpu as pltpu
from jax.sharding import PartitionSpec as P

HEADS = 16
HDIM = 72
LANES = 128
HALF = 64
FOLD = 40
F32 = jnp.float32
BF16 = jnp.bfloat16
LIMIT = 56 * 1024 * 1024
LAST = (((1,), (1,)), ((), ()))


def vmem_specs(count):
    return [pl.BlockSpec(memory_space=pltpu.VMEM)] * count


def low_lanes(rows):
    return lax.broadcasted_iota(jnp.int32, (rows, LANES), 1) < HALF


def swap(block):
    return pltpu.roll(block, HALF, 1)


def pack_kernel(q_ref, k_ref, v_ref, g_ref, out_ref):
    for frame in range(2):
        for pair, (first, second) in enumerate(((q_ref, k_ref), (v_ref, g_ref))):
            rows = jnp.concatenate([first[frame], second[frame]], axis=0).astype(F32)
            columns = rows.T
            for head in range(HEADS):
                out_ref[frame * HEADS + head, pair] = columns[
                    head * HDIM : (head + 1) * HDIM
                ].astype(BF16)


def pack(q, k, v, g):
    return pl.pallas_call(
        pack_kernel,
        out_shape=jax.ShapeDtypeStruct((2 * HEADS, 2, HDIM, LANES), BF16),
        in_specs=vmem_specs(4),
        out_specs=pl.BlockSpec(memory_space=pltpu.VMEM),
        compiler_params=pltpu.CompilerParams(vmem_limit_bytes=LIMIT),
        name="spatial_pack",
    )(q, k, v, g)


def attend_kernel(
    in_ref, out_ref, q_t, k_t, g_t, q_n, k_n, v_n, g_n, s_buf, p_buf, dq_t, dk_n, dv_n, *, step
):
    length = q_t.shape[1]
    pairs = length // LANES
    scale = 1.0 / math.sqrt(HDIM)
    power = scale * math.log2(math.e)

    def split(j, pair):
        first = in_ref[2 * j, pair].astype(F32)
        second = in_ref[2 * j + 1, pair].astype(F32)
        low = low_lanes(HDIM)
        return (
            jnp.where(low, first, swap(second)),
            jnp.where(low, swap(first), second),
        )

    for j in range(pairs):
        at = slice(j * LANES, (j + 1) * LANES)
        q, k = split(j, 0)
        v, g = split(j, 1)
        q_t[:, at] = q.astype(BF16)
        k_t[:, at] = k.astype(BF16)
        g_t[:, at] = g.astype(BF16)
        q_n[at, :] = q.T.astype(BF16)
        k_n[at, :] = k.T.astype(BF16)
        v_n[at, :] = v.T.astype(BF16)
        g_n[at, :] = g.T.astype(BF16)

    blocks = length // step

    def products(i, slot):
        at = pl.ds(pl.multiple_of(i * step, step), step)
        s_buf[slot] = jnp.dot(k_n[...], q_t[:, at], preferred_element_type=F32)
        p_buf[slot] = jnp.dot(v_n[...], g_t[:, at], preferred_element_type=F32)

    def rest(i, slot, first):
        at = pl.ds(pl.multiple_of(i * step, step), step)
        scores = s_buf[slot]
        peak = jnp.max(scores, axis=0, keepdims=True)
        raised = jnp.exp2((scores - peak) * power)
        over = 1.0 / jnp.sum(raised, axis=0, keepdims=True)
        grads = p_buf[slot]
        inner = jnp.sum(raised * grads, axis=0, keepdims=True) * over
        weights = raised * over
        low_w = weights.astype(BF16)
        low_s = (weights * (grads - inner)).astype(BF16)
        dv = jnp.dot(low_w, g_n[at, :], preferred_element_type=F32)
        dk = jnp.dot(low_s, q_n[at, :], preferred_element_type=F32)
        if first:
            dv_n[...] = dv
            dk_n[...] = dk
        else:
            dv_n[...] += dv
            dk_n[...] += dk
        dq_t[:, at] = jnp.dot(k_t[...], low_s, preferred_element_type=F32) * scale

    products(0, 0)
    products(1, 1)
    rest(0, 0, True)

    def body(i, _):
        slot = lax.rem(i, 2)
        products(i + 1, 1 - slot)
        rest(i, slot, False)
        return 0

    lax.fori_loop(1, blocks - 1, body, 0)
    rest(blocks - 1, (blocks - 1) % 2, False)

    for j in range(pairs):
        at = slice(j * LANES, (j + 1) * LANES)
        dq = dq_t[:, at]
        dk = (dk_n[at, :] * scale).T
        dv = dv_n[at, :].T
        low = low_lanes(HDIM)
        low_f = low_lanes(FOLD)
        upper, lower = dv[:FOLD], dv[HDIM - FOLD :]
        out_ref[2 * j] = jnp.concatenate(
            [jnp.where(low, dq, swap(dk)), jnp.where(low_f, upper, swap(lower))], axis=0
        ).astype(BF16)
        out_ref[2 * j + 1] = jnp.concatenate(
            [jnp.where(low, swap(dq), dk), jnp.where(low_f, swap(upper), lower)], axis=0
        ).astype(BF16)


def attend(received, step=256):
    sources = received.shape[0]
    length = sources * HALF
    wide = pltpu.VMEM((HDIM, length), BF16)
    tall = pltpu.VMEM((length, HDIM), BF16)
    return pl.pallas_call(
        functools.partial(attend_kernel, step=step),
        out_shape=jax.ShapeDtypeStruct((sources, HDIM + FOLD, LANES), BF16),
        in_specs=vmem_specs(1),
        out_specs=pl.BlockSpec(memory_space=pltpu.VMEM),
        scratch_shapes=[
            wide, wide, wide, tall, tall, tall, tall,
            pltpu.VMEM((2, length, step), F32),
            pltpu.VMEM((2, length, step), F32),
            pltpu.VMEM((HDIM, length), F32),
            pltpu.VMEM((length, HDIM), F32),
            pltpu.VMEM((length, HDIM), F32),
        ],
        compiler_params=pltpu.CompilerParams(vmem_limit_bytes=LIMIT),
        cost_estimate=pl.CostEstimate(
            flops=10 * length * length * 256, bytes_accessed=2200000, transcendentals=length * length
        ),
        name="spatial_attention",
    )(received)


def unpack_kernel(in_ref, dq_ref, dk_ref, dv_ref):
    low = low_lanes(HEADS * HDIM)
    values = []
    for frame in range(2):
        items = [in_ref[frame * HEADS + head].astype(F32) for head in range(HEADS)]
        both = jnp.concatenate([item[:HDIM] for item in items], axis=0).T.astype(BF16)
        dq_ref[frame] = both[:HALF]
        dk_ref[frame] = both[HALF:]
        values.append(
            jnp.concatenate(
                [
                    jnp.concatenate(
                        [item[HDIM:], swap(item[HDIM + 2 * FOLD - HDIM :])], axis=0
                    )
                    for item in items
                ],
                axis=0,
            )
        )
    both = jnp.where(low, values[0], swap(values[1])).T.astype(BF16)
    dv_ref[0] = both[:HALF]
    dv_ref[1] = both[HALF:]


def unpack(received):
    shape = jax.ShapeDtypeStruct((2, HALF, HEADS * HDIM), BF16)
    return pl.pallas_call(
        unpack_kernel,
        out_shape=(shape, shape, shape),
        in_specs=vmem_specs(1),
        out_specs=tuple(vmem_specs(3)),
        compiler_params=pltpu.CompilerParams(vmem_limit_bytes=LIMIT),
        name="spatial_unpack",
    )(received)


def frames_back(queries, keys_in, values, out_grad):
    scale = 1.0 / math.sqrt(queries.shape[-1])
    scores = (
        jnp.einsum("fthd,gthd->thfg", queries, keys_in, preferred_element_type=jnp.float32) * scale
    )
    peak = jnp.max(scores, axis=-1, keepdims=True)
    raised = jnp.exp(scores - peak)
    weights = raised / jnp.sum(raised, axis=-1, keepdims=True)
    prob_grad = jnp.einsum("fthd,gthd->thfg", out_grad, values, preferred_element_type=jnp.float32)
    inner = jnp.sum(weights * prob_grad, axis=-1, keepdims=True)
    score_low = (weights * (prob_grad - inner)).astype(jnp.bfloat16)
    weight_low = weights.astype(jnp.bfloat16)
    query_grad = (
        jnp.einsum("thfg,gthd->fthd", score_low, keys_in, preferred_element_type=jnp.float32)
        * scale
    )
    key_grad = (
        jnp.einsum("thfg,fthd->gthd", score_low, queries, preferred_element_type=jnp.float32)
        * scale
    )
    value_grad = jnp.einsum(
        "thfg,fthd->gthd", weight_low, out_grad, preferred_element_type=jnp.float32
    )
    output = jnp.einsum("thfg,gthd->fthd", weight_low, values, preferred_element_type=jnp.float32)
    return (
        query_grad.astype(jnp.bfloat16),
        key_grad.astype(jnp.bfloat16),
        value_grad.astype(jnp.bfloat16),
        output.astype(jnp.bfloat16),
    )


def space_perm(move):
    pairs = []
    for index in range(32):
        z, y, c = index // 8, (index // 2) % 4, index % 2
        z, y, c = move(z, y, c)
        pairs.append((index, (z % 4) * 8 + (y % 4) * 2 + c % 2))
    return pairs


def collect(block, own, moves, axis):
    size = len(moves) + 1
    out = jnp.zeros((size,) + block.shape, block.dtype)
    out = lax.dynamic_update_index_in_dim(out, block, own, 0)
    for shift, move in enumerate(moves, 1):
        got = lax.ppermute(block, axis, move)
        out = lax.dynamic_update_index_in_dim(out, got, lax.rem(own + size - shift, size), 0)
    return out


def sum_weight_grad(partial):
    rows, width = partial.shape
    blocks = partial.astype(BF16).reshape(4, 32, rows // 128, width).transpose(1, 0, 2, 3)
    got = lax.all_to_all(blocks, "space", split_axis=0, concat_axis=0, tiled=True)
    mine = jnp.sum(got.astype(F32), axis=0)
    dp = lax.axis_index("dp")
    total = lax.dynamic_index_in_dim(mine, dp, 0, keepdims=False)
    for shift in range(1, 4):
        send = lax.dynamic_index_in_dim(mine, lax.rem(dp + shift, 4), 0, keepdims=False)
        total = total + lax.ppermute(send, "dp", [(i, (i + shift) % 4) for i in range(4)])
    space = lax.axis_index("space")
    z, y, c = space // 8, lax.rem(space // 2, 4), lax.rem(space, 2)
    out = collect(total, z, [space_perm(lambda a, b, e, s=s: (a + s, b, e)) for s in (1, 2, 3)], "space")
    out = collect(out, y, [space_perm(lambda a, b, e, s=s: (a, b + s, e)) for s in (1, 2, 3)], "space")
    out = collect(out, c, [space_perm(lambda a, b, e: (a, b, e + 1))], "space")
    return out.transpose(2, 1, 0, 3, 4).reshape(rows // 4, width)


def shards(
    q_spatial,
    k_spatial,
    v_spatial,
    grad_spatial,
    q_temporal,
    k_temporal,
    v_temporal,
    grad_out,
    w_tout,
):
    packed = pack(q_spatial[0], k_spatial[0], v_spatial[0], grad_spatial[0])
    received = lax.all_to_all(packed, "space", split_axis=0, concat_axis=0, tiled=True)
    results = attend(received)
    returned = lax.all_to_all(results, "space", split_axis=0, concat_axis=0, tiled=True)
    dq, dk, dv = unpack(returned)

    heads_in = (
        lax.all_to_all(q_temporal, "tm", split_axis=3, concat_axis=1, tiled=True),
        lax.all_to_all(k_temporal, "tm", split_axis=3, concat_axis=1, tiled=True),
        lax.all_to_all(v_temporal, "tm", split_axis=3, concat_axis=1, tiled=True),
    )
    grad_all = lax.all_gather(grad_out, "tm", axis=1, tiled=True)
    width = grad_out.shape[3]
    all_frames = grad_all.shape[1]
    tokens = grad_all.shape[2]
    grad_rows = grad_all.reshape(all_frames * tokens, width)
    local_width = w_tout.shape[1]
    local_heads = local_width // HDIM
    head_grad = jnp.dot(
        grad_rows,
        lax.all_gather(w_tout, "dp", axis=0, tiled=True),
        preferred_element_type=jnp.float32,
    )

    def head_split(field):
        return field.reshape(all_frames, tokens, local_heads, HDIM)

    def head_join(field):
        return field.reshape(1, all_frames, tokens, local_width)

    temporal = frames_back(
        head_split(heads_in[0]),
        head_split(heads_in[1]),
        head_split(heads_in[2]),
        head_split(head_grad.astype(jnp.bfloat16)),
    )
    back = (
        lax.all_to_all(head_join(temporal[0]), "tm", split_axis=1, concat_axis=3, tiled=True),
        lax.all_to_all(head_join(temporal[1]), "tm", split_axis=1, concat_axis=3, tiled=True),
        lax.all_to_all(head_join(temporal[2]), "tm", split_axis=1, concat_axis=3, tiled=True),
    )
    output_rows = temporal[3].reshape(all_frames * tokens, local_width)
    weight_scale = 1.0 / math.sqrt(65536)
    partial = (
        lax.dot_general(
            grad_rows, output_rows, (((0,), (0,)), ((), ())), preferred_element_type=jnp.float32
        )
        * weight_scale
    )
    weight_grad = sum_weight_grad(partial)
    return (dq[None], dk[None], dv[None], back[0], back[1], back[2], weight_grad)


def solution(mesh):
    return jax.shard_map(
        shards,
        mesh=mesh,
        in_specs=(
            P("dp", "tm", "space", None),
            P("dp", "tm", "space", None),
            P("dp", "tm", "space", None),
            P("dp", "tm", "space", None),
            P("dp", "tm", "space", None),
            P("dp", "tm", "space", None),
            P("dp", "tm", "space", None),
            P("dp", "tm", "space", None),
            P("dp", "tm"),
        ),
        out_specs=(
            P("dp", "tm", "space", None),
            P("dp", "tm", "space", None),
            P("dp", "tm", "space", None),
            P("dp", "tm", "space", None),
            P("dp", "tm", "space", None),
            P("dp", "tm", "space", None),
            P("dp", "tm"),
        ),
        check_vma=False,
    )
```

time: 696 us -> 278 us (0.40); the launches traced: 686 us -> 277 us
  waiting for transfers between devices: 371 us -> 56.1 us
  matrix products: 59.8 us -> 8.51 us
  other arithmetic: 43.9 us -> 0.74 us
  local copies, waits for them, and re-layouts: 61.7 us -> 27.3 us
  Pallas kernels: 0 us -> 28.6 us
    psum x1 -> x0, waiting for transfers between devices: 313 us -> none  [shards(): lax.psum(lax.dot_general(columns, output_rows, contract_first, preferred_...]
    dot_general x22 -> x2, matrix products: 47.9 us -> 2.41 us  [the longest x1 1.86 us: shards(): jnp.dot(grad_rows, lax.all_gather(w_tout, 'dp', axis=0, tiled=True), pref...]
    ppermute x0 -> x10, starting transfers between devices: none -> 44.8 us  [the longest x7 29.8 us: collect(): got = lax.ppermute(block, axis, move)]
    all_to_all x10 -> x6, starting transfers between devices: 86.6 us -> 48 us  [the longest x1 23.5 us: shards(): lax.all_to_all(packed, 'space', split_axis=0, concat_axis=0, tiled=True)]
    unnamed x5 -> x0, other arithmetic: 34.6 us -> none
    pallas_call x0 -> x3, Pallas kernels: none -> 28.6 us  [the longest x1 23.5 us: attend(): pl.pallas_call(functools.partial(attend_kernel, step=step), out_shape=jax...]
    unnamed x59 -> x32, local copies, waits for them, and re-layouts: 24.3 us -> 9.52 us
    reshape x15 -> x3, local copies, waits for them, and re-layouts: 13.5 us -> 1.61 us  [the longest x1 0.84 us: sum_weight_grad(): return out.transpose(2, 1, 0, 3, 4).reshape(rows // 4, width)]
  transfers between devices with their start and end apart: 15 -> 20, of which waited for: 9 -> 11; matrix products, arithmetic and copies ran while one was open for 23% -> 9% of each run, Pallas kernels for 0% -> 9%
where the time goes in v1:
time: 278 us; the launch traced here: 277 us
  starting transfers between devices  105 us (38%)
  waiting for transfers between devices  56.1 us (20%)
  blocking collectives  36.4 us (13%)
  Pallas kernels  28.6 us (10%)
  local copies, waits for them, and re-layouts  27.3 us (10%)
  between operations  14.8 us (5%)
  matrix products  8.51 us (3%)
    all_gather x1, blocking collectives, shards(): lax.all_gather(w_tout, 'dp', axis=0, tiled=True)  36.4 us
    ppermute x7, starting transfers between devices, collect(): got = lax.ppermute(block, axis, move)  29.8 us
    all_to_all x1, waiting for transfers between devices, shards(): lax.all_to_all(packed, 'space', split_axis=0, concat_axis=0, tiled=True)  24.3 us
    all_to_all x1, starting transfers between devices, shards(): lax.all_to_all(packed, 'space', split_axis=0, concat_axis=0, tiled=True)  23.5 us
    pallas_call x1, Pallas kernels, attend(): pl.pallas_call(functools.partial(attend_kernel, step=step), out_shape=jax...  23.5 us
    ppermute x3, starting transfers between devices, sum_weight_grad(): lax.ppermute(send, 'dp', [(i, (i + shift) % 4) for i in range(4)])  14.9 us
    unnamed x32, local copies, waits for them, and re-layouts  9.52 us
    all_to_all x1, starting transfers between devices, shards(): lax.all_to_all(results, 'space', split_axis=0, concat_axis=0, tiled=True)  7.73 us
  transfers between devices with their start and end apart: 20, of which 11 were waited for; matrix products, arithmetic and copies ran while one was open for 9% of the time, Pallas kernels for 9%

profile of v1, /device:TPU:1, one launch (start us, length us, event | category | flops | bytes accessed | tf_op | source)
XLA Modules:
  0.0 277.0 jit_solution(6737516710000864119)
XLA Ops:
  7.2 0.7 all-gather.2.cloned.1.call-update
  7.9 1.6 copy.104
  9.5 1.2 reshape.68
  10.7 4.8 %all-to-all-start.2 = ((bf16[4,2,18432]{2,1,0:T(2,128)(2,1)}), bf16[4,2,18432]{2,1,0:T(2,128)(2,1)S(1)}, u32[]{:S(2)}, u32[]{:S(2)}) async-start(bf16[4,2,18432]{2,1,0:T(2,128)(2,1)} %reshape.68), calls=%async_computation.2 | async-start | bytes 589824 | tf_op jit(solution)/shard_map/all_to_all | solution.py:290
  15.5 0.7 copy.106
  16.2 1.2 reshape.66
  17.4 3.8 %all-to-all-done.2 = bf16[4,2,18432]{2,1,0:T(2,128)(2,1)S(1)} async-done(((bf16[4,2,18432]{2,1,0:T(2,128)(2,1)}), bf16[4,2,18432]{2,1,0:T(2,128)(2,1)S(1)}, u32[]{:S(2)}, u32[]{:S(2)}) %all-to-all-start.2) | async-done | bytes 294944 | tf_op jit(solution)/shard_map/all_to_all | solution.py:290
  21.2 3.5 %all-to-all-start.3 = ((bf16[4,2,18432]{2,1,0:T(2,128)(2,1)}), bf16[4,2,18432]{2,1,0:T(2,128)(2,1)S(1)}, u32[]{:S(2)}, u32[]{:S(2)}) async-start(bf16[4,2,18432]{2,1,0:T(2,128)(2,1)} %reshape.66), calls=%async_computation.3 | async-start | bytes 589824 | tf_op jit(solution)/shard_map/all_to_all | solution.py:291
  24.7 0.7 copy.111
  25.4 1.2 reshape.64
  26.6 3.8 %all-to-all-done.3 = bf16[4,2,18432]{2,1,0:T(2,128)(2,1)S(1)} async-done(((bf16[4,2,18432]{2,1,0:T(2,128)(2,1)}), bf16[4,2,18432]{2,1,0:T(2,128)(2,1)S(1)}, u32[]{:S(2)}, u32[]{:S(2)}) %all-to-all-start.3) | async-done | bytes 294944 | tf_op jit(solution)/shard_map/all_to_all | solution.py:291
  30.3 3.5 %all-to-all-start.4 = ((bf16[4,2,18432]{2,1,0:T(2,128)(2,1)}), bf16[4,2,18432]{2,1,0:T(2,128)(2,1)S(1)}, u32[]{:S(2)}, u32[]{:S(2)}) async-start(bf16[4,2,18432]{2,1,0:T(2,128)(2,1)} %reshape.64), calls=%async_computation.4 | async-start | bytes 589824 | tf_op jit(solution)/shard_map/all_to_all | solution.py:292
  33.8 36.4 %all_gather.7 = bf16[1152,288]{1,0:T(8,128)(2,1)S(1)} all-gather(bf16[288,288]{1,0:T(8,128)(2,1)S(1)} %copy-done.9), channel_id=1, replica_groups=mesh['dp'=4,'tm'=4,'space'=32] {'dp'}, dimensions={0}, use_global_device_ids=true | all-gather | bytes 829440 | tf_op jit(solution)/shard_map/all_gather | solution.py:303
  70.6 0.5 copy.105
  71.8 0.5 copy.107
  73.0 0.5 copy.112
  73.5 1.1 reshape.57
  74.6 2.1 fusion.33
  76.8 1.9 convolution_convert_fusion.2
  79.0 1.8 copy.113
  80.8 1.9 multiply_reduce_fusion
  83.0 0.5 fusion.7
  83.7 1.1 reshape.59
  84.9 4.2 %all-to-all-start.6 = ((bf16[1,8,64,288]{3,2,0,1:T(8,128)(2,1)}), bf16[1,8,64,288]{3,2,0,1:T(8,128)(2,1)S(1)}, u32[]{:S(2)}, u32[]{:S(2)}) async-start(bf16[1,8,64,288]{3,2,0,1:T(8,128)(2,1)} %bitcast.20), calls=%async_computation.6 | async-start | bytes 786432 | tf_op jit(solution)/shard_map/all_to_all | solution.py:321
  89.0 0.5 fusion.8
  89.8 1.1 reshape.58
  90.9 4.4 %all-to-all-done.6 = bf16[1,8,64,288]{3,2,0,1:T(8,128)(2,1)S(1)} async-done(((bf16[1,8,64,288]{3,2,0,1:T(8,128)(2,1)}), bf16[1,8,64,288]{3,2,0,1:T(8,128)(2,1)S(1)}, u32[]{:S(2)}, u32[]{:S(2)}) %all-to-all-start.6) | async-done | bytes 294944 | tf_op jit(solution)/shard_map/all_to_all | solution.py:321
  95.2 3.6 %all-to-all-start.5 = ((bf16[1,8,64,288]{3,2,0,1:T(8,128)(2,1)}), bf16[1,8,64,288]{3,2,0,1:T(8,128)(2,1)S(1)}, u32[]{:S(2)}, u32[]{:S(2)}) async-start(bf16[1,8,64,288]{3,2,0,1:T(8,128)(2,1)} %bitcast.16), calls=%async_computation.5 | async-start | bytes 786432 | tf_op jit(solution)/shard_map/all_to_all | solution.py:320
  99.5 1.1 reshape.60
  100.7 4.3 %all-to-all-done.5 = bf16[1,8,64,288]{3,2,0,1:T(8,128)(2,1)S(1)} async-done(((bf16[1,8,64,288]{3,2,0,1:T(8,128)(2,1)}), bf16[1,8,64,288]{3,2,0,1:T(8,128)(2,1)S(1)}, u32[]{:S(2)}, u32[]{:S(2)}) %all-to-all-start.5) | async-done | bytes 294944 | tf_op jit(solution)/shard_map/all_to_all | solution.py:320
  104.9 3.5 %all-to-all-start.7 = ((bf16[1,8,64,288]{3,2,0,1:T(8,128)(2,1)}), bf16[1,8,64,288]{3,2,0,1:T(8,128)(2,1)S(1)}, u32[]{:S(2)}, u32[]{:S(2)}) async-start(bf16[1,8,64,288]{3,2,0,1:T(8,128)(2,1)} %bitcast.24), calls=%async_computation.7 | async-start | bytes 786432 | tf_op jit(solution)/shard_map/all_to_all | solution.py:322
  108.4 2.6 spatial_pack.1
  111.0 3.6 %all-to-all-done.7 = bf16[1,8,64,288]{3,2,0,1:T(8,128)(2,1)S(1)} async-done(((bf16[1,8,64,288]{3,2,0,1:T(8,128)(2,1)}), bf16[1,8,64,288]{3,2,0,1:T(8,128)(2,1)S(1)}, u32[]{:S(2)}, u32[]{:S(2)}) %all-to-all-start.7) | async-done | bytes 294944 | tf_op jit(solution)/shard_map/all_to_all | solution.py:322
  114.6 0.7 copy-done.1
  115.3 23.5 %all-to-all-start = ((bf16[32,2,72,128]{3,2,1,0:T(8,128)(2,1)}), bf16[32,2,72,128]{3,2,1,0:T(8,128)(2,1)}, u32[]{:S(2)}, u32[]{:S(2)}) async-start(bf16[32,2,72,128]{3,2,1,0:T(8,128)(2,1)} %spatial_pack.1), calls=%async_computation | async-start | bytes 2359296 | tf_op jit(solution)/shard_map/all_to_all | solution.py:284
  138.8 0.6 fusion.10
  139.4 0.7 copy.130
  140.7 0.5 fusion.2
  142.1 1.7 copy.132
  143.7 24.3 %all-to-all-done.in_ref = bf16[32,2,72,128]{3,2,1,0:T(8,128)(2,1)} async-done(((bf16[32,2,72,128]{3,2,1,0:T(8,128)(2,1)}), bf16[32,2,72,128]{3,2,1,0:T(8,128)(2,1)}, u32[]{:S(2)}, u32[]{:S(2)}) %all-to-all-start) | async-done | bytes 1179680 | tf_op jit(solution)/shard_map/all_to_all | solution.py:284
  168.0 5.5 %all-to-all-start.8 = ((bf16[32,4,9,288]{3,1,2,0:T(4,128)(2,1)}), bf16[32,4,9,288]{3,1,2,0:T(4,128)(2,1)S(1)}, u32[]{:S(2)}, u32[]{:S(2)}) async-start(bf16[32,4,9,288]{3,1,2,0:T(4,128)(2,1)} %copy.132), calls=%async_computation.8 | async-start | bytes 1769472 | tf_op jit(solution)/shard_map/all_to_all | solution.py:257
  173.5 23.5 %spatial_attention.1 = bf16[32,112,128]{2,1,0:T(8,128)(2,1)} custom-call(bf16[32,2,72,128]{3,2,1,0:T(8,128)(2,1)} %all-to-all-done.in_ref), custom_call_target="tpu_custom_call" | custom-call | flops 10737418240 | bytes 2200000 | tf_op jit(solution)/shard_map/spatial_attention/pallas_call | solution.py:146
  197.0 7.7 %all-to-all-start.1 = ((bf16[32,112,128]{2,1,0:T(8,128)(2,1)}), bf16[32,112,128]{2,1,0:T(8,128)(2,1)S(1)}, u32[]{:S(2)}, u32[]{:S(2)}) async-start(bf16[32,112,128]{2,1,0:T(8,128)(2,1)} %spatial_attention.1), calls=%async_computation.1 | async-start | bytes 1835008 | tf_op jit(solution)/shard_map/all_to_all | solution.py:286
  205.2 2.8 %collective-permute-start = (f32[9,288]{1,0:T(8,128)S(1)}, f32[9,288]{1,0:T(8,128)S(1)}, u32[]{:S(2)}, u32[]{:S(2)}) collective-permute-start(f32[9,288]{1,0:T(8,128)S(1)} %bitcast.130), channel_id=1, source_target_pairs={{0,128},{128,256},{256,384},{384,0},{1,129},{129,257},{257,385},{3... | collective-permute-start | bytes 31112 | tf_op jit(solution)/shard_map/ppermute | solution.py:263
  208.0 6.8 %collective-permute-start.1 = (f32[9,288]{1,0:T(8,128)S(1)}, f32[9,288]{1,0:T(8,128)S(1)}, u32[]{:S(2)}, u32[]{:S(2)}) collective-permute-start(f32[9,288]{1,0:T(8,128)S(1)} %bitcast.131), channel_id=1, source_target_pairs={{0,256},{128,384},{256,0},{384,128},{1,257},{129,385},{257,1},{385... | collective-permute-start | bytes 31112 | tf_op jit(solution)/shard_map/ppermute | solution.py:263
  214.8 5.4 %collective-permute-start.2 = (f32[9,288]{1,0:T(8,128)S(1)}, f32[9,288]{1,0:T(8,128)S(1)}, u32[]{:S(2)}, u32[]{:S(2)}) collective-permute-start(f32[9,288]{1,0:T(8,128)S(1)} %bitcast.132), channel_id=1, source_target_pairs={{0,384},{128,0},{256,128},{384,256},{1,385},{129,1},{257,129},{385... | collective-permute-start | bytes 31112 | tf_op jit(solution)/shard_map/ppermute | solution.py:263
  220.2 3.0 %collective-permute-done = f32[9,288]{1,0:T(8,128)S(1)} collective-permute-done((f32[9,288]{1,0:T(8,128)S(1)}, f32[9,288]{1,0:T(8,128)S(1)}, u32[]{:S(2)}, u32[]{:S(2)}) %collective-permute-start) | collective-permute-done | bytes 10400 | tf_op jit(solution)/shard_map/ppermute | solution.py:263
  223.2 3.3 %collective-permute-done.1 = f32[9,288]{1,0:T(8,128)S(1)} collective-permute-done((f32[9,288]{1,0:T(8,128)S(1)}, f32[9,288]{1,0:T(8,128)S(1)}, u32[]{:S(2)}, u32[]{:S(2)}) %collective-permute-start.1) | collective-permute-done | bytes 10400 | tf_op jit(solution)/shard_map/ppermute | solution.py:263
  226.5 7.0 %collective-permute-start.3 = (f32[9,288]{1,0:T(8,128)S(1)}, f32[9,288]{1,0:T(8,128)S(1)}, u32[]{:S(2)}, u32[]{:S(2)}) collective-permute-start(f32[9,288]{1,0:T(8,128)S(1)} %get-tuple-element.14), channel_id=1, source_target_pairs={{0,8},{1,9},{2,10},{3,11},{4,12},{5,13},{6,14},{7,15},{8,16},{9,17... | collective-permute-start | bytes 31112 | tf_op jit(solution)/shard_map/ppermute | solution.py:249
  233.9 1.0 all_to_all.99
  235.2 1.0 all_to_all.95
  236.6 1.0 all_to_all.103
  237.6 2.7 collective-permute-start.4
  240.3 4.3 %collective-permute-start.5 = (f32[9,288]{1,0:T(8,128)S(1)}, f32[9,288]{1,0:T(8,128)S(1)}, u32[]{:S(2)}, u32[]{:S(2)}) collective-permute-start(f32[9,288]{1,0:T(8,128)S(1)} %get-tuple-element.14), channel_id=1, source_target_pairs={{0,24},{1,25},{2,26},{3,27},{4,28},{5,29},{6,30},{7,31},{8,0},{9,1... | collective-permute-start | bytes 31112 | tf_op jit(solution)/shard_map/ppermute | solution.py:249
  244.6 0.9 collective-permute-done.5
  245.5 3.1 %collective-permute-start.6 = (f32[4,9,288]{2,1,0:T(8,128)S(1)}, f32[4,9,288]{2,1,0:T(8,128)S(1)}, u32[]{:S(2)}, u32[]{:S(2)}) collective-permute-start(f32[4,9,288]{2,1,0:T(8,128)S(1)} %bitcast_dynamic-update-slice_fusion.6), channel_id=1, source_target_pairs={{0,2},{1,3},{2,4},{3,5},{4,6},{5,7},{6,0},{7,1},{8,10},{9,11},{10,... | collective-permute-start | bytes 124424 | tf_op jit(solution)/shard_map/ppermute | solution.py:249
  248.6 4.3 %collective-permute-start.7 = (f32[4,9,288]{2,1,0:T(8,128)S(1)}, f32[4,9,288]{2,1,0:T(8,128)S(1)}, u32[]{:S(2)}, u32[]{:S(2)}) collective-permute-start(f32[4,9,288]{2,1,0:T(8,128)S(1)} %bitcast_dynamic-update-slice_fusion.6), channel_id=1, source_target_pairs={{0,4},{1,5},{2,6},{3,7},{4,0},{5,1},{6,2},{7,3},{8,12},{9,13},{10,... | collective-permute-start | bytes 124424 | tf_op jit(solution)/shard_map/ppermute | solution.py:249
  252.9 3.1 %collective-permute-start.8 = (f32[4,9,288]{2,1,0:T(8,128)S(1)}, f32[4,9,288]{2,1,0:T(8,128)S(1)}, u32[]{:S(2)}, u32[]{:S(2)}) collective-permute-start(f32[4,9,288]{2,1,0:T(8,128)S(1)} %bitcast_dynamic-update-slice_fusion.6), channel_id=1, source_target_pairs={{0,6},{1,7},{2,0},{3,1},{4,2},{5,3},{6,4},{7,5},{8,14},{9,15},{10,... | collective-permute-start | bytes 124424 | tf_op jit(solution)/shard_map/ppermute | solution.py:249
  256.1 2.9 %collective-permute-done.8 = f32[4,9,288]{2,1,0:T(8,128)S(1)} collective-permute-done((f32[4,9,288]{2,1,0:T(8,128)S(1)}, f32[4,9,288]{2,1,0:T(8,128)S(1)}, u32[]{:S(2)}, u32[]{:S(2)}) %collective-permute-start.8) | collective-permute-done | bytes 41504 | tf_op jit(solution)/shard_map/ppermute | solution.py:249
  259.0 5.4 %collective-permute-start.9 = (f32[4,4,9,288]{3,2,0,1:T(8,128)S(1)}, f32[4,4,9,288]{3,2,0,1:T(8,128)S(1)}, u32[]{:S(2)}, u32[]{:S(2)}) collective-permute-start(f32[4,4,9,288]{3,2,0,1:T(8,128)S(1)} %bitcast_dynamic-update-slice_fusion.5), channel_id=1, source_target_pairs={{0,1},{1,0},{2,3},{3,2},{4,5},{5,4},{6,7},{7,6},{8,9},{9,8},{10,11... | collective-permute-start | bytes 497672 | tf_op jit(solution)/shard_map/ppermute | solution.py:249
  264.6 1.2 collective-permute-done.9
  265.8 0.8 reshape.63
  266.7 0.9 copy-done
  267.6 2.5 spatial_unpack.1
  (63 shorter events, 6.6 us)
Async XLA Ops:
  7.2 69.6 %all-gather.2.cloned.1.call-start = ((), (), s32[]{:S(2)}) async-start(), calls=%async_computation.9 | async-start | bytes 1474560 | tf_op jit(solution)/shard_map/all_gather | solution.py:294
  7.9 7.6 %copy-start.7 = (bf16[1,2,64,1152]{3,2,1,0:T(8,128)(2,1)S(1)}, bf16[1,2,64,1152]{3,2,1,0:T(8,128)(2,1)}, u32[]{:S(2)}) copy-start(bf16[1,2,64,1152]{3,2,1,0:T(8,128)(2,1)} %param.14) | copy-start | bytes 884740
  10.7 10.5 %all-to-all-start.2 = ((bf16[4,2,18432]{2,1,0:T(2,128)(2,1)}), bf16[4,2,18432]{2,1,0:T(2,128)(2,1)S(1)}, u32[]{:S(2)}, u32[]{:S(2)}) async-start(bf16[4,2,18432]{2,1,0:T(2,128)(2,1)} %reshape.68), calls=%async_computation.2 | async-start | bytes 589824 | tf_op jit(solution)/shard_map/all_to_all | solution.py:290
  15.5 9.2 %copy-start.8 = (bf16[1,2,64,1152]{3,2,1,0:T(8,128)(2,1)S(1)}, bf16[1,2,64,1152]{3,2,1,0:T(8,128)(2,1)}, u32[]{:S(2)}) copy-start(bf16[1,2,64,1152]{3,2,1,0:T(8,128)(2,1)} %param.15) | copy-start | bytes 884740
  21.2 9.1 %all-to-all-start.3 = ((bf16[4,2,18432]{2,1,0:T(2,128)(2,1)}), bf16[4,2,18432]{2,1,0:T(2,128)(2,1)S(1)}, u32[]{:S(2)}, u32[]{:S(2)}) async-start(bf16[4,2,18432]{2,1,0:T(2,128)(2,1)} %reshape.66), calls=%async_computation.3 | async-start | bytes 589824 | tf_op jit(solution)/shard_map/all_to_all | solution.py:291
  24.7 9.1 %copy-start.9 = (bf16[288,288]{1,0:T(8,128)(2,1)S(1)}, bf16[288,288]{1,0:T(8,128)(2,1)}, u32[]{:S(2)}) copy-start(bf16[288,288]{1,0:T(8,128)(2,1)} %param.17) | copy-start | bytes 497668
  30.3 42.3 %all-to-all-start.4 = ((bf16[4,2,18432]{2,1,0:T(2,128)(2,1)}), bf16[4,2,18432]{2,1,0:T(2,128)(2,1)S(1)}, u32[]{:S(2)}, u32[]{:S(2)}) async-start(bf16[4,2,18432]{2,1,0:T(2,128)(2,1)} %reshape.64), calls=%async_computation.4 | async-start | bytes 589824 | tf_op jit(solution)/shard_map/all_to_all | solution.py:292
  78.7 2.1 copy-start.4
  84.9 10.4 %all-to-all-start.6 = ((bf16[1,8,64,288]{3,2,0,1:T(8,128)(2,1)}), bf16[1,8,64,288]{3,2,0,1:T(8,128)(2,1)S(1)}, u32[]{:S(2)}, u32[]{:S(2)}) async-start(bf16[1,8,64,288]{3,2,0,1:T(8,128)(2,1)} %bitcast.20), calls=%async_computation.6 | async-start | bytes 786432 | tf_op jit(solution)/shard_map/all_to_all | solution.py:321
  89.6 9.3 %copy-start.6 = (bf16[8,64,4,72]{3,0,2,1:T(8,128)(2,1)S(1)}, bf16[8,64,4,72]{3,0,2,1:T(8,128)(2,1)}, u32[]{:S(2)}) copy-start(bf16[8,64,4,72]{3,0,2,1:T(8,128)(2,1)} %copy.113) | copy-start | bytes 884740
  95.2 9.7 %all-to-all-start.5 = ((bf16[1,8,64,288]{3,2,0,1:T(8,128)(2,1)}), bf16[1,8,64,288]{3,2,0,1:T(8,128)(2,1)S(1)}, u32[]{:S(2)}, u32[]{:S(2)}) async-start(bf16[1,8,64,288]{3,2,0,1:T(8,128)(2,1)} %bitcast.16), calls=%async_computation.5 | async-start | bytes 786432 | tf_op jit(solution)/shard_map/all_to_all | solution.py:320
  104.9 9.7 %all-to-all-start.7 = ((bf16[1,8,64,288]{3,2,0,1:T(8,128)(2,1)}), bf16[1,8,64,288]{3,2,0,1:T(8,128)(2,1)S(1)}, u32[]{:S(2)}, u32[]{:S(2)}) async-start(bf16[1,8,64,288]{3,2,0,1:T(8,128)(2,1)} %bitcast.24), calls=%async_computation.7 | async-start | bytes 786432 | tf_op jit(solution)/shard_map/all_to_all | solution.py:322
  111.0 27.8 %copy-start.5 = (bf16[8,64,4,72]{3,2,1,0:T(4,128)(2,1)S(1)}, bf16[8,64,4,72]{3,2,1,0:T(4,128)(2,1)}, u32[]{:S(2)}) copy-start(bf16[8,64,4,72]{3,2,1,0:T(4,128)(2,1)} %reshape.57) | copy-start | bytes 884740
  114.6 0.7 copy-start.1
  115.3 52.7 %all-to-all-start = ((bf16[32,2,72,128]{3,2,1,0:T(8,128)(2,1)}), bf16[32,2,72,128]{3,2,1,0:T(8,128)(2,1)}, u32[]{:S(2)}, u32[]{:S(2)}) async-start(bf16[32,2,72,128]{3,2,1,0:T(8,128)(2,1)} %spatial_pack.1), calls=%async_computation | async-start | bytes 2359296 | tf_op jit(solution)/shard_map/all_to_all | solution.py:284
  139.4 1.3 copy-start.3
  168.0 29.0 %all-to-all-start.8 = ((bf16[32,4,9,288]{3,1,2,0:T(4,128)(2,1)}), bf16[32,4,9,288]{3,1,2,0:T(4,128)(2,1)S(1)}, u32[]{:S(2)}, u32[]{:S(2)}) async-start(bf16[32,4,9,288]{3,1,2,0:T(4,128)(2,1)} %copy.132), calls=%async_computation.8 | async-start | bytes 1769472 | tf_op jit(solution)/shard_map/all_to_all | solution.py:257
  197.0 69.7 %all-to-all-start.1 = ((bf16[32,112,128]{2,1,0:T(8,128)(2,1)}), bf16[32,112,128]{2,1,0:T(8,128)(2,1)S(1)}, u32[]{:S(2)}, u32[]{:S(2)}) async-start(bf16[32,112,128]{2,1,0:T(8,128)(2,1)} %spatial_attention.1), calls=%async_computation.1 | async-start | bytes 1835008 | tf_op jit(solution)/shard_map/all_to_all | solution.py:286
  205.2 18.0 %collective-permute-start = (f32[9,288]{1,0:T(8,128)S(1)}, f32[9,288]{1,0:T(8,128)S(1)}, u32[]{:S(2)}, u32[]{:S(2)}) collective-permute-start(f32[9,288]{1,0:T(8,128)S(1)} %bitcast.130), channel_id=1, source_target_pairs={{0,128},{128,256},{256,384},{384,0},{1,129},{129,257},{257,385},{3... | collective-permute-start | bytes 31112 | tf_op jit(solution)/shard_map/ppermute | solution.py:263
  208.0 18.4 %collective-permute-start.1 = (f32[9,288]{1,0:T(8,128)S(1)}, f32[9,288]{1,0:T(8,128)S(1)}, u32[]{:S(2)}, u32[]{:S(2)}) collective-permute-start(f32[9,288]{1,0:T(8,128)S(1)} %bitcast.131), channel_id=1, source_target_pairs={{0,256},{128,384},{256,0},{384,128},{1,257},{129,385},{257,1},{385... | collective-permute-start | bytes 31112 | tf_op jit(solution)/shard_map/ppermute | solution.py:263
  214.8 11.7 %collective-permute-start.2 = (f32[9,288]{1,0:T(8,128)S(1)}, f32[9,288]{1,0:T(8,128)S(1)}, u32[]{:S(2)}, u32[]{:S(2)}) collective-permute-start(f32[9,288]{1,0:T(8,128)S(1)} %bitcast.132), channel_id=1, source_target_pairs={{0,384},{128,0},{256,128},{384,256},{1,385},{129,1},{257,129},{385... | collective-permute-start | bytes 31112 | tf_op jit(solution)/shard_map/ppermute | solution.py:263
  226.5 18.0 %collective-permute-start.3 = (f32[9,288]{1,0:T(8,128)S(1)}, f32[9,288]{1,0:T(8,128)S(1)}, u32[]{:S(2)}, u32[]{:S(2)}) collective-permute-start(f32[9,288]{1,0:T(8,128)S(1)} %get-tuple-element.14), channel_id=1, source_target_pairs={{0,8},{1,9},{2,10},{3,11},{4,12},{5,13},{6,14},{7,15},{8,16},{9,17... | collective-permute-start | bytes 31112 | tf_op jit(solution)/shard_map/ppermute | solution.py:249
  233.9 2.3 copy-start.2
  237.6 7.0 %collective-permute-start.4 = (f32[9,288]{1,0:T(8,128)S(1)}, f32[9,288]{1,0:T(8,128)S(1)}, u32[]{:S(2)}, u32[]{:S(2)}) collective-permute-start(f32[9,288]{1,0:T(8,128)S(1)} %get-tuple-element.14), channel_id=1, source_target_pairs={{0,16},{1,17},{2,18},{3,19},{4,20},{5,21},{6,22},{7,23},{8,24},{9,... | collective-permute-start | bytes 31112 | tf_op jit(solution)/shard_map/ppermute | solution.py:249
  240.3 5.2 %collective-permute-start.5 = (f32[9,288]{1,0:T(8,128)S(1)}, f32[9,288]{1,0:T(8,128)S(1)}, u32[]{:S(2)}, u32[]{:S(2)}) collective-permute-start(f32[9,288]{1,0:T(8,128)S(1)} %get-tuple-element.14), channel_id=1, source_target_pairs={{0,24},{1,25},{2,26},{3,27},{4,28},{5,29},{6,30},{7,31},{8,0},{9,1... | collective-permute-start | bytes 31112 | tf_op jit(solution)/shard_map/ppermute | solution.py:249
  245.5 10.6 %collective-permute-start.6 = (f32[4,9,288]{2,1,0:T(8,128)S(1)}, f32[4,9,288]{2,1,0:T(8,128)S(1)}, u32[]{:S(2)}, u32[]{:S(2)}) collective-permute-start(f32[4,9,288]{2,1,0:T(8,128)S(1)} %bitcast_dynamic-update-slice_fusion.6), channel_id=1, source_target_pairs={{0,2},{1,3},{2,4},{3,5},{4,6},{5,7},{6,0},{7,1},{8,10},{9,11},{10,... | collective-permute-start | bytes 124424 | tf_op jit(solution)/shard_map/ppermute | solution.py:249
  248.6 7.5 %collective-permute-start.7 = (f32[4,9,288]{2,1,0:T(8,128)S(1)}, f32[4,9,288]{2,1,0:T(8,128)S(1)}, u32[]{:S(2)}, u32[]{:S(2)}) collective-permute-start(f32[4,9,288]{2,1,0:T(8,128)S(1)} %bitcast_dynamic-update-slice_fusion.6), channel_id=1, source_target_pairs={{0,4},{1,5},{2,6},{3,7},{4,0},{5,1},{6,2},{7,3},{8,12},{9,13},{10,... | collective-permute-start | bytes 124424 | tf_op jit(solution)/shard_map/ppermute | solution.py:249
  252.9 6.1 %collective-permute-start.8 = (f32[4,9,288]{2,1,0:T(8,128)S(1)}, f32[4,9,288]{2,1,0:T(8,128)S(1)}, u32[]{:S(2)}, u32[]{:S(2)}) collective-permute-start(f32[4,9,288]{2,1,0:T(8,128)S(1)} %bitcast_dynamic-update-slice_fusion.6), channel_id=1, source_target_pairs={{0,6},{1,7},{2,0},{3,1},{4,2},{5,3},{6,4},{7,5},{8,14},{9,15},{10,... | collective-permute-start | bytes 124424 | tf_op jit(solution)/shard_map/ppermute | solution.py:249
  259.0 6.7 %collective-permute-start.9 = (f32[4,4,9,288]{3,2,0,1:T(8,128)S(1)}, f32[4,4,9,288]{3,2,0,1:T(8,128)S(1)}, u32[]{:S(2)}, u32[]{:S(2)}) collective-permute-start(f32[4,4,9,288]{3,2,0,1:T(8,128)S(1)} %bitcast_dynamic-update-slice_fusion.5), channel_id=1, source_target_pairs={{0,1},{1,0},{2,3},{3,2},{4,5},{5,4},{6,7},{7,6},{8,9},{9,8},{10,11... | collective-permute-start | bytes 497672 | tf_op jit(solution)/shard_map/ppermute | solution.py:249
  266.7 0.9 copy-start
Sparse Core Ops, SparseCore 0:
  10.1 39.0 all-gather.1

commit v2 on v1

--- a/solution.py
+++ b/solution.py
@@ -200,36 +200,296 @@
     )(received)
 
 
-def frames_back(queries, keys_in, values, out_grad):
-    scale = 1.0 / math.sqrt(queries.shape[-1])
-    scores = (
-        jnp.einsum("fthd,gthd->thfg", queries, keys_in, preferred_element_type=jnp.float32) * scale
-    )
-    peak = jnp.max(scores, axis=-1, keepdims=True)
-    raised = jnp.exp(scores - peak)
-    weights = raised / jnp.sum(raised, axis=-1, keepdims=True)
-    prob_grad = jnp.einsum("fthd,gthd->thfg", out_grad, values, preferred_element_type=jnp.float32)
-    inner = jnp.sum(weights * prob_grad, axis=-1, keepdims=True)
-    score_low = (weights * (prob_grad - inner)).astype(jnp.bfloat16)
-    weight_low = weights.astype(jnp.bfloat16)
-    query_grad = (
-        jnp.einsum("thfg,gthd->fthd", score_low, keys_in, preferred_element_type=jnp.float32)
-        * scale
-    )
-    key_grad = (
-        jnp.einsum("thfg,fthd->gthd", score_low, queries, preferred_element_type=jnp.float32)
-        * scale
-    )
-    value_grad = jnp.einsum(
-        "thfg,fthd->gthd", weight_low, out_grad, preferred_element_type=jnp.float32
-    )
-    output = jnp.einsum("thfg,gthd->fthd", weight_low, values, preferred_element_type=jnp.float32)
-    return (
-        query_grad.astype(jnp.bfloat16),
-        key_grad.astype(jnp.bfloat16),
-        value_grad.astype(jnp.bfloat16),
-        output.astype(jnp.bfloat16),
-    )
+def flip(block):
+    return pltpu.roll(block, HALF, 1)
+
+
+def send_pack_kernel(me_ref, q_ref, k_ref, v_ref, out0, out1, out2, out3, held):
+    for part, ref in enumerate((q_ref, k_ref, v_ref)):
+        rows = jnp.concatenate([ref[0], ref[1]], axis=0).astype(F32)
+        columns = rows.T.astype(BF16)
+        at = slice(part * LANES, (part + 1) * LANES)
+        held[0, :, at] = columns[:288]
+        held[1, :, at] = columns[288:576]
+        held[2, :, at] = columns[576:864]
+        held[3, :, at] = columns[864:]
+    me = me_ref[0]
+    for shift, out in enumerate((out0, out1, out2, out3)):
+        out[...] = held[lax.rem(me + shift, 4)]
+
+
+def send_pack(me, q, k, v):
+    shape = jax.ShapeDtypeStruct((288, 3 * LANES), BF16)
+    return pl.pallas_call(
+        send_pack_kernel,
+        out_shape=(shape,) * 4,
+        in_specs=[pl.BlockSpec(memory_space=pltpu.SMEM)] + vmem_specs(3),
+        out_specs=tuple(vmem_specs(4)),
+        scratch_shapes=[pltpu.VMEM((4, 288, 3 * LANES), BF16)],
+        compiler_params=pltpu.CompilerParams(vmem_limit_bytes=LIMIT),
+        name="temporal_pack",
+    )(me, q, k, v)
+
+
+def rows_of(values):
+    return jnp.concatenate([jnp.sum(value, axis=0, keepdims=True) for value in values], axis=0)
+
+
+def frame_weights(query, keys):
+    scores = rows_of([query * key for key in keys])
+    peak = jnp.max(scores, axis=0, keepdims=True)
+    raised = jnp.exp2((scores - peak) * (math.log2(math.e) / math.sqrt(HDIM)))
+    return raised / jnp.sum(raised, axis=0, keepdims=True)
+
+
+def rounded(value):
+    return value.astype(BF16).astype(F32)
+
+
+def head_rows(wide, head, part):
+    rows = pl.ds(pl.multiple_of(head * HDIM, 8), HDIM)
+    at = slice(part * LANES, (part + 1) * LANES)
+    return [wide[shift, rows, at] for shift in range(4)]
+
+
+def both_ways(blocks):
+    out = []
+    for block in blocks:
+        out += [block, flip(block)]
+    return out
+
+
+def tout_kernel(me_ref, in0, in1, in2, in3, out_ref, wide, total):
+    for shift, ref in enumerate((in0, in1, in2, in3)):
+        wide[shift] = ref[...].astype(F32)
+
+    def body(head, _):
+        queries = head_rows(wide, head, 0)
+        keys = both_ways(head_rows(wide, head, 1))
+        values = both_ways(head_rows(wide, head, 2))
+        for shift in range(4):
+            weights = rounded(frame_weights(queries[shift], keys))
+            out = weights[0:1] * values[0]
+            for j in range(1, 8):
+                out = out + weights[j : j + 1] * values[j]
+            total[shift, pl.ds(pl.multiple_of(head * HDIM, 8), HDIM)] = out
+        return 0
+
+    lax.fori_loop(0, 4, body, 0)
+    me = me_ref[0]
+    for shift in range(4):
+        out_ref[lax.rem(me + 4 - shift, 4)] = total[shift].astype(BF16)
+
+
+def temporal_out(me, pieces):
+    return pl.pallas_call(
+        tout_kernel,
+        out_shape=jax.ShapeDtypeStruct((4, 288, LANES), BF16),
+        in_specs=[pl.BlockSpec(memory_space=pltpu.SMEM)] + vmem_specs(4),
+        out_specs=pl.BlockSpec(memory_space=pltpu.VMEM),
+        scratch_shapes=[
+            pltpu.VMEM((4, 288, 3 * LANES), F32),
+            pltpu.VMEM((4, 288, LANES), F32),
+        ],
+        compiler_params=pltpu.CompilerParams(vmem_limit_bytes=LIMIT),
+        name="temporal_tout",
+    )(me, *pieces)
+
+
+def partial_kernel(tout_ref, grad_ref, out_ref, full, piece, *, scale):
+    total = jnp.dot(tout_ref[0], grad_ref[0], preferred_element_type=F32)
+    for a in range(1, 4):
+        total = total + jnp.dot(tout_ref[a], grad_ref[a], preferred_element_type=F32)
+    full[...] = total * scale
+    piece[...] = jnp.zeros_like(piece)
+
+    for s in range(32):
+        for tile in range(9):
+            at = slice(tile * LANES, (tile + 1) * LANES)
+            piece[tile * 8 : tile * 8 + 8] = full[8 * s : 8 * s + 8, at]
+            piece[72 + tile : 73 + tile] = full[256 + s : 257 + s, at]
+        out_ref[s] = piece[...].astype(BF16)
+
+
+def weight_partial(tout, grads, scale):
+    return pl.pallas_call(
+        functools.partial(partial_kernel, scale=scale),
+        out_shape=jax.ShapeDtypeStruct((32, 96, LANES), BF16),
+        in_specs=vmem_specs(2),
+        out_specs=pl.BlockSpec(memory_space=pltpu.VMEM),
+        scratch_shapes=[pltpu.VMEM((288, 1152), F32), pltpu.VMEM((96, LANES), F32)],
+        compiler_params=pltpu.CompilerParams(vmem_limit_bytes=LIMIT),
+        name="weight_partial",
+    )(tout, grads)
+
+
+def weight_sum_kernel(dp_ref, in_ref, keep_ref, send_ref, rows, parts):
+    total = in_ref[0].astype(F32)
+    for s in range(1, 32):
+        total = total + in_ref[s].astype(F32)
+    rows[8:16] = jnp.zeros((8, 1152), F32)
+    for tile in range(9):
+        at = slice(tile * LANES, (tile + 1) * LANES)
+        rows[0:8, at] = total[tile * 8 : tile * 8 + 8]
+        rows[8:9, at] = total[72 + tile : 73 + tile]
+    for d in range(4):
+        parts[d] = rows[:, d * 288 : (d + 1) * 288]
+    dp = dp_ref[0]
+    keep_ref[0] = parts[dp]
+    keep_ref[1] = parts[lax.rem(dp + 2, 4)]
+    other = dp + 1 - 2 * lax.rem(dp, 2)
+    send_ref[0] = parts[other]
+    send_ref[1] = parts[lax.rem(other + 2, 4)]
+
+
+def weight_sum(dp, received):
+    shape = jax.ShapeDtypeStruct((2, 16, 288), F32)
+    return pl.pallas_call(
+        weight_sum_kernel,
+        out_shape=(shape, shape),
+        in_specs=[pl.BlockSpec(memory_space=pltpu.SMEM)] + vmem_specs(1),
+        out_specs=tuple(vmem_specs(2)),
+        scratch_shapes=[pltpu.VMEM((16, 1152), F32), pltpu.VMEM((4, 16, 288), F32)],
+        compiler_params=pltpu.CompilerParams(vmem_limit_bytes=LIMIT),
+        name="weight_sum",
+    )(dp, received)
+
+
+def weight_share_kernel(mine_ref, got_ref, out_ref, wide, folded):
+    wide[...] = jnp.zeros_like(wide)
+    folded[...] = jnp.zeros_like(folded)
+    wide[:, :288] = mine_ref[...] + got_ref[...]
+    for tile in range(3):
+        at = slice(tile * LANES, (tile + 1) * LANES)
+        folded[tile * 8 : tile * 8 + 8] = wide[0:8, at]
+        folded[24 + tile : 25 + tile] = wide[8:9, at]
+    copy = folded[...].astype(BF16)
+    for s in range(32):
+        out_ref[s] = copy
+
+
+def weight_share(mine, got):
+    return pl.pallas_call(
+        weight_share_kernel,
+        out_shape=jax.ShapeDtypeStruct((32, 32, LANES), BF16),
+        in_specs=vmem_specs(2),
+        out_specs=pl.BlockSpec(memory_space=pltpu.VMEM),
+        scratch_shapes=[pltpu.VMEM((16, 3 * LANES), F32), pltpu.VMEM((32, LANES), F32)],
+        compiler_params=pltpu.CompilerParams(vmem_limit_bytes=LIMIT),
+        name="weight_share",
+    )(mine, got)
+
+
+def weight_final_kernel(in_ref, out_ref, full):
+    for s in range(32):
+        block = in_ref[s].astype(F32)
+        for tile in range(3):
+            at = slice(tile * LANES, (tile + 1) * LANES)
+            full[8 * s : 8 * s + 8, at] = block[tile * 8 : tile * 8 + 8]
+            full[256 + s : 257 + s, at] = block[24 + tile : 25 + tile]
+    out_ref[...] = full[...].T[:288]
+
+
+def weight_final(gathered):
+    return pl.pallas_call(
+        weight_final_kernel,
+        out_shape=jax.ShapeDtypeStruct((288, 288), F32),
+        in_specs=vmem_specs(1),
+        out_specs=pl.BlockSpec(memory_space=pltpu.VMEM),
+        scratch_shapes=[pltpu.VMEM((288, 3 * LANES), F32)],
+        compiler_params=pltpu.CompilerParams(vmem_limit_bytes=LIMIT),
+        name="weight_final",
+    )(gathered)
+
+
+def temporal_kernel(
+    me_ref, in0, in1, in2, in3, grad_ref, w_ref, out0, out1, out2, out3, wide, back
+):
+    me = me_ref[0]
+    for shift, ref in enumerate((in0, in1, in2, in3)):
+        wide[shift, :, : 3 * LANES] = ref[...].astype(F32)
+        grads = grad_ref[lax.rem(me + 4 - shift, 4)]
+        tgrad = rounded(jnp.dot(grads, w_ref[...], preferred_element_type=F32))
+        wide[shift, :, 3 * LANES :] = tgrad.T
+    scale = 1.0 / math.sqrt(HDIM)
+
+    def body(head, _):
+        rows = pl.ds(pl.multiple_of(head * HDIM, 8), HDIM)
+        queries = head_rows(wide, head, 0)
+        keys = both_ways(head_rows(wide, head, 1))
+        values = both_ways(head_rows(wide, head, 2))
+        grads = head_rows(wide, head, 3)
+        low_w, low_s = [], []
+        for shift in range(4):
+            weights = frame_weights(queries[shift], keys)
+            pgrad = rows_of([grads[shift] * value for value in values])
+            inner = jnp.sum(weights * pgrad, axis=0, keepdims=True)
+            low_w.append(rounded(weights))
+            low_s.append(rounded(weights * (pgrad - inner)))
+            dq = low_s[shift][0:1] * keys[0]
+            for j in range(1, 8):
+                dq = dq + low_s[shift][j : j + 1] * keys[j]
+            back[shift, rows, 0:LANES] = dq * scale
+        for b in range(4):
+            for part, (coefs, terms, factor) in enumerate(
+                ((low_s, queries, scale), (low_w, grads, 1.0)), 1
+            ):
+                sums = []
+                for way in range(2):
+                    j = 2 * b + way
+                    total = coefs[0][j : j + 1] * terms[0]
+                    for shift in range(1, 4):
+                        total = total + coefs[shift][j : j + 1] * terms[shift]
+                    sums.append(total)
+                back[b, rows, part * LANES : (part + 1) * LANES] = (
+                    sums[0] + flip(sums[1])
+                ) * factor
+        return 0
+
+    lax.fori_loop(0, 4, body, 0)
+    for shift, out in enumerate((out0, out1, out2, out3)):
+        out[...] = back[shift].astype(BF16)
+
+
+def temporal_back(me, pieces, grads, w):
+    shape = jax.ShapeDtypeStruct((288, 3 * LANES), BF16)
+    return pl.pallas_call(
+        temporal_kernel,
+        out_shape=(shape,) * 4,
+        in_specs=[pl.BlockSpec(memory_space=pltpu.SMEM)] + vmem_specs(6),
+        out_specs=tuple(vmem_specs(4)),
+        scratch_shapes=[
+            pltpu.VMEM((4, 288, 4 * LANES), F32),
+            pltpu.VMEM((4, 288, 3 * LANES), F32),
+        ],
+        compiler_params=pltpu.CompilerParams(vmem_limit_bytes=LIMIT),
+        name="temporal_back",
+    )(me, *pieces, grads, w)
+
+
+def receive_kernel(me_ref, in0, in1, in2, in3, dq_ref, dk_ref, dv_ref, held):
+    me = me_ref[0]
+    for shift, ref in enumerate((in0, in1, in2, in3)):
+        held[lax.rem(me + shift, 4)] = ref[...]
+    for part, out in enumerate((dq_ref, dk_ref, dv_ref)):
+        at = slice(part * LANES, (part + 1) * LANES)
+        columns = jnp.concatenate([held[t, :, at] for t in range(4)], axis=0).astype(F32)
+        rows = columns.T.astype(BF16)
+        out[0] = rows[:HALF]
+        out[1] = rows[HALF:]
+
+
+def receive(me, pieces):
+    shape = jax.ShapeDtypeStruct((2, HALF, HEADS * HDIM), BF16)
+    return pl.pallas_call(
+        receive_kernel,
+        out_shape=(shape,) * 3,
+        in_specs=[pl.BlockSpec(memory_space=pltpu.SMEM)] + vmem_specs(4),
+        out_specs=tuple(vmem_specs(3)),
+        scratch_shapes=[pltpu.VMEM((4, 288, 3 * LANES), BF16)],
+        compiler_params=pltpu.CompilerParams(vmem_limit_bytes=LIMIT),
+        name="temporal_unpack",
+    )(me, *pieces)
 
 
 def space_perm(move):
@@ -241,32 +501,36 @@
     return pairs
 
 
-def collect(block, own, moves, axis):
-    size = len(moves) + 1
-    out = jnp.zeros((size,) + block.shape, block.dtype)
-    out = lax.dynamic_update_index_in_dim(out, block, own, 0)
-    for shift, move in enumerate(moves, 1):
-        got = lax.ppermute(block, axis, move)
-        out = lax.dynamic_update_index_in_dim(out, got, lax.rem(own + size - shift, size), 0)
-    return out
-
-
-def sum_weight_grad(partial):
-    rows, width = partial.shape
-    blocks = partial.astype(BF16).reshape(4, 32, rows // 128, width).transpose(1, 0, 2, 3)
-    got = lax.all_to_all(blocks, "space", split_axis=0, concat_axis=0, tiled=True)
-    mine = jnp.sum(got.astype(F32), axis=0)
-    dp = lax.axis_index("dp")
-    total = lax.dynamic_index_in_dim(mine, dp, 0, keepdims=False)
-    for shift in range(1, 4):
-        send = lax.dynamic_index_in_dim(mine, lax.rem(dp + shift, 4), 0, keepdims=False)
-        total = total + lax.ppermute(send, "dp", [(i, (i + shift) % 4) for i in range(4)])
+Y_MOVES = [space_perm(lambda z, y, c, s=s: (z, y ^ s, c)) for s in (1, 2)]
+C_MOVE = space_perm(lambda z, y, c: (z, y, c ^ 1))
+SWAP = [[(i, i ^ s) for i in range(4)] for s in (1, 2)]
+RING = [[(i, (i + s) % 4) for i in range(4)] for s in (1, 2, 3)]
+RING_BACK = [[(i, (i - s) % 4) for i in range(4)] for s in (1, 2, 3)]
+
+
+def pair_up(block, bit, move, axis):
+    got = lax.ppermute(block, axis, move)
+    low = jnp.where(bit == 0, block, got)
+    high = jnp.where(bit == 0, got, block)
+    return jnp.stack([low, high])
+
+
+def gather_dp(w):
+    space, dp = lax.axis_index("space"), lax.axis_index("dp")
+    y, c = lax.rem(space // 2, 4), lax.rem(space, 2)
+    own = lax.dynamic_index_in_dim(w.reshape(2, 4, 36, 288), c, 0, keepdims=False)
+    own = lax.dynamic_index_in_dim(own, y, 0, keepdims=False)
+    out = pair_up(own, lax.rem(dp, 2), SWAP[0], "dp")
+    return pair_up(out, dp // 2, SWAP[1], "dp")
+
+
+def gather_near(block):
     space = lax.axis_index("space")
-    z, y, c = space // 8, lax.rem(space // 2, 4), lax.rem(space, 2)
-    out = collect(total, z, [space_perm(lambda a, b, e, s=s: (a + s, b, e)) for s in (1, 2, 3)], "space")
-    out = collect(out, y, [space_perm(lambda a, b, e, s=s: (a, b + s, e)) for s in (1, 2, 3)], "space")
-    out = collect(out, c, [space_perm(lambda a, b, e: (a, b, e + 1))], "space")
-    return out.transpose(2, 1, 0, 3, 4).reshape(rows // 4, width)
+    y, c = lax.rem(space // 2, 4), lax.rem(space, 2)
+    out = pair_up(block, lax.rem(y, 2), Y_MOVES[0], "space")
+    out = pair_up(out, y // 2, Y_MOVES[1], "space")
+    out = pair_up(out, c, C_MOVE, "space")
+    return out.transpose(3, 4, 0, 1, 2, 5, 6).reshape(1152, 288)
 
 
 def shards(
@@ -280,57 +544,40 @@
     grad_out,
     w_tout,
 ):
+    me = lax.axis_index("tm").reshape(1)
+    dp = lax.axis_index("dp").reshape(1)
+    grads = lax.all_gather(grad_out, "tm", axis=1, tiled=True).reshape(4, LANES, 1152)
     packed = pack(q_spatial[0], k_spatial[0], v_spatial[0], grad_spatial[0])
     received = lax.all_to_all(packed, "space", split_axis=0, concat_axis=0, tiled=True)
+
+    sends = send_pack(me, q_temporal[0], k_temporal[0], v_temporal[0])
+    pieces = (sends[0],) + tuple(
+        lax.ppermute(sends[shift], "tm", RING[shift - 1]) for shift in (1, 2, 3)
+    )
+    tout = temporal_out(me, pieces)
+    partial = weight_partial(tout, grads, 1.0 / math.sqrt(65536))
+    weight = gather_dp(w_tout)
+
+    received, partial = lax.optimization_barrier((received, partial))
+    summed = lax.all_to_all(partial, "space", split_axis=0, concat_axis=0, tiled=True)
     results = attend(received)
+    results, summed, weight, *pieces = lax.optimization_barrier((results, summed, weight) + pieces)
     returned = lax.all_to_all(results, "space", split_axis=0, concat_axis=0, tiled=True)
+
+    keep, send = weight_sum(dp, summed)
+    keep = keep + lax.ppermute(send, "dp", SWAP[0])
+    shared = weight_share(keep[0], lax.ppermute(keep[1], "dp", SWAP[1]))
+
+    backs = temporal_back(me, pieces, grads, gather_near(weight))
+    shared, returned = lax.optimization_barrier((shared, returned))
+    gathered = lax.all_to_all(shared, "space", split_axis=0, concat_axis=0, tiled=True)
+    homes = (backs[0],) + tuple(
+        lax.ppermute(backs[shift], "tm", RING_BACK[shift - 1]) for shift in (1, 2, 3)
+    )
+    dq_t, dk_t, dv_t = receive(me, homes)
     dq, dk, dv = unpack(returned)
-
-    heads_in = (
-        lax.all_to_all(q_temporal, "tm", split_axis=3, concat_axis=1, tiled=True),
-        lax.all_to_all(k_temporal, "tm", split_axis=3, concat_axis=1, tiled=True),
-        lax.all_to_all(v_temporal, "tm", split_axis=3, concat_axis=1, tiled=True),
-    )
-    grad_all = lax.all_gather(grad_out, "tm", axis=1, tiled=True)
-    width = grad_out.shape[3]
-    all_frames = grad_all.shape[1]
-    tokens = grad_all.shape[2]
-    grad_rows = grad_all.reshape(all_frames * tokens, width)
-    local_width = w_tout.shape[1]
-    local_heads = local_width // HDIM
-    head_grad = jnp.dot(
-        grad_rows,
-        lax.all_gather(w_tout, "dp", axis=0, tiled=True),
-        preferred_element_type=jnp.float32,
-    )
-
-    def head_split(field):
-        return field.reshape(all_frames, tokens, local_heads, HDIM)
-
-    def head_join(field):
-        return field.reshape(1, all_frames, tokens, local_width)
-
-    temporal = frames_back(
-        head_split(heads_in[0]),
-        head_split(heads_in[1]),
-        head_split(heads_in[2]),
-        head_split(head_grad.astype(jnp.bfloat16)),
-    )
-    back = (
-        lax.all_to_all(head_join(temporal[0]), "tm", split_axis=1, concat_axis=3, tiled=True),
-        lax.all_to_all(head_join(temporal[1]), "tm", split_axis=1, concat_axis=3, tiled=True),
-        lax.all_to_all(head_join(temporal[2]), "tm", split_axis=1, concat_axis=3, tiled=True),
-    )
-    output_rows = temporal[3].reshape(all_frames * tokens, local_width)
-    weight_scale = 1.0 / math.sqrt(65536)
-    partial = (
-        lax.dot_general(
-            grad_rows, output_rows, (((0,), (0,)), ((), ())), preferred_element_type=jnp.float32
-        )
-        * weight_scale
-    )
-    weight_grad = sum_weight_grad(partial)
-    return (dq[None], dk[None], dv[None], back[0], back[1], back[2], weight_grad)
+    weight_grad = weight_final(gathered)
+    return (dq[None], dk[None], dv[None], dq_t[None], dk_t[None], dv_t[None], weight_grad)
 
 
 def solution(mesh):

time: 278 us -> 235 us (0.85)
  blocking collectives: 36.4 us -> 0 us
  local copies, waits for them, and re-layouts: 27.3 us -> 4.69 us
  Pallas kernels: 28.6 us -> 51.2 us
  matrix products: 8.51 us -> 0 us
    all_gather x1 -> x0, blocking collectives: 36.4 us -> none  [shards(): lax.all_gather(w_tout, 'dp', axis=0, tiled=True)]
    ppermute x10 -> x13, waiting for transfers between devices: 11.3 us -> 44.3 us  [the longest x5 11.7 us: pair_up(): got = lax.ppermute(block, axis, move)]
    all_to_all x1, waiting for transfers between devices: 24.3 us -> 0.01 us  [shards(): lax.all_to_all(packed, 'space', split_axis=0, concat_axis=0, tiled=True)]
    pallas_call x0 -> x8, Pallas kernels: none -> 22.7 us  [the longest x1 5.85 us: temporal_back(): pl.pallas_call(temporal_kernel, out_shape=(shape,) * 4, in_specs=[pl.Bloc...]
    all_to_all x7 -> x2, waiting for transfers between devices: 19.8 us -> 0.01 us  [the longest x1 0.01 us: shards(): lax.all_to_all(partial, 'space', split_axis=0, concat_axis=0, tiled=True)]
    all_to_all x1, starting transfers between devices: 23.5 us -> 10.5 us  [shards(): lax.all_to_all(packed, 'space', split_axis=0, concat_axis=0, tiled=True)]
    all_to_all x1, starting transfers between devices: 7.73 us -> 19.2 us  [shards(): lax.all_to_all(results, 'space', split_axis=0, concat_axis=0, tiled=True)]
    all_gather x1, waiting for transfers between devices: 0.02 us -> 11.3 us  [shards(): lax.all_gather(grad_out, 'tm', axis=1, tiled=True).reshape(4, LANES, 1152)]
  transfers between devices with their start and end apart: 20 -> 18, of which waited for: 11 -> 11; matrix products, arithmetic and copies ran while one was open for 9% -> 1% of each run, Pallas kernels for 9% -> 20%
where the time goes in v2:
time: 235 us; the launch traced here: 234 us
  starting transfers between devices  106 us (45%)
  waiting for transfers between devices  56.3 us (24%)
  Pallas kernels  51.2 us (22%)
  between operations  14.4 us (6%)
  local copies, waits for them, and re-layouts  4.69 us (2%)
    ppermute x5, starting transfers between devices, pair_up(): got = lax.ppermute(block, axis, move)  27.4 us
    pallas_call x1, Pallas kernels, attend(): pl.pallas_call(functools.partial(attend_kernel, step=step), out_shape=jax...  23.4 us
    all_to_all x1, starting transfers between devices, shards(): lax.all_to_all(results, 'space', split_axis=0, concat_axis=0, tiled=True)  19.2 us
    all_to_all x1, starting transfers between devices, shards(): lax.all_to_all(shared, 'space', split_axis=0, concat_axis=0, tiled=True)  13.7 us
    ppermute x5, waiting for transfers between devices, pair_up(): got = lax.ppermute(block, axis, move)  11.7 us
    all_gather x1, waiting for transfers between devices, shards(): lax.all_gather(grad_out, 'tm', axis=1, tiled=True).reshape(4, LANES, 1152)  11.3 us
    all_to_all x1, starting transfers between devices, shards(): lax.all_to_all(packed, 'space', split_axis=0, concat_axis=0, tiled=True)  10.5 us
    ppermute x3, starting transfers between devices, shards(): lax.ppermute(sends[shift], 'tm', RING[shift - 1])  10.2 us
  transfers between devices with their start and end apart: 18, of which 11 were waited for; matrix products, arithmetic and copies ran while one was open for 1% of the time, Pallas kernels for 20%

profile of v2, /device:TPU:1, one launch (start us, length us, event | category | flops | bytes accessed | tf_op | source)
XLA Modules:
  0.0 234.0 jit_solution(15153858224637366602)
XLA Ops:
  7.2 2.6 %spatial_pack.1 = bf16[32,2,72,128]{3,2,1,0:T(8,128)(2,1)} custom-call(bf16[2,64,1152]{2,1,0:T(8,128)(2,1)} %bitcast.55, bf16[2,64,1152]{2,1,0:T(8,128)(2,1)} %bitcast.56, bf16[2,64,1152]{2,1,0:T(8,128)(2,1)} %bitcast.57, bf16[2,64,1152]{2,1,0:T(8,128)(2,1)} %bitcast.58), custom_call_target="tpu_custom_call" | custom-call | tf_op jit(solution)/shard_map/spatial_pack/pallas_call | solution.py:45
  9.8 10.5 %all-to-all-start = ((bf16[32,2,72,128]{3,2,1,0:T(8,128)(2,1)}), bf16[32,2,72,128]{3,2,1,0:T(8,128)(2,1)S(1)}, u32[]{:S(2)}, u32[]{:S(2)}) async-start(bf16[32,2,72,128]{3,2,1,0:T(8,128)(2,1)} %spatial_pack.1), calls=%async_computation | async-start | bytes 2359296 | tf_op jit(solution)/shard_map/all_to_all | solution.py:551
  20.3 0.0 all-gather.2.cloned.1.call-start
  20.3 0.7 all-gather.2.cloned.1.call-update
  21.0 2.5 %temporal_pack.1 = (bf16[288,384]{1,0:T(8,128)(2,1)}, bf16[288,384]{1,0:T(8,128)(2,1)}, bf16[288,384]{1,0:T(8,128)(2,1)}, bf16[288,384]{1,0:T(8,128)(2,1)}) custom-call(s32[1]{0:T(128)} %bitcast.5.me_ref, bf16[2,64,1152]{2,1,0:T(8,128)(2,1)} %bitcast.59, bf16[2,64,1152]{2,1,0:T(8,128)(2,1)} %bitcast.60, bf16[2,64,1152]{2,1,0:T(8,128)(2,1)} %bitcast.61), custom_call_target="tpu_custom_call" | custom-call | tf_op jit(solution)/shard_map/temporal_pack/pallas_call | solution.py:223
  23.6 2.8 %collective-permute-start = (bf16[288,384]{1,0:T(8,128)(2,1)}, bf16[288,384]{1,0:T(8,128)(2,1)S(1)}, u32[]{:S(2)}, u32[]{:S(2)}) collective-permute-start(bf16[288,384]{1,0:T(8,128)(2,1)} %get-tuple-element.35), channel_id=1, source_target_pairs={{0,32},{32,64},{64,96},{96,0},{1,33},{33,65},{65,97},{97,1},{2,34}... | collective-permute-start | bytes 663560 | tf_op jit(solution)/shard_map/ppermute | solution.py:555
  26.4 4.4 %collective-permute-start.1 = (bf16[288,384]{1,0:T(8,128)(2,1)}, bf16[288,384]{1,0:T(8,128)(2,1)S(1)}, u32[]{:S(2)}, u32[]{:S(2)}) collective-permute-start(bf16[288,384]{1,0:T(8,128)(2,1)} %get-tuple-element.36), channel_id=1, source_target_pairs={{0,64},{32,96},{64,0},{96,32},{1,65},{33,97},{65,1},{97,33},{2,66}... | collective-permute-start | bytes 663560 | tf_op jit(solution)/shard_map/ppermute | solution.py:555
  30.8 3.1 %collective-permute-start.2 = (bf16[288,384]{1,0:T(8,128)(2,1)}, bf16[288,384]{1,0:T(8,128)(2,1)S(1)}, u32[]{:S(2)}, u32[]{:S(2)}) collective-permute-start(bf16[288,384]{1,0:T(8,128)(2,1)} %get-tuple-element.37), channel_id=1, source_target_pairs={{0,96},{32,0},{64,32},{96,64},{1,97},{33,1},{65,33},{97,65},{2,98}... | collective-permute-start | bytes 663560 | tf_op jit(solution)/shard_map/ppermute | solution.py:555
  33.8 0.0 collective-permute-done.in1
  33.8 0.0 copy-start.4
  33.9 5.2 %collective-permute-done.1.in2 = bf16[288,384]{1,0:T(8,128)(2,1)S(1)} collective-permute-done((bf16[288,384]{1,0:T(8,128)(2,1)}, bf16[288,384]{1,0:T(8,128)(2,1)S(1)}, u32[]{:S(2)}, u32[]{:S(2)}) %collective-permute-start.1) | collective-permute-done | bytes 221216 | tf_op jit(solution)/shard_map/ppermute | solution.py:555
  39.1 1.3 collective-permute-done.2.in3
  40.4 0.0 copy-done.5
  40.5 0.7 copy-done.6
  41.1 3.1 %temporal_tout.1.tout_ref = bf16[4,288,128]{2,1,0:T(8,128)(2,1)} custom-call(s32[1]{0:T(128)} %bitcast.5.me_ref, bf16[288,384]{1,0:T(8,128)(2,1)} %get-tuple-element.48.in0, bf16[288,384]{1,0:T(8,128)(2,1)} %copy-done.4, bf16[288,384]{1,0:T(8,128)(2,1)} %copy-done.5, bf16[288,384]{1,0:T(8,128)(2,1)} %copy-done.6), custom_call_target="tpu_custom_call" | custom-call | tf_op jit(solution)/shard_map/temporal_tout/pallas_call | solution.py:285
  44.3 11.3 %all-gather.2.cloned.1.call-done = bf16[1,8,64,1152]{3,2,0,1:T(8,128)(2,1)} async-done(((bf16[1,2,64,1152]{3,2,0,1:T(8,128)(2,1)}), bf16[1,8,64,1152]{3,2,0,1:T(8,128)(2,1)}) %all-gather.2.cloned.1.call-update) | async-done | bytes 1179664 | tf_op jit(solution)/shard_map/all_gather | solution.py:549
  55.6 3.3 %weight_partial.1 = bf16[32,96,128]{2,1,0:T(8,128)(2,1)} custom-call(bf16[4,288,128]{2,1,0:T(8,128)(2,1)} %temporal_tout.1.tout_ref, bf16[4,128,1152]{2,1,0:T(8,128)(2,1)} %bitcast.53), custom_call_target="tpu_custom_call" | custom-call | tf_op jit(solution)/shard_map/weight_partial/pallas_call | solution.py:315
  58.9 0.0 all-to-all-done.in_ref
  58.9 9.2 %all-to-all-start.1 = ((bf16[32,96,128]{2,1,0:T(8,128)(2,1)}), bf16[32,96,128]{2,1,0:T(8,128)(2,1)S(1)}, u32[]{:S(2)}, u32[]{:S(2)}) async-start(bf16[32,96,128]{2,1,0:T(8,128)(2,1)} %weight_partial.1), calls=%async_computation.1 | async-start | bytes 1572864 | tf_op jit(solution)/shard_map/all_to_all | solution.py:562
  68.2 0.1 reshape.34
  68.3 7.4 %collective-permute-start.3 = (bf16[36,288]{1,0:T(8,128)(2,1)S(1)}, bf16[36,288]{1,0:T(8,128)(2,1)S(1)}, u32[]{:S(2)}, u32[]{:S(2)}) collective-permute-start(bf16[36,288]{1,0:T(8,128)(2,1)S(1)} %dynamic-slice_bitcast_fusion), channel_id=1, source_target_pairs={{0,128},{128,0},{256,384},{384,256},{1,129},{129,1},{257,385},{385... | collective-permute-start | bytes 62216 | tf_op jit(solution)/shard_map/ppermute | solution.py:512
  75.6 6.1 %collective-permute-done.3 = bf16[36,288]{1,0:T(8,128)(2,1)S(1)} collective-permute-done((bf16[36,288]{1,0:T(8,128)(2,1)S(1)}, bf16[36,288]{1,0:T(8,128)(2,1)S(1)}, u32[]{:S(2)}, u32[]{:S(2)}) %collective-permute-start.3) | collective-permute-done | bytes 20768 | tf_op jit(solution)/shard_map/ppermute | solution.py:512
  81.8 9.8 %collective-permute-start.4 = (bf16[2,36,288]{2,1,0:T(8,128)(2,1)S(1)}, bf16[2,36,288]{2,1,0:T(8,128)(2,1)S(1)}, u32[]{:S(2)}, u32[]{:S(2)}) collective-permute-start(bf16[2,36,288]{2,1,0:T(8,128)(2,1)S(1)} %pad_maximum_fusion.3), channel_id=1, source_target_pairs={{0,256},{128,384},{256,0},{384,128},{1,257},{129,385},{257,1},{385... | collective-permute-start | bytes 124424 | tf_op jit(solution)/shard_map/ppermute | solution.py:512
  91.7 3.9 %collective-permute-done.4 = bf16[2,36,288]{2,1,0:T(8,128)(2,1)S(1)} collective-permute-done((bf16[2,36,288]{2,1,0:T(8,128)(2,1)S(1)}, bf16[2,36,288]{2,1,0:T(8,128)(2,1)S(1)}, u32[]{:S(2)}, u32[]{:S(2)}) %collective-permute-start.4) | collective-permute-done | bytes 41504 | tf_op jit(solution)/shard_map/ppermute | solution.py:512
  95.7 23.4 %spatial_attention.1 = bf16[32,112,128]{2,1,0:T(8,128)(2,1)} custom-call(bf16[32,2,72,128]{3,2,1,0:T(8,128)(2,1)} %copy-done.2), custom_call_target="tpu_custom_call" | custom-call | flops 10737418240 | bytes 2200000 | tf_op jit(solution)/shard_map/spatial_attention/pallas_call | solution.py:146
  119.1 0.0 all-to-all-done.1.in_ref
  119.1 19.2 %all-to-all-start.2 = ((bf16[32,112,128]{2,1,0:T(8,128)(2,1)}), bf16[32,112,128]{2,1,0:T(8,128)(2,1)S(1)}, u32[]{:S(2)}, u32[]{:S(2)}) async-start(bf16[32,112,128]{2,1,0:T(8,128)(2,1)} %spatial_attention.1), calls=%async_computation.2 | async-start | bytes 1835008 | tf_op jit(solution)/shard_map/all_to_all | solution.py:565
  138.3 3.5 %collective-permute-start.7 = (bf16[2,2,36,288]{3,2,1,0:T(8,128)(2,1)S(1)}, bf16[2,2,36,288]{3,2,1,0:T(8,128)(2,1)S(1)}, u32[]{:S(2)}, u32[]{:S(2)}) collective-permute-start(bf16[2,2,36,288]{3,2,1,0:T(8,128)(2,1)S(1)} %pad_maximum_fusion.2), channel_id=1, source_target_pairs={{0,2},{1,3},{2,0},{3,1},{4,6},{5,7},{6,4},{7,5},{8,10},{9,11},{10,... | collective-permute-start | bytes 248840 | tf_op jit(solution)/shard_map/ppermute | solution.py:512
  141.8 0.0 copy-done.1
  141.8 1.9 weight_sum.1
  143.8 2.3 collective-permute-start.5
  146.1 8.5 %collective-permute-done.5 = f32[2,16,288]{2,1,0:T(8,128)S(1)} collective-permute-done((f32[2,16,288]{2,1,0:T(8,128)}, f32[2,16,288]{2,1,0:T(8,128)S(1)}, u32[]{:S(2)}, u32[]{:S(2)}) %collective-permute-start.5) | collective-permute-done | bytes 36896 | tf_op jit(solution)/shard_map/ppermute | solution.py:568
  154.6 0.8 add.20
  155.4 0.0 collective-permute-done.7
  155.5 0.1 pad_maximum_fusion.1
  155.5 4.6 %collective-permute-start.8 = (bf16[2,2,2,36,288]{4,3,0,2,1:T(8,128)(2,1)S(1)}, bf16[2,2,2,36,288]{4,3,0,2,1:T(8,128)(2,1)S(1)}, u32[]{:S(2)}, u32[]{:S(2)}) collective-permute-start(bf16[2,2,2,36,288]{4,3,0,2,1:T(8,128)(2,1)S(1)} %pad_maximum_fusion.1), channel_id=1, source_target_pairs={{0,4},{1,5},{2,6},{3,7},{4,0},{5,1},{6,2},{7,3},{8,12},{9,13},{10,... | collective-permute-start | bytes 497672 | tf_op jit(solution)/shard_map/ppermute | solution.py:512
  160.1 0.6 slice_bitcast_fusion
  160.7 5.3 %collective-permute-start.6 = (f32[16,288]{1,0:T(8,128)S(1)}, f32[16,288]{1,0:T(8,128)S(1)}, u32[]{:S(2)}, u32[]{:S(2)}) collective-permute-start(f32[16,288]{1,0:T(8,128)S(1)} %get-tuple-element.71), channel_id=1, source_target_pairs={{0,256},{128,384},{256,0},{384,128},{1,257},{129,385},{257,1},{385... | collective-permute-start | bytes 55304 | tf_op jit(solution)/shard_map/ppermute | solution.py:569
  166.0 7.9 %collective-permute-done.6.got_ref = f32[16,288]{1,0:T(8,128)S(1)} collective-permute-done((f32[16,288]{1,0:T(8,128)S(1)}, f32[16,288]{1,0:T(8,128)S(1)}, u32[]{:S(2)}, u32[]{:S(2)}) %collective-permute-start.6) | collective-permute-done | bytes 18464 | tf_op jit(solution)/shard_map/ppermute | solution.py:569
  174.0 0.6 copy-done.11
  174.6 1.5 weight_share.1
  176.1 0.0 collective-permute-done.8
  176.1 0.1 select_bitcast_fusion.3
  176.2 0.0 all-to-all-done.2.in_ref
  176.2 13.7 %all-to-all-start.3 = ((bf16[32,32,128]{2,1,0:T(8,128)(2,1)}), bf16[32,32,128]{2,1,0:T(8,128)(2,1)S(1)}, u32[]{:S(2)}, u32[]{:S(2)}) async-start(bf16[32,32,128]{2,1,0:T(8,128)(2,1)} %weight_share.1), calls=%async_computation.3 | async-start | bytes 524288 | tf_op jit(solution)/shard_map/all_to_all | solution.py:573
  189.9 0.1 pad_maximum_fusion
  190.0 2.1 collective-permute-start.9
  192.2 1.6 collective-permute-done.9
  193.8 0.2 select_bitcast_fusion.1
  193.9 0.2 maximum_bitcast_fusion
  194.1 1.3 reshape.35.w_ref
  195.4 5.8 %temporal_back.1 = (bf16[288,384]{1,0:T(8,128)(2,1)}, bf16[288,384]{1,0:T(8,128)(2,1)}, bf16[288,384]{1,0:T(8,128)(2,1)}, bf16[288,384]{1,0:T(8,128)(2,1)}) custom-call(s32[1]{0:T(128)} %bitcast.5.me_ref, bf16[288,384]{1,0:T(8,128)(2,1)} %get-tuple-element.48.in0, bf16[288,384]{1,0:T(8,128)(2,1)} %copy-done.4, bf16[288,384]{1,0:T(8,128)(2,1)} %copy-done.5, ...), custom_call_target="tpu_custom_call" | custom-call | tf_op jit(solution)/shard_map/temporal_back/pallas_call | solution.py:456
  201.3 2.2 collective-permute-start.10
  203.6 3.8 %collective-permute-start.11 = (bf16[288,384]{1,0:T(8,128)(2,1)}, bf16[288,384]{1,0:T(8,128)(2,1)S(1)}, u32[]{:S(2)}, u32[]{:S(2)}) collective-permute-start(bf16[288,384]{1,0:T(8,128)(2,1)} %get-tuple-element.55), channel_id=1, source_target_pairs={{0,64},{32,96},{64,0},{96,32},{1,65},{33,97},{65,1},{97,33},{2,66}... | collective-permute-start | bytes 663560 | tf_op jit(solution)/shard_map/ppermute | solution.py:575
  207.3 1.9 collective-permute-start.12
  209.2 0.9 collective-permute-done.10.in1
  210.2 3.4 %collective-permute-done.11.in2 = bf16[288,384]{1,0:T(8,128)(2,1)S(1)} collective-permute-done((bf16[288,384]{1,0:T(8,128)(2,1)}, bf16[288,384]{1,0:T(8,128)(2,1)S(1)}, u32[]{:S(2)}, u32[]{:S(2)}) %collective-permute-start.11) | collective-permute-done | bytes 221216 | tf_op jit(solution)/shard_map/ppermute | solution.py:575
  213.6 5.2 %collective-permute-done.12.in3 = bf16[288,384]{1,0:T(8,128)(2,1)S(1)} collective-permute-done((bf16[288,384]{1,0:T(8,128)(2,1)}, bf16[288,384]{1,0:T(8,128)(2,1)S(1)}, u32[]{:S(2)}, u32[]{:S(2)}) %collective-permute-start.12) | collective-permute-done | bytes 221216 | tf_op jit(solution)/shard_map/ppermute | solution.py:575
  218.8 0.7 copy-done.10
  219.5 2.5 %temporal_unpack.1 = (bf16[2,64,1152]{2,1,0:T(8,128)(2,1)}, bf16[2,64,1152]{2,1,0:T(8,128)(2,1)}, bf16[2,64,1152]{2,1,0:T(8,128)(2,1)}) custom-call(s32[1]{0:T(128)} %bitcast.5.me_ref, bf16[288,384]{1,0:T(8,128)(2,1)} %get-tuple-element.53.in0, bf16[288,384]{1,0:T(8,128)(2,1)} %copy-done.8, bf16[288,384]{1,0:T(8,128)(2,1)} %copy-done.9, ...), custom_call_target="tpu_custom_call" | custom-call | tf_op jit(solution)/shard_map/temporal_unpack/pallas_call | solution.py:484
  222.0 2.5 %spatial_unpack.1 = (bf16[2,64,1152]{2,1,0:T(8,128)(2,1)}, bf16[2,64,1152]{2,1,0:T(8,128)(2,1)}, bf16[2,64,1152]{2,1,0:T(8,128)(2,1)}) custom-call(bf16[32,112,128]{2,1,0:T(8,128)(2,1)} %copy-done), custom_call_target="tpu_custom_call" | custom-call | tf_op jit(solution)/shard_map/spatial_unpack/pallas_call | solution.py:193
  224.5 0.0 all-to-all-done.3.in_ref
  224.5 0.7 copy-done.3
  225.2 1.9 weight_final.1
  (23 shorter events, 0.2 us)
Async XLA Ops:
  9.8 49.1 %all-to-all-start = ((bf16[32,2,72,128]{3,2,1,0:T(8,128)(2,1)}), bf16[32,2,72,128]{3,2,1,0:T(8,128)(2,1)S(1)}, u32[]{:S(2)}, u32[]{:S(2)}) async-start(bf16[32,2,72,128]{3,2,1,0:T(8,128)(2,1)} %spatial_pack.1), calls=%async_computation | async-start | bytes 2359296 | tf_op jit(solution)/shard_map/all_to_all | solution.py:551
  20.3 35.3 %all-gather.2.cloned.1.call-start = ((), (), s32[]{:S(2)}) async-start(), calls=%async_computation.4 | async-start | bytes 1474560 | tf_op jit(solution)/shard_map/all_gather | solution.py:549
  23.6 10.3 %collective-permute-start = (bf16[288,384]{1,0:T(8,128)(2,1)}, bf16[288,384]{1,0:T(8,128)(2,1)S(1)}, u32[]{:S(2)}, u32[]{:S(2)}) collective-permute-start(bf16[288,384]{1,0:T(8,128)(2,1)} %get-tuple-element.35), channel_id=1, source_target_pairs={{0,32},{32,64},{64,96},{96,0},{1,33},{33,65},{65,97},{97,1},{2,34}... | collective-permute-start | bytes 663560 | tf_op jit(solution)/shard_map/ppermute | solution.py:555
  26.4 12.7 %collective-permute-start.1 = (bf16[288,384]{1,0:T(8,128)(2,1)}, bf16[288,384]{1,0:T(8,128)(2,1)S(1)}, u32[]{:S(2)}, u32[]{:S(2)}) collective-permute-start(bf16[288,384]{1,0:T(8,128)(2,1)} %get-tuple-element.36), channel_id=1, source_target_pairs={{0,64},{32,96},{64,0},{96,32},{1,65},{33,97},{65,1},{97,33},{2,66}... | collective-permute-start | bytes 663560 | tf_op jit(solution)/shard_map/ppermute | solution.py:555
  30.8 9.7 %collective-permute-start.2 = (bf16[288,384]{1,0:T(8,128)(2,1)}, bf16[288,384]{1,0:T(8,128)(2,1)S(1)}, u32[]{:S(2)}, u32[]{:S(2)}) collective-permute-start(bf16[288,384]{1,0:T(8,128)(2,1)} %get-tuple-element.37), channel_id=1, source_target_pairs={{0,96},{32,0},{64,32},{96,64},{1,97},{33,1},{65,33},{97,65},{2,98}... | collective-permute-start | bytes 663560 | tf_op jit(solution)/shard_map/ppermute | solution.py:555
  33.8 6.6 %copy-start.4 = (bf16[288,384]{1,0:T(8,128)(2,1)}, bf16[288,384]{1,0:T(8,128)(2,1)S(1)}, u32[]{:S(2)}) copy-start(bf16[288,384]{1,0:T(8,128)(2,1)S(1)} %collective-permute-done.in1) | copy-start | bytes 663556
  39.1 1.3 copy-start.5
  40.4 0.7 copy-start.6
  58.9 9.2 %copy-start.7 = (bf16[288,288]{1,0:T(8,128)(2,1)S(1)}, bf16[288,288]{1,0:T(8,128)(2,1)}, u32[]{:S(2)}) copy-start(bf16[288,288]{1,0:T(8,128)(2,1)} %param.17) | copy-start | bytes 497668
  58.9 22.9 %copy-start.2 = (bf16[32,2,72,128]{3,2,1,0:T(8,128)(2,1)}, bf16[32,2,72,128]{3,2,1,0:T(8,128)(2,1)S(1)}, u32[]{:S(2)}) copy-start(bf16[32,2,72,128]{3,2,1,0:T(8,128)(2,1)S(1)} %all-to-all-done.in_ref) | copy-start | bytes 3538948
  58.9 60.2 %all-to-all-start.1 = ((bf16[32,96,128]{2,1,0:T(8,128)(2,1)}), bf16[32,96,128]{2,1,0:T(8,128)(2,1)S(1)}, u32[]{:S(2)}, u32[]{:S(2)}) async-start(bf16[32,96,128]{2,1,0:T(8,128)(2,1)} %weight_partial.1), calls=%async_computation.1 | async-start | bytes 1572864 | tf_op jit(solution)/shard_map/all_to_all | solution.py:562
  68.3 13.5 %collective-permute-start.3 = (bf16[36,288]{1,0:T(8,128)(2,1)S(1)}, bf16[36,288]{1,0:T(8,128)(2,1)S(1)}, u32[]{:S(2)}, u32[]{:S(2)}) collective-permute-start(bf16[36,288]{1,0:T(8,128)(2,1)S(1)} %dynamic-slice_bitcast_fusion), channel_id=1, source_target_pairs={{0,128},{128,0},{256,384},{384,256},{1,129},{129,1},{257,385},{385... | collective-permute-start | bytes 62216 | tf_op jit(solution)/shard_map/ppermute | solution.py:512
  81.8 13.8 %collective-permute-start.4 = (bf16[2,36,288]{2,1,0:T(8,128)(2,1)S(1)}, bf16[2,36,288]{2,1,0:T(8,128)(2,1)S(1)}, u32[]{:S(2)}, u32[]{:S(2)}) collective-permute-start(bf16[2,36,288]{2,1,0:T(8,128)(2,1)S(1)} %pad_maximum_fusion.3), channel_id=1, source_target_pairs={{0,256},{128,384},{256,0},{384,128},{1,257},{129,385},{257,1},{385... | collective-permute-start | bytes 124424 | tf_op jit(solution)/shard_map/ppermute | solution.py:512
  119.1 22.7 %copy-start.1 = (bf16[32,96,128]{2,1,0:T(8,128)(2,1)}, bf16[32,96,128]{2,1,0:T(8,128)(2,1)S(1)}, u32[]{:S(2)}) copy-start(bf16[32,96,128]{2,1,0:T(8,128)(2,1)S(1)} %all-to-all-done.1.in_ref) | copy-start | bytes 2359300
  119.1 57.0 %all-to-all-start.2 = ((bf16[32,112,128]{2,1,0:T(8,128)(2,1)}), bf16[32,112,128]{2,1,0:T(8,128)(2,1)S(1)}, u32[]{:S(2)}, u32[]{:S(2)}) async-start(bf16[32,112,128]{2,1,0:T(8,128)(2,1)} %spatial_attention.1), calls=%async_computation.2 | async-start | bytes 1835008 | tf_op jit(solution)/shard_map/all_to_all | solution.py:565
  138.3 17.1 %collective-permute-start.7 = (bf16[2,2,36,288]{3,2,1,0:T(8,128)(2,1)S(1)}, bf16[2,2,36,288]{3,2,1,0:T(8,128)(2,1)S(1)}, u32[]{:S(2)}, u32[]{:S(2)}) collective-permute-start(bf16[2,2,36,288]{3,2,1,0:T(8,128)(2,1)S(1)} %pad_maximum_fusion.2), channel_id=1, source_target_pairs={{0,2},{1,3},{2,0},{3,1},{4,6},{5,7},{6,4},{7,5},{8,10},{9,11},{10,... | collective-permute-start | bytes 248840 | tf_op jit(solution)/shard_map/ppermute | solution.py:512
  143.8 10.8 %collective-permute-start.5 = (f32[2,16,288]{2,1,0:T(8,128)}, f32[2,16,288]{2,1,0:T(8,128)S(1)}, u32[]{:S(2)}, u32[]{:S(2)}) collective-permute-start(f32[2,16,288]{2,1,0:T(8,128)} %get-tuple-element.42), channel_id=1, source_target_pairs={{0,128},{128,0},{256,384},{384,256},{1,129},{129,1},{257,385},{385... | collective-permute-start | bytes 110600 | tf_op jit(solution)/shard_map/ppermute | solution.py:568
  155.5 20.6 %collective-permute-start.8 = (bf16[2,2,2,36,288]{4,3,0,2,1:T(8,128)(2,1)S(1)}, bf16[2,2,2,36,288]{4,3,0,2,1:T(8,128)(2,1)S(1)}, u32[]{:S(2)}, u32[]{:S(2)}) collective-permute-start(bf16[2,2,2,36,288]{4,3,0,2,1:T(8,128)(2,1)S(1)} %pad_maximum_fusion.1), channel_id=1, source_target_pairs={{0,4},{1,5},{2,6},{3,7},{4,0},{5,1},{6,2},{7,3},{8,12},{9,13},{10,... | collective-permute-start | bytes 497672 | tf_op jit(solution)/shard_map/ppermute | solution.py:512
  160.7 13.3 %collective-permute-start.6 = (f32[16,288]{1,0:T(8,128)S(1)}, f32[16,288]{1,0:T(8,128)S(1)}, u32[]{:S(2)}, u32[]{:S(2)}) collective-permute-start(f32[16,288]{1,0:T(8,128)S(1)} %get-tuple-element.71), channel_id=1, source_target_pairs={{0,256},{128,384},{256,0},{384,128},{1,257},{129,385},{257,1},{385... | collective-permute-start | bytes 55304 | tf_op jit(solution)/shard_map/ppermute | solution.py:569
  174.0 0.6 copy-start.11
  176.2 17.8 %copy-start = (bf16[32,112,128]{2,1,0:T(8,128)(2,1)}, bf16[32,112,128]{2,1,0:T(8,128)(2,1)S(1)}, u32[]{:S(2)}) copy-start(bf16[32,112,128]{2,1,0:T(8,128)(2,1)S(1)} %all-to-all-done.2.in_ref) | copy-start | bytes 2752516
  176.2 48.3 %all-to-all-start.3 = ((bf16[32,32,128]{2,1,0:T(8,128)(2,1)}), bf16[32,32,128]{2,1,0:T(8,128)(2,1)S(1)}, u32[]{:S(2)}, u32[]{:S(2)}) async-start(bf16[32,32,128]{2,1,0:T(8,128)(2,1)} %weight_share.1), calls=%async_computation.3 | async-start | bytes 524288 | tf_op jit(solution)/shard_map/all_to_all | solution.py:573
  190.0 3.8 %collective-permute-start.9 = (bf16[2,2,2,2,36,288]{5,4,1,0,3,2:T(8,128)(2,1)S(1)}, bf16[2,2,2,2,36,288]{5,4,1,0,3,2:T(8,128)(2,1)S(1)}, u32[]{:S(2)}, u32[]{:S(2)}) collective-permute-start(bf16[2,2,2,2,36,288]{5,4,1,0,3,2:T(8,128)(2,1)S(1)} %pad_maximum_fusion), channel_id=1, source_target_pairs={{0,1},{1,0},{2,3},{3,2},{4,5},{5,4},{6,7},{7,6},{8,9},{9,8},{10,11... | collective-permute-start | bytes 995336 | tf_op jit(solution)/shard_map/ppermute | solution.py:512
  201.3 8.9 %collective-permute-start.10 = (bf16[288,384]{1,0:T(8,128)(2,1)}, bf16[288,384]{1,0:T(8,128)(2,1)S(1)}, u32[]{:S(2)}, u32[]{:S(2)}) collective-permute-start(bf16[288,384]{1,0:T(8,128)(2,1)} %get-tuple-element.54), channel_id=1, source_target_pairs={{0,96},{32,0},{64,32},{96,64},{1,97},{33,1},{65,33},{97,65},{2,98}... | collective-permute-start | bytes 663560 | tf_op jit(solution)/shard_map/ppermute | solution.py:575
  203.6 10.1 %collective-permute-start.11 = (bf16[288,384]{1,0:T(8,128)(2,1)}, bf16[288,384]{1,0:T(8,128)(2,1)S(1)}, u32[]{:S(2)}, u32[]{:S(2)}) collective-permute-start(bf16[288,384]{1,0:T(8,128)(2,1)} %get-tuple-element.55), channel_id=1, source_target_pairs={{0,64},{32,96},{64,0},{96,32},{1,65},{33,97},{65,1},{97,33},{2,66}... | collective-permute-start | bytes 663560 | tf_op jit(solution)/shard_map/ppermute | solution.py:575
  207.3 11.5 %collective-permute-start.12 = (bf16[288,384]{1,0:T(8,128)(2,1)}, bf16[288,384]{1,0:T(8,128)(2,1)S(1)}, u32[]{:S(2)}, u32[]{:S(2)}) collective-permute-start(bf16[288,384]{1,0:T(8,128)(2,1)} %get-tuple-element.56), channel_id=1, source_target_pairs={{0,32},{32,64},{64,96},{96,0},{1,33},{33,65},{65,97},{97,1},{2,34}... | collective-permute-start | bytes 663560 | tf_op jit(solution)/shard_map/ppermute | solution.py:575
  210.2 8.7 %copy-start.8 = (bf16[288,384]{1,0:T(8,128)(2,1)}, bf16[288,384]{1,0:T(8,128)(2,1)S(1)}, u32[]{:S(2)}) copy-start(bf16[288,384]{1,0:T(8,128)(2,1)S(1)} %collective-permute-done.10.in1) | copy-start | bytes 663556
  213.6 5.2 %copy-start.9 = (bf16[288,384]{1,0:T(8,128)(2,1)}, bf16[288,384]{1,0:T(8,128)(2,1)S(1)}, u32[]{:S(2)}) copy-start(bf16[288,384]{1,0:T(8,128)(2,1)S(1)} %collective-permute-done.11.in2) | copy-start | bytes 663556
  218.8 0.7 copy-start.10
  224.5 0.7 copy-start.3
Sparse Core Ops, SparseCore 0:
  23.2 32.3 all-gather.1

commit v3 on v2

--- a/solution.py
+++ b/solution.py
@@ -164,20 +164,20 @@
     )(received)
 
 
-def unpack_kernel(in_ref, dq_ref, dk_ref, dv_ref):
+def unpack_kernel(in_ref, dq_ref, dk_ref, dv_ref, dw_ref, full):
     low = low_lanes(HEADS * HDIM)
     values = []
     for frame in range(2):
-        items = [in_ref[frame * HEADS + head].astype(F32) for head in range(HEADS)]
+        items = [
+            in_ref[frame * HEADS + head, : HDIM + FOLD].astype(F32) for head in range(HEADS)
+        ]
         both = jnp.concatenate([item[:HDIM] for item in items], axis=0).T.astype(BF16)
         dq_ref[frame] = both[:HALF]
         dk_ref[frame] = both[HALF:]
         values.append(
             jnp.concatenate(
                 [
-                    jnp.concatenate(
-                        [item[HDIM:], swap(item[HDIM + 2 * FOLD - HDIM :])], axis=0
-                    )
+                    jnp.concatenate([item[HDIM:], swap(item[2 * FOLD :])], axis=0)
                     for item in items
                 ],
                 axis=0,
@@ -186,15 +186,26 @@
     both = jnp.where(low, values[0], swap(values[1])).T.astype(BF16)
     dv_ref[0] = both[:HALF]
     dv_ref[1] = both[HALF:]
+    for s in range(2 * HEADS):
+        block = in_ref[s, HDIM + FOLD :].astype(F32)
+        start = 144 * (s % 2) + 8 * (s // 2)
+        for tile in range(3):
+            at = slice(tile * LANES, (tile + 1) * LANES)
+            full[start : start + 8, at] = block[tile * 8 : tile * 8 + 8]
+        start = 144 * (s % 2) + 128 + s // 2
+        for r in range(3):
+            full[start : start + 1, 96 * r : 96 * r + 96] = block[16 + r : 17 + r, 32:]
+    dw_ref[...] = full[...].T[:288]
 
 
 def unpack(received):
     shape = jax.ShapeDtypeStruct((2, HALF, HEADS * HDIM), BF16)
     return pl.pallas_call(
         unpack_kernel,
-        out_shape=(shape, shape, shape),
+        out_shape=(shape, shape, shape, jax.ShapeDtypeStruct((288, 288), F32)),
         in_specs=vmem_specs(1),
-        out_specs=tuple(vmem_specs(3)),
+        out_specs=tuple(vmem_specs(4)),
+        scratch_shapes=[pltpu.VMEM((288, 3 * LANES), F32)],
         compiler_params=pltpu.CompilerParams(vmem_limit_bytes=LIMIT),
         name="spatial_unpack",
     )(received)
@@ -204,7 +215,8 @@
     return pltpu.roll(block, HALF, 1)
 
 
-def send_pack_kernel(me_ref, q_ref, k_ref, v_ref, out0, out1, out2, out3, held):
+def send_pack_kernel(me_ref, q_ref, k_ref, v_ref, w_ref, out0, out1, out2, out3, slice_ref, held):
+    slice_ref[...] = w_ref[me_ref[1]]
     for part, ref in enumerate((q_ref, k_ref, v_ref)):
         rows = jnp.concatenate([ref[0], ref[1]], axis=0).astype(F32)
         columns = rows.T.astype(BF16)
@@ -218,17 +230,18 @@
         out[...] = held[lax.rem(me + shift, 4)]
 
 
-def send_pack(me, q, k, v):
+def send_pack(me, q, k, v, w):
     shape = jax.ShapeDtypeStruct((288, 3 * LANES), BF16)
+    part = jax.ShapeDtypeStruct((36, 288), BF16)
     return pl.pallas_call(
         send_pack_kernel,
-        out_shape=(shape,) * 4,
-        in_specs=[pl.BlockSpec(memory_space=pltpu.SMEM)] + vmem_specs(3),
-        out_specs=tuple(vmem_specs(4)),
+        out_shape=(shape,) * 4 + (part,),
+        in_specs=[pl.BlockSpec(memory_space=pltpu.SMEM)] + vmem_specs(4),
+        out_specs=tuple(vmem_specs(5)),
         scratch_shapes=[pltpu.VMEM((4, 288, 3 * LANES), BF16)],
         compiler_params=pltpu.CompilerParams(vmem_limit_bytes=LIMIT),
         name="temporal_pack",
-    )(me, q, k, v)
+    )(me, q, k, v, w)
 
 
 def rows_of(values):
@@ -259,7 +272,13 @@
     return out
 
 
-def tout_kernel(me_ref, in0, in1, in2, in3, out_ref, wide, total):
+def pair_up(bit, own_ref, got_ref, out_ref):
+    out_ref[bit] = own_ref[...]
+    out_ref[1 - bit] = got_ref[...]
+
+
+def tout_kernel(me_ref, in0, in1, in2, in3, own_ref, got_ref, out_ref, w_ref, wide, total):
+    pair_up(lax.rem(me_ref[2], 2), own_ref, got_ref, w_ref)
     for shift, ref in enumerate((in0, in1, in2, in3)):
         wide[shift] = ref[...].astype(F32)
 
@@ -281,125 +300,105 @@
         out_ref[lax.rem(me + 4 - shift, 4)] = total[shift].astype(BF16)
 
 
-def temporal_out(me, pieces):
+def temporal_out(me, pieces, own, got):
     return pl.pallas_call(
         tout_kernel,
-        out_shape=jax.ShapeDtypeStruct((4, 288, LANES), BF16),
-        in_specs=[pl.BlockSpec(memory_space=pltpu.SMEM)] + vmem_specs(4),
-        out_specs=pl.BlockSpec(memory_space=pltpu.VMEM),
+        out_shape=(
+            jax.ShapeDtypeStruct((4, 288, LANES), BF16),
+            jax.ShapeDtypeStruct((2, 36, 288), BF16),
+        ),
+        in_specs=[pl.BlockSpec(memory_space=pltpu.SMEM)] + vmem_specs(6),
+        out_specs=tuple(vmem_specs(2)),
         scratch_shapes=[
             pltpu.VMEM((4, 288, 3 * LANES), F32),
             pltpu.VMEM((4, 288, LANES), F32),
         ],
         compiler_params=pltpu.CompilerParams(vmem_limit_bytes=LIMIT),
         name="temporal_tout",
-    )(me, *pieces)
-
-
-def partial_kernel(tout_ref, grad_ref, out_ref, full, piece, *, scale):
+    )(me, *pieces, own, got)
+
+
+def partial_kernel(
+    me_ref, tout_ref, grad_ref, own_ref, got_ref, keep_ref, send_ref, w_ref, full, *, scale
+):
+    pair_up(me_ref[2] // 2, own_ref, got_ref, w_ref)
     total = jnp.dot(tout_ref[0], grad_ref[0], preferred_element_type=F32)
     for a in range(1, 4):
         total = total + jnp.dot(tout_ref[a], grad_ref[a], preferred_element_type=F32)
-    full[...] = total * scale
-    piece[...] = jnp.zeros_like(piece)
-
-    for s in range(32):
-        for tile in range(9):
-            at = slice(tile * LANES, (tile + 1) * LANES)
-            piece[tile * 8 : tile * 8 + 8] = full[8 * s : 8 * s + 8, at]
-            piece[72 + tile : 73 + tile] = full[256 + s : 257 + s, at]
-        out_ref[s] = piece[...].astype(BF16)
-
-
-def weight_partial(tout, grads, scale):
+    total = total * scale
+    full[0] = total[:144]
+    full[1] = total[144:]
+    core = me_ref[3]
+    keep_ref[...] = full[core]
+    send_ref[...] = full[1 - core].astype(BF16)
+
+
+def weight_partial(me, tout, grads, own, got, scale):
     return pl.pallas_call(
         functools.partial(partial_kernel, scale=scale),
-        out_shape=jax.ShapeDtypeStruct((32, 96, LANES), BF16),
+        out_shape=(
+            jax.ShapeDtypeStruct((144, 1152), F32),
+            jax.ShapeDtypeStruct((144, 1152), BF16),
+            jax.ShapeDtypeStruct((2, 2, 36, 288), BF16),
+        ),
+        in_specs=[pl.BlockSpec(memory_space=pltpu.SMEM)] + vmem_specs(4),
+        out_specs=tuple(vmem_specs(3)),
+        scratch_shapes=[pltpu.VMEM((2, 144, 1152), F32)],
+        compiler_params=pltpu.CompilerParams(vmem_limit_bytes=LIMIT),
+        name="weight_partial",
+    )(me, tout, grads, own, got)
+
+
+def weight_split_kernel(keep_ref, got_ref, out_ref, full, part):
+    full[...] = keep_ref[...] + got_ref[...].astype(F32)
+    part[...] = jnp.zeros_like(part)
+    row = lax.broadcasted_iota(jnp.int32, (16, 8, LANES), 1)
+    for d in range(4):
+        part[:, :288] = full[:, d * 288 : (d + 1) * 288]
+        tiles = [
+            part[:128, tile * LANES : (tile + 1) * LANES].reshape(16, 8, LANES)
+            for tile in range(3)
+        ]
+        rest = part[128:144, :]
+        for r in range(3):
+            moved = jnp.concatenate(
+                [jnp.zeros((16, 32), F32), rest[:, 96 * r : 96 * r + 96]], axis=1
+            )
+            tiles[2] = tiles[2] + jnp.where(row == r, moved[:, None, :], 0.0)
+        out_ref[d * 16 : (d + 1) * 16] = jnp.concatenate(tiles, axis=1).astype(BF16)
+
+
+def weight_split(keep, got):
+    return pl.pallas_call(
+        weight_split_kernel,
+        out_shape=jax.ShapeDtypeStruct((64, 24, LANES), BF16),
         in_specs=vmem_specs(2),
         out_specs=pl.BlockSpec(memory_space=pltpu.VMEM),
-        scratch_shapes=[pltpu.VMEM((288, 1152), F32), pltpu.VMEM((96, LANES), F32)],
-        compiler_params=pltpu.CompilerParams(vmem_limit_bytes=LIMIT),
-        name="weight_partial",
-    )(tout, grads)
-
-
-def weight_sum_kernel(dp_ref, in_ref, keep_ref, send_ref, rows, parts):
+        scratch_shapes=[pltpu.VMEM((144, 1152), F32), pltpu.VMEM((144, 3 * LANES), F32)],
+        compiler_params=pltpu.CompilerParams(vmem_limit_bytes=LIMIT),
+        name="weight_split",
+    )(keep, got)
+
+
+def weight_join_kernel(spatial_ref, in_ref, out_ref):
     total = in_ref[0].astype(F32)
-    for s in range(1, 32):
+    for s in range(1, 64):
         total = total + in_ref[s].astype(F32)
-    rows[8:16] = jnp.zeros((8, 1152), F32)
-    for tile in range(9):
-        at = slice(tile * LANES, (tile + 1) * LANES)
-        rows[0:8, at] = total[tile * 8 : tile * 8 + 8]
-        rows[8:9, at] = total[72 + tile : 73 + tile]
-    for d in range(4):
-        parts[d] = rows[:, d * 288 : (d + 1) * 288]
-    dp = dp_ref[0]
-    keep_ref[0] = parts[dp]
-    keep_ref[1] = parts[lax.rem(dp + 2, 4)]
-    other = dp + 1 - 2 * lax.rem(dp, 2)
-    send_ref[0] = parts[other]
-    send_ref[1] = parts[lax.rem(other + 2, 4)]
-
-
-def weight_sum(dp, received):
-    shape = jax.ShapeDtypeStruct((2, 16, 288), F32)
-    return pl.pallas_call(
-        weight_sum_kernel,
-        out_shape=(shape, shape),
-        in_specs=[pl.BlockSpec(memory_space=pltpu.SMEM)] + vmem_specs(1),
-        out_specs=tuple(vmem_specs(2)),
-        scratch_shapes=[pltpu.VMEM((16, 1152), F32), pltpu.VMEM((4, 16, 288), F32)],
-        compiler_params=pltpu.CompilerParams(vmem_limit_bytes=LIMIT),
-        name="weight_sum",
-    )(dp, received)
-
-
-def weight_share_kernel(mine_ref, got_ref, out_ref, wide, folded):
-    wide[...] = jnp.zeros_like(wide)
-    folded[...] = jnp.zeros_like(folded)
-    wide[:, :288] = mine_ref[...] + got_ref[...]
-    for tile in range(3):
-        at = slice(tile * LANES, (tile + 1) * LANES)
-        folded[tile * 8 : tile * 8 + 8] = wide[0:8, at]
-        folded[24 + tile : 25 + tile] = wide[8:9, at]
-    copy = folded[...].astype(BF16)
+    copy = total.astype(BF16)
     for s in range(32):
-        out_ref[s] = copy
-
-
-def weight_share(mine, got):
-    return pl.pallas_call(
-        weight_share_kernel,
-        out_shape=jax.ShapeDtypeStruct((32, 32, LANES), BF16),
+        out_ref[s, : HDIM + FOLD] = spatial_ref[s]
+        out_ref[s, HDIM + FOLD :] = copy
+
+
+def weight_join(spatial, received):
+    return pl.pallas_call(
+        weight_join_kernel,
+        out_shape=jax.ShapeDtypeStruct((32, HDIM + FOLD + 24, LANES), BF16),
         in_specs=vmem_specs(2),
         out_specs=pl.BlockSpec(memory_space=pltpu.VMEM),
-        scratch_shapes=[pltpu.VMEM((16, 3 * LANES), F32), pltpu.VMEM((32, LANES), F32)],
-        compiler_params=pltpu.CompilerParams(vmem_limit_bytes=LIMIT),
-        name="weight_share",
-    )(mine, got)
-
-
-def weight_final_kernel(in_ref, out_ref, full):
-    for s in range(32):
-        block = in_ref[s].astype(F32)
-        for tile in range(3):
-            at = slice(tile * LANES, (tile + 1) * LANES)
-            full[8 * s : 8 * s + 8, at] = block[tile * 8 : tile * 8 + 8]
-            full[256 + s : 257 + s, at] = block[24 + tile : 25 + tile]
-    out_ref[...] = full[...].T[:288]
-
-
-def weight_final(gathered):
-    return pl.pallas_call(
-        weight_final_kernel,
-        out_shape=jax.ShapeDtypeStruct((288, 288), F32),
-        in_specs=vmem_specs(1),
-        out_specs=pl.BlockSpec(memory_space=pltpu.VMEM),
-        scratch_shapes=[pltpu.VMEM((288, 3 * LANES), F32)],
-        compiler_params=pltpu.CompilerParams(vmem_limit_bytes=LIMIT),
-        name="weight_final",
-    )(gathered)
+        compiler_params=pltpu.CompilerParams(vmem_limit_bytes=LIMIT),
+        name="weight_join",
+    )(spatial, received)
 
 
 def temporal_kernel(
@@ -492,45 +491,18 @@
     )(me, *pieces)
 
 
-def space_perm(move):
-    pairs = []
-    for index in range(32):
-        z, y, c = index // 8, (index // 2) % 4, index % 2
-        z, y, c = move(z, y, c)
-        pairs.append((index, (z % 4) * 8 + (y % 4) * 2 + c % 2))
-    return pairs
-
-
-Y_MOVES = [space_perm(lambda z, y, c, s=s: (z, y ^ s, c)) for s in (1, 2)]
-C_MOVE = space_perm(lambda z, y, c: (z, y, c ^ 1))
 SWAP = [[(i, i ^ s) for i in range(4)] for s in (1, 2)]
+SWAP_CORE = [(0, 1), (1, 0)]
 RING = [[(i, (i + s) % 4) for i in range(4)] for s in (1, 2, 3)]
 RING_BACK = [[(i, (i - s) % 4) for i in range(4)] for s in (1, 2, 3)]
 
 
-def pair_up(block, bit, move, axis):
-    got = lax.ppermute(block, axis, move)
-    low = jnp.where(bit == 0, block, got)
-    high = jnp.where(bit == 0, got, block)
-    return jnp.stack([low, high])
-
-
-def gather_dp(w):
-    space, dp = lax.axis_index("space"), lax.axis_index("dp")
-    y, c = lax.rem(space // 2, 4), lax.rem(space, 2)
-    own = lax.dynamic_index_in_dim(w.reshape(2, 4, 36, 288), c, 0, keepdims=False)
-    own = lax.dynamic_index_in_dim(own, y, 0, keepdims=False)
-    out = pair_up(own, lax.rem(dp, 2), SWAP[0], "dp")
-    return pair_up(out, dp // 2, SWAP[1], "dp")
-
-
 def gather_near(block):
-    space = lax.axis_index("space")
-    y, c = lax.rem(space // 2, 4), lax.rem(space, 2)
-    out = pair_up(block, lax.rem(y, 2), Y_MOVES[0], "space")
-    out = pair_up(out, y // 2, Y_MOVES[1], "space")
-    out = pair_up(out, c, C_MOVE, "space")
-    return out.transpose(3, 4, 0, 1, 2, 5, 6).reshape(1152, 288)
+    y, c = lax.axis_index("y"), lax.axis_index("c")
+    for bit, move, axis in ((lax.rem(y, 2), SWAP[0], "y"), (y // 2, SWAP[1], "y"), (c, SWAP_CORE, "c")):
+        got = lax.ppermute(block, axis, move)
+        block = jnp.stack([jnp.where(bit == 0, block, got), jnp.where(bit == 0, got, block)])
+    return block.transpose(3, 4, 0, 1, 2, 5, 6).reshape(1152, 288)
 
 
 def shards(
@@ -544,65 +516,50 @@
     grad_out,
     w_tout,
 ):
-    me = lax.axis_index("tm").reshape(1)
-    dp = lax.axis_index("dp").reshape(1)
+    y, c = lax.axis_index("y"), lax.axis_index("c")
+    me = jnp.stack([lax.axis_index("tm"), 4 * c + y, lax.axis_index("dp"), c])
+    space = ("z", "y", "c")
     grads = lax.all_gather(grad_out, "tm", axis=1, tiled=True).reshape(4, LANES, 1152)
     packed = pack(q_spatial[0], k_spatial[0], v_spatial[0], grad_spatial[0])
-    received = lax.all_to_all(packed, "space", split_axis=0, concat_axis=0, tiled=True)
-
-    sends = send_pack(me, q_temporal[0], k_temporal[0], v_temporal[0])
+    packed, q, k, v, w = lax.optimization_barrier(
+        (packed, q_temporal[0], k_temporal[0], v_temporal[0], w_tout.reshape(8, 36, 288))
+    )
+    received = lax.all_to_all(packed, space, split_axis=0, concat_axis=0, tiled=True)
+
+    *sends, own = send_pack(me, q, k, v, w)
+    got = lax.ppermute(own, "dp", SWAP[0])
     pieces = (sends[0],) + tuple(
         lax.ppermute(sends[shift], "tm", RING[shift - 1]) for shift in (1, 2, 3)
     )
-    tout = temporal_out(me, pieces)
-    partial = weight_partial(tout, grads, 1.0 / math.sqrt(65536))
-    weight = gather_dp(w_tout)
-
-    received, partial = lax.optimization_barrier((received, partial))
-    summed = lax.all_to_all(partial, "space", split_axis=0, concat_axis=0, tiled=True)
+    tout, own = temporal_out(me, pieces, own, got)
+    got = lax.ppermute(own, "dp", SWAP[1])
+    keep, send, weight = weight_partial(me, tout, grads, own, got, 1.0 / math.sqrt(65536))
+    blocks = weight_split(keep, lax.ppermute(send, "c", SWAP_CORE))
+
+    received, blocks = lax.optimization_barrier((received, blocks))
+    blocks = lax.all_to_all(blocks, ("dp", "z", "y"), split_axis=0, concat_axis=0, tiled=True)
     results = attend(received)
-    results, summed, weight, *pieces = lax.optimization_barrier((results, summed, weight) + pieces)
-    returned = lax.all_to_all(results, "space", split_axis=0, concat_axis=0, tiled=True)
-
-    keep, send = weight_sum(dp, summed)
-    keep = keep + lax.ppermute(send, "dp", SWAP[0])
-    shared = weight_share(keep[0], lax.ppermute(keep[1], "dp", SWAP[1]))
+    results, weight, *pieces = lax.optimization_barrier((results, weight) + pieces)
+    results = weight_join(results, blocks)
+    returned = lax.all_to_all(results, space, split_axis=0, concat_axis=0, tiled=True)
 
     backs = temporal_back(me, pieces, grads, gather_near(weight))
-    shared, returned = lax.optimization_barrier((shared, returned))
-    gathered = lax.all_to_all(shared, "space", split_axis=0, concat_axis=0, tiled=True)
     homes = (backs[0],) + tuple(
         lax.ppermute(backs[shift], "tm", RING_BACK[shift - 1]) for shift in (1, 2, 3)
     )
     dq_t, dk_t, dv_t = receive(me, homes)
-    dq, dk, dv = unpack(returned)
-    weight_grad = weight_final(gathered)
+    dq, dk, dv, weight_grad = unpack(returned)
     return (dq[None], dk[None], dv[None], dq_t[None], dk_t[None], dv_t[None], weight_grad)
 
 
 def solution(mesh):
+    sizes = (mesh.shape["dp"], mesh.shape["tm"], 4, 4, 2)
+    split = jax.sharding.Mesh(mesh.devices.reshape(sizes), ("dp", "tm", "z", "y", "c"))
+    field = P("dp", "tm", ("z", "y", "c"), None)
     return jax.shard_map(
         shards,
-        mesh=mesh,
-        in_specs=(
-            P("dp", "tm", "space", None),
-            P("dp", "tm", "space", None),
-            P("dp", "tm", "space", None),
-            P("dp", "tm", "space", None),
-            P("dp", "tm", "space", None),
-            P("dp", "tm", "space", None),
-            P("dp", "tm", "space", None),
-            P("dp", "tm", "space", None),
-            P("dp", "tm"),
-        ),
-        out_specs=(
-            P("dp", "tm", "space", None),
-            P("dp", "tm", "space", None),
-            P("dp", "tm", "space", None),
-            P("dp", "tm", "space", None),
-            P("dp", "tm", "space", None),
-            P("dp", "tm", "space", None),
-            P("dp", "tm"),
-        ),
+        mesh=split,
+        in_specs=(field,) * 8 + (P("dp", "tm"),),
+        out_specs=(field,) * 6 + (P("dp", "tm"),),
         check_vma=False,
     )

time: 235 us -> 202 us (0.86)
  waiting for transfers between devices: 56.3 us -> 29.9 us
  starting transfers between devices: 106 us -> 96.2 us
  local copies, waits for them, and re-layouts: 4.69 us -> 7.77 us
    all_to_all x4 -> x3, starting transfers between devices: 52.6 us -> 37.6 us  [the longest x1 19.5 us: shards(): lax.all_to_all(blocks, ('dp', 'z', 'y'), split_axis=0, concat_axis=0, til...]
    all_gather x1, waiting for transfers between devices: 11.3 us -> 0.01 us  [shards(): lax.all_gather(grad_out, 'tm', axis=1, tiled=True).reshape(4, LANES, 1152)]
    ppermute x3, waiting for transfers between devices: 6.59 us -> 0.01 us  [shards(): lax.ppermute(sends[shift], 'tm', RING[shift - 1])]
    ppermute x3, waiting for transfers between devices: 9.58 us -> 4.26 us  [shards(): lax.ppermute(backs[shift], 'tm', RING_BACK[shift - 1])]
    ppermute x7 -> x6, waiting for transfers between devices: 28.1 us -> 23.5 us  [the longest x3 17.5 us: gather_near(): got = lax.ppermute(block, axis, move)]
    ppermute x3, starting transfers between devices: 7.93 us -> 11.1 us  [shards(): lax.ppermute(backs[shift], 'tm', RING_BACK[shift - 1])]
    ppermute x7 -> x6, starting transfers between devices: 35 us -> 37.1 us  [the longest x3 12.4 us: gather_near(): got = lax.ppermute(block, axis, move)]
    pallas_call x6 -> x5, Pallas kernels: 13.5 us -> 13.2 us  [the longest x1 3.1 us: temporal_out(): pl.pallas_call(tout_kernel, out_shape=(jax.ShapeDtypeStruct((4, 288, LANE...]
  transfers between devices with their start and end apart: 18 -> 16, of which waited for: 11 -> 8; matrix products, arithmetic and copies ran while one was open for 1% -> 1% of each run, Pallas kernels for 20% -> 21%
where the time goes in v3:
time: 202 us; the launch traced here: 200 us
  starting transfers between devices  96.2 us (48%)
  Pallas kernels  50.7 us (25%)
  waiting for transfers between devices  29.9 us (15%)
  between operations  14.3 us (7%)
  local copies, waits for them, and re-layouts  7.77 us (4%)
    pallas_call x1, Pallas kernels, attend(): pl.pallas_call(functools.partial(attend_kernel, step=step), out_shape=jax...  23.4 us
    all_to_all x1, starting transfers between devices, shards(): lax.all_to_all(blocks, ('dp', 'z', 'y'), split_axis=0, concat_axis=0, til...  19.5 us
    ppermute x3, waiting for transfers between devices, gather_near(): got = lax.ppermute(block, axis, move)  17.5 us
    ppermute x3, starting transfers between devices, gather_near(): got = lax.ppermute(block, axis, move)  12.4 us
    ppermute x3, starting transfers between devices, shards(): lax.ppermute(backs[shift], 'tm', RING_BACK[shift - 1])  11.1 us
    ppermute x1, starting transfers between devices, shards(): got = lax.ppermute(own, 'dp', SWAP[1])  11.1 us
    all_to_all x1, starting transfers between devices, shards(): lax.all_to_all(packed, space, split_axis=0, concat_axis=0, tiled=True)  10.5 us
    ppermute x3, starting transfers between devices, shards(): lax.ppermute(sends[shift], 'tm', RING[shift - 1])  10.2 us
  transfers between devices with their start and end apart: 16, of which 8 were waited for; matrix products, arithmetic and copies ran while one was open for 1% of the time, Pallas kernels for 21%

profile of v3, /device:TPU:1, one launch (start us, length us, event | category | flops | bytes accessed | tf_op | source)
XLA Modules:
  0.0 200.1 jit_solution(13112001800282428329)
XLA Ops:
  7.2 1.7 reshape.23.w_ref
  8.8 2.6 %spatial_pack.1 = bf16[32,2,72,128]{3,2,1,0:T(8,128)(2,1)} custom-call(bf16[2,64,1152]{2,1,0:T(8,128)(2,1)} %bitcast.35, bf16[2,64,1152]{2,1,0:T(8,128)(2,1)} %bitcast.36, bf16[2,64,1152]{2,1,0:T(8,128)(2,1)} %bitcast.37, bf16[2,64,1152]{2,1,0:T(8,128)(2,1)} %bitcast.38), custom_call_target="tpu_custom_call" | custom-call | tf_op jit(solution)/shard_map/spatial_pack/pallas_call | solution.py:45
  11.5 10.5 %all-to-all-start = ((bf16[32,2,72,128]{3,2,1,0:T(8,128)(2,1)}), bf16[32,2,72,128]{3,2,1,0:T(8,128)(2,1)S(1)}, u32[]{:S(2)}, u32[]{:S(2)}) async-start(bf16[32,2,72,128]{3,2,1,0:T(8,128)(2,1)} %spatial_pack.1), calls=%async_computation | async-start | bytes 2359296 | tf_op jit(solution)/shard_map/all_to_all | solution.py:527
  21.9 0.0 all-gather.2.cloned.1.call-start
  22.0 0.7 all-gather.2.cloned.1.call-update
  22.7 0.7 pad_add_fusion.me_ref
  23.3 2.6 %temporal_pack.1 = (bf16[288,384]{1,0:T(8,128)(2,1)}, bf16[288,384]{1,0:T(8,128)(2,1)}, bf16[288,384]{1,0:T(8,128)(2,1)}, bf16[288,384]{1,0:T(8,128)(2,1)}, bf16[36,288]{1,0:T(8,128)(2,1)}) custom-call(s32[4]{0:T(128)} %pad_add_fusion.me_ref, bf16[2,64,1152]{2,1,0:T(8,128)(2,1)} %bitcast.40, bf16[2,64,1152]{2,1,0:T(8,128)(2,1)} %bitcast.41, ...), custom_call_target="tpu_custom_call" | custom-call | tf_op jit(solution)/shard_map/temporal_pack/pallas_call | solution.py:236
  26.0 2.8 %collective-permute-start = (bf16[288,384]{1,0:T(8,128)(2,1)}, bf16[288,384]{1,0:T(8,128)(2,1)S(1)}, u32[]{:S(2)}, u32[]{:S(2)}) collective-permute-start(bf16[288,384]{1,0:T(8,128)(2,1)} %get-tuple-element.47), channel_id=1, source_target_pairs={{0,32},{32,64},{64,96},{96,0},{1,33},{33,65},{65,97},{97,1},{2,34}... | collective-permute-start | bytes 663560 | tf_op jit(solution)/shard_map/ppermute | solution.py:532
  28.8 4.4 %collective-permute-start.1 = (bf16[288,384]{1,0:T(8,128)(2,1)}, bf16[288,384]{1,0:T(8,128)(2,1)S(1)}, u32[]{:S(2)}, u32[]{:S(2)}) collective-permute-start(bf16[288,384]{1,0:T(8,128)(2,1)} %get-tuple-element.48), channel_id=1, source_target_pairs={{0,64},{32,96},{64,0},{96,32},{1,65},{33,97},{65,1},{97,33},{2,66}... | collective-permute-start | bytes 663560 | tf_op jit(solution)/shard_map/ppermute | solution.py:532
  33.2 3.1 %collective-permute-start.2 = (bf16[288,384]{1,0:T(8,128)(2,1)}, bf16[288,384]{1,0:T(8,128)(2,1)S(1)}, u32[]{:S(2)}, u32[]{:S(2)}) collective-permute-start(bf16[288,384]{1,0:T(8,128)(2,1)} %get-tuple-element.49), channel_id=1, source_target_pairs={{0,96},{32,0},{64,32},{96,64},{1,97},{33,1},{65,33},{97,65},{2,98}... | collective-permute-start | bytes 663560 | tf_op jit(solution)/shard_map/ppermute | solution.py:532
  36.2 8.8 %collective-permute-start.3 = (bf16[36,288]{1,0:T(8,128)(2,1)}, bf16[36,288]{1,0:T(8,128)(2,1)S(1)}, u32[]{:S(2)}, u32[]{:S(2)}) collective-permute-start(bf16[36,288]{1,0:T(8,128)(2,1)} %get-tuple-element.50.own_ref), channel_id=1, source_target_pairs={{0,128},{128,0},{256,384},{384,256},{1,129},{129,1},{257,385},{385... | collective-permute-start | bytes 62216 | tf_op jit(solution)/shard_map/ppermute | solution.py:530
  45.1 1.7 collective-permute-done.3.got_ref
  46.7 0.0 collective-permute-done.in1
  46.7 0.0 collective-permute-done.1.in2
  46.8 0.0 copy-start.4
  46.8 0.0 collective-permute-done.2.in3
  46.8 0.0 copy-start.5
  46.8 0.6 copy-done.12
  47.4 0.1 copy-done.3
  47.4 0.1 copy-done.4
  47.5 0.1 copy-done.5
  47.6 3.1 %temporal_tout.1 = (bf16[4,288,128]{2,1,0:T(8,128)(2,1)}, bf16[2,36,288]{2,1,0:T(8,128)(2,1)}) custom-call(s32[4]{0:T(128)} %pad_add_fusion.me_ref, bf16[288,384]{1,0:T(8,128)(2,1)} %get-tuple-element.62.in0, bf16[288,384]{1,0:T(8,128)(2,1)} %copy-done.3, bf16[288,384]{1,0:T(8,128)(2,1)} %copy-done.4, bf16[288,384]{1,0:T(8,128)(2,1)} %copy-done.5, ...), custom_call_target="tpu_custom_call" | custom-call | tf_op jit(solution)/shard_map/temporal_tout/pallas_call | solution.py:304
  50.7 11.1 %collective-permute-start.4 = (bf16[2,36,288]{2,1,0:T(8,128)(2,1)}, bf16[2,36,288]{2,1,0:T(8,128)(2,1)S(1)}, u32[]{:S(2)}, u32[]{:S(2)}) collective-permute-start(bf16[2,36,288]{2,1,0:T(8,128)(2,1)} %get-tuple-element.52.own_ref), channel_id=1, source_target_pairs={{0,256},{128,384},{256,0},{384,128},{1,257},{129,385},{257,1},{385... | collective-permute-start | bytes 124424 | tf_op jit(solution)/shard_map/ppermute | solution.py:535
  61.8 2.8 %collective-permute-done.4.got_ref = bf16[2,36,288]{2,1,0:T(8,128)(2,1)S(1)} collective-permute-done((bf16[2,36,288]{2,1,0:T(8,128)(2,1)}, bf16[2,36,288]{2,1,0:T(8,128)(2,1)S(1)}, u32[]{:S(2)}, u32[]{:S(2)}) %collective-permute-start.4) | collective-permute-done | bytes 41504 | tf_op jit(solution)/shard_map/ppermute | solution.py:535
  64.6 0.6 copy-done.11
  65.2 3.2 %weight_partial.1 = (f32[144,1152]{1,0:T(8,128)}, bf16[144,1152]{1,0:T(8,128)(2,1)}, bf16[2,2,36,288]{3,2,1,0:T(8,128)(2,1)}) custom-call(s32[4]{0:T(128)} %pad_add_fusion.me_ref, bf16[4,288,128]{2,1,0:T(8,128)(2,1)} %get-tuple-element.51.tout_ref, bf16[4,128,1152]{2,1,0:T(8,128)(2,1)} %bitcast.33, bf16[2,36,288]{2,1,0:T(8,128)(2,1)} %get-tuple-element.52.own_ref, ...), custom_call_target="tpu_custom_call" | custom-call | tf_op jit(solution)/shard_map/weight_partial/pallas_call | solution.py:337
  68.4 4.8 %collective-permute-start.5 = (bf16[144,1152]{1,0:T(8,128)(2,1)}, bf16[144,1152]{1,0:T(8,128)(2,1)S(1)}, u32[]{:S(2)}, u32[]{:S(2)}) collective-permute-start(bf16[144,1152]{1,0:T(8,128)(2,1)} %get-tuple-element.54), channel_id=1, source_target_pairs={{0,1},{1,0},{2,3},{3,2},{4,5},{5,4},{6,7},{7,6},{8,9},{9,8},{10,11... | collective-permute-start | bytes 995336 | tf_op jit(solution)/shard_map/ppermute | solution.py:537
  73.3 1.4 collective-permute-done.5.got_ref
  74.7 0.7 copy-done.6
  75.4 2.4 %weight_split.1 = bf16[64,24,128]{2,1,0:T(8,128)(2,1)} custom-call(f32[144,1152]{1,0:T(8,128)} %get-tuple-element.53.keep_ref, bf16[144,1152]{1,0:T(8,128)(2,1)} %copy-done.6), custom_call_target="tpu_custom_call" | custom-call | tf_op jit(solution)/shard_map/weight_split/pallas_call | solution.py:372
  77.8 0.0 all-to-all-done.in_ref
  77.8 19.5 %all-to-all-start.1 = ((bf16[64,24,128]{2,1,0:T(8,128)(2,1)}), bf16[64,24,128]{2,1,0:T(8,128)(2,1)S(1)}, u32[]{:S(2)}, u32[]{:S(2)}) async-start(bf16[64,24,128]{2,1,0:T(8,128)(2,1)} %weight_split.1), calls=%async_computation.1 | async-start | bytes 786432 | tf_op jit(solution)/shard_map/all_to_all | solution.py:540
  97.3 23.4 %spatial_attention.1.spatial_ref = bf16[32,112,128]{2,1,0:T(8,128)(2,1)} custom-call(bf16[32,2,72,128]{3,2,1,0:T(8,128)(2,1)} %copy-done.2), custom_call_target="tpu_custom_call" | custom-call | flops 10737418240 | bytes 2200000 | tf_op jit(solution)/shard_map/spatial_attention/pallas_call | solution.py:146
  120.7 1.5 all-to-all-done.1.in_ref
  122.2 0.7 copy-done.1
  122.9 2.4 %weight_join.1 = bf16[32,136,128]{2,1,0:T(8,128)(2,1)} custom-call(bf16[32,112,128]{2,1,0:T(8,128)(2,1)} %spatial_attention.1.spatial_ref, bf16[64,24,128]{2,1,0:T(8,128)(2,1)} %copy-done.1), custom_call_target="tpu_custom_call" | custom-call | tf_op jit(solution)/shard_map/weight_join/pallas_call | solution.py:394
  125.3 7.7 %all-to-all-start.2 = ((bf16[32,136,128]{2,1,0:T(8,128)(2,1)}), bf16[32,136,128]{2,1,0:T(8,128)(2,1)S(1)}, u32[]{:S(2)}, u32[]{:S(2)}) async-start(bf16[32,136,128]{2,1,0:T(8,128)(2,1)} %weight_join.1), calls=%async_computation.2 | async-start | bytes 2228224 | tf_op jit(solution)/shard_map/all_to_all | solution.py:544
  133.0 3.3 %collective-permute-start.6 = (bf16[2,2,36,288]{3,2,1,0:T(8,128)(2,1)S(1)}, bf16[2,2,36,288]{3,2,1,0:T(8,128)(2,1)S(1)}, u32[]{:S(2)}, u32[]{:S(2)}) collective-permute-start(bf16[2,2,36,288]{3,2,1,0:T(8,128)(2,1)S(1)} %copy-done.10), channel_id=1, source_target_pairs={{0,2},{2,0},{4,6},{6,4},{1,3},{3,1},{5,7},{7,5},{8,10},{10,8},{12,... | collective-permute-start | bytes 248840 | tf_op jit(solution)/shard_map/ppermute | solution.py:503
  136.3 9.3 %collective-permute-done.6 = bf16[2,2,36,288]{3,2,1,0:T(8,128)(2,1)S(1)} collective-permute-done((bf16[2,2,36,288]{3,2,1,0:T(8,128)(2,1)S(1)}, bf16[2,2,36,288]{3,2,1,0:T(8,128)(2,1)S(1)}, u32[]{:S(2)}, u32[]{:S(2)}) %collective-permute-start.6) | collective-permute-done | bytes 82976 | tf_op jit(solution)/shard_map/ppermute | solution.py:503
  145.6 0.1 pad_maximum_fusion.1
  145.7 4.7 %collective-permute-start.7 = (bf16[2,2,2,36,288]{4,3,2,1,0:T(8,128)(2,1)S(1)}, bf16[2,2,2,36,288]{4,3,2,1,0:T(8,128)(2,1)S(1)}, u32[]{:S(2)}, u32[]{:S(2)}) collective-permute-start(bf16[2,2,2,36,288]{4,3,2,1,0:T(8,128)(2,1)S(1)} %pad_maximum_fusion.1), channel_id=1, source_target_pairs={{0,4},{2,6},{4,0},{6,2},{1,5},{3,7},{5,1},{7,3},{8,12},{10,14},{12... | collective-permute-start | bytes 497672 | tf_op jit(solution)/shard_map/ppermute | solution.py:503
  150.4 6.8 %collective-permute-done.7 = bf16[2,2,2,36,288]{4,3,2,1,0:T(8,128)(2,1)S(1)} collective-permute-done((bf16[2,2,2,36,288]{4,3,2,1,0:T(8,128)(2,1)S(1)}, bf16[2,2,2,36,288]{4,3,2,1,0:T(8,128)(2,1)S(1)}, u32[]{:S(2)}, u32[]{:S(2)}) %collective-permute-start.7) | collective-permute-done | bytes 165920 | tf_op jit(solution)/shard_map/ppermute | solution.py:503
  157.1 0.1 select_bitcast_fusion.3
  157.2 0.1 pad_maximum_fusion
  157.3 4.4 %collective-permute-start.8 = (bf16[2,2,2,2,36,288]{5,4,3,2,1,0:T(8,128)(2,1)S(1)}, bf16[2,2,2,2,36,288]{5,4,3,2,1,0:T(8,128)(2,1)S(1)}, u32[]{:S(2)}, u32[]{:S(2)}) collective-permute-start(bf16[2,2,2,2,36,288]{5,4,3,2,1,0:T(8,128)(2,1)S(1)} %pad_maximum_fusion), channel_id=1, source_target_pairs={{0,1},{1,0},{2,3},{3,2},{4,5},{5,4},{6,7},{7,6},{8,9},{9,8},{10,11... | collective-permute-start | bytes 995336 | tf_op jit(solution)/shard_map/ppermute | solution.py:503
  161.8 1.5 collective-permute-done.8
  163.2 0.2 select_bitcast_fusion.1
  163.4 0.2 maximum_bitcast_fusion
  163.6 0.1 copy.19
  163.7 1.3 reshape.25.w_ref
  165.0 5.8 %temporal_back.1 = (bf16[288,384]{1,0:T(8,128)(2,1)}, bf16[288,384]{1,0:T(8,128)(2,1)}, bf16[288,384]{1,0:T(8,128)(2,1)}, bf16[288,384]{1,0:T(8,128)(2,1)}) custom-call(s32[4]{0:T(128)} %pad_add_fusion.me_ref, bf16[288,384]{1,0:T(8,128)(2,1)} %get-tuple-element.62.in0, bf16[288,384]{1,0:T(8,128)(2,1)} %copy-done.3, bf16[288,384]{1,0:T(8,128)(2,1)} %copy-done.4, ...), custom_call_target="tpu_custom_call" | custom-call | tf_op jit(solution)/shard_map/temporal_back/pallas_call | solution.py:455
  170.8 4.6 %collective-permute-start.10 = (bf16[288,384]{1,0:T(8,128)(2,1)}, bf16[288,384]{1,0:T(8,128)(2,1)S(1)}, u32[]{:S(2)}, u32[]{:S(2)}) collective-permute-start(bf16[288,384]{1,0:T(8,128)(2,1)} %get-tuple-element.69), channel_id=1, source_target_pairs={{0,64},{32,96},{64,0},{96,32},{1,65},{33,97},{65,1},{97,33},{2,66}... | collective-permute-start | bytes 663560 | tf_op jit(solution)/shard_map/ppermute | solution.py:548
  175.5 2.2 %collective-permute-start.11 = (bf16[288,384]{1,0:T(8,128)(2,1)}, bf16[288,384]{1,0:T(8,128)(2,1)S(1)}, u32[]{:S(2)}, u32[]{:S(2)}) collective-permute-start(bf16[288,384]{1,0:T(8,128)(2,1)} %get-tuple-element.70), channel_id=1, source_target_pairs={{0,32},{32,64},{64,96},{96,0},{1,33},{33,65},{65,97},{97,1},{2,34}... | collective-permute-start | bytes 663560 | tf_op jit(solution)/shard_map/ppermute | solution.py:548
  177.7 4.3 %collective-permute-start.9 = (bf16[288,384]{1,0:T(8,128)(2,1)}, bf16[288,384]{1,0:T(8,128)(2,1)S(1)}, u32[]{:S(2)}, u32[]{:S(2)}) collective-permute-start(bf16[288,384]{1,0:T(8,128)(2,1)} %get-tuple-element.68), channel_id=1, source_target_pairs={{0,96},{32,0},{64,32},{96,64},{1,97},{33,1},{65,33},{97,65},{2,98}... | collective-permute-start | bytes 663560 | tf_op jit(solution)/shard_map/ppermute | solution.py:548
  182.0 0.0 collective-permute-done.10.in2
  182.0 0.0 copy-start.7
  182.0 4.3 %collective-permute-done.11.in3 = bf16[288,384]{1,0:T(8,128)(2,1)S(1)} collective-permute-done((bf16[288,384]{1,0:T(8,128)(2,1)}, bf16[288,384]{1,0:T(8,128)(2,1)S(1)}, u32[]{:S(2)}, u32[]{:S(2)}) %collective-permute-start.11) | collective-permute-done | bytes 221216 | tf_op jit(solution)/shard_map/ppermute | solution.py:548
  186.3 0.0 collective-permute-done.9.in1
  186.3 0.7 copy-done.8
  186.9 0.1 copy-done.9
  187.0 2.5 %temporal_unpack.1 = (bf16[2,64,1152]{2,1,0:T(8,128)(2,1)}, bf16[2,64,1152]{2,1,0:T(8,128)(2,1)}, bf16[2,64,1152]{2,1,0:T(8,128)(2,1)}) custom-call(s32[4]{0:T(128)} %pad_add_fusion.me_ref, bf16[288,384]{1,0:T(8,128)(2,1)} %get-tuple-element.67.in0, bf16[288,384]{1,0:T(8,128)(2,1)} %copy-done.9, bf16[288,384]{1,0:T(8,128)(2,1)} %copy-done.7, ...), custom_call_target="tpu_custom_call" | custom-call | tf_op jit(solution)/shard_map/temporal_unpack/pallas_call | solution.py:483
  189.5 0.0 all-to-all-done.2.in_ref
  189.5 1.0 copy-done
  190.5 2.7 %spatial_unpack.1 = (bf16[2,64,1152]{2,1,0:T(8,128)(2,1)}, bf16[2,64,1152]{2,1,0:T(8,128)(2,1)}, bf16[2,64,1152]{2,1,0:T(8,128)(2,1)}, f32[288,288]{1,0:T(8,128)}) custom-call(bf16[32,136,128]{2,1,0:T(8,128)(2,1)} %copy-done), custom_call_target="tpu_custom_call" | custom-call | tf_op jit(solution)/shard_map/spatial_unpack/pallas_call | solution.py:203
  (15 shorter events, 0.1 us)
Async XLA Ops:
  11.5 66.3 %all-to-all-start = ((bf16[32,2,72,128]{3,2,1,0:T(8,128)(2,1)}), bf16[32,2,72,128]{3,2,1,0:T(8,128)(2,1)S(1)}, u32[]{:S(2)}, u32[]{:S(2)}) async-start(bf16[32,2,72,128]{3,2,1,0:T(8,128)(2,1)} %spatial_pack.1), calls=%async_computation | async-start | bytes 2359296 | tf_op jit(solution)/shard_map/all_to_all | solution.py:527
  21.9 42.7 %all-gather.2.cloned.1.call-start = ((), (), s32[]{:S(2)}) async-start(), calls=%async_computation.3 | async-start | bytes 1474560 | tf_op jit(solution)/shard_map/all_gather | solution.py:522
  26.0 20.8 %collective-permute-start = (bf16[288,384]{1,0:T(8,128)(2,1)}, bf16[288,384]{1,0:T(8,128)(2,1)S(1)}, u32[]{:S(2)}, u32[]{:S(2)}) collective-permute-start(bf16[288,384]{1,0:T(8,128)(2,1)} %get-tuple-element.47), channel_id=1, source_target_pairs={{0,32},{32,64},{64,96},{96,0},{1,33},{33,65},{65,97},{97,1},{2,34}... | collective-permute-start | bytes 663560 | tf_op jit(solution)/shard_map/ppermute | solution.py:532
  28.8 18.0 %collective-permute-start.1 = (bf16[288,384]{1,0:T(8,128)(2,1)}, bf16[288,384]{1,0:T(8,128)(2,1)S(1)}, u32[]{:S(2)}, u32[]{:S(2)}) collective-permute-start(bf16[288,384]{1,0:T(8,128)(2,1)} %get-tuple-element.48), channel_id=1, source_target_pairs={{0,64},{32,96},{64,0},{96,32},{1,65},{33,97},{65,1},{97,33},{2,66}... | collective-permute-start | bytes 663560 | tf_op jit(solution)/shard_map/ppermute | solution.py:532
  33.2 13.6 %collective-permute-start.2 = (bf16[288,384]{1,0:T(8,128)(2,1)}, bf16[288,384]{1,0:T(8,128)(2,1)S(1)}, u32[]{:S(2)}, u32[]{:S(2)}) collective-permute-start(bf16[288,384]{1,0:T(8,128)(2,1)} %get-tuple-element.49), channel_id=1, source_target_pairs={{0,96},{32,0},{64,32},{96,64},{1,97},{33,1},{65,33},{97,65},{2,98}... | collective-permute-start | bytes 663560 | tf_op jit(solution)/shard_map/ppermute | solution.py:532
  36.2 10.5 %collective-permute-start.3 = (bf16[36,288]{1,0:T(8,128)(2,1)}, bf16[36,288]{1,0:T(8,128)(2,1)S(1)}, u32[]{:S(2)}, u32[]{:S(2)}) collective-permute-start(bf16[36,288]{1,0:T(8,128)(2,1)} %get-tuple-element.50.own_ref), channel_id=1, source_target_pairs={{0,128},{128,0},{256,384},{384,256},{1,129},{129,1},{257,385},{385... | collective-permute-start | bytes 62216 | tf_op jit(solution)/shard_map/ppermute | solution.py:530
  46.7 0.6 copy-start.12
  46.7 0.7 copy-start.3
  46.8 0.8 copy-start.4
  46.8 0.8 copy-start.5
  50.7 13.9 %collective-permute-start.4 = (bf16[2,36,288]{2,1,0:T(8,128)(2,1)}, bf16[2,36,288]{2,1,0:T(8,128)(2,1)S(1)}, u32[]{:S(2)}, u32[]{:S(2)}) collective-permute-start(bf16[2,36,288]{2,1,0:T(8,128)(2,1)} %get-tuple-element.52.own_ref), channel_id=1, source_target_pairs={{0,256},{128,384},{256,0},{384,128},{1,257},{129,385},{257,1},{385... | collective-permute-start | bytes 124424 | tf_op jit(solution)/shard_map/ppermute | solution.py:535
  64.6 0.6 copy-start.11
  68.4 6.3 %collective-permute-start.5 = (bf16[144,1152]{1,0:T(8,128)(2,1)}, bf16[144,1152]{1,0:T(8,128)(2,1)S(1)}, u32[]{:S(2)}, u32[]{:S(2)}) collective-permute-start(bf16[144,1152]{1,0:T(8,128)(2,1)} %get-tuple-element.54), channel_id=1, source_target_pairs={{0,1},{1,0},{2,3},{3,2},{4,5},{5,4},{6,7},{7,6},{8,9},{9,8},{10,11... | collective-permute-start | bytes 995336 | tf_op jit(solution)/shard_map/ppermute | solution.py:537
  74.7 0.7 copy-start.6
  77.8 19.5 %copy-start.2 = (bf16[32,2,72,128]{3,2,1,0:T(8,128)(2,1)}, bf16[32,2,72,128]{3,2,1,0:T(8,128)(2,1)S(1)}, u32[]{:S(2)}) copy-start(bf16[32,2,72,128]{3,2,1,0:T(8,128)(2,1)S(1)} %all-to-all-done.in_ref) | copy-start | bytes 3538948
  77.8 44.4 %all-to-all-start.1 = ((bf16[64,24,128]{2,1,0:T(8,128)(2,1)}), bf16[64,24,128]{2,1,0:T(8,128)(2,1)S(1)}, u32[]{:S(2)}, u32[]{:S(2)}) async-start(bf16[64,24,128]{2,1,0:T(8,128)(2,1)} %weight_split.1), calls=%async_computation.1 | async-start | bytes 786432 | tf_op jit(solution)/shard_map/all_to_all | solution.py:540
  122.2 0.7 copy-start.1
  125.3 7.7 %copy-start.10 = (bf16[2,2,36,288]{3,2,1,0:T(8,128)(2,1)S(1)}, bf16[2,2,36,288]{3,2,1,0:T(8,128)(2,1)}, u32[]{:S(2)}) copy-start(bf16[2,2,36,288]{3,2,1,0:T(8,128)(2,1)} %get-tuple-element.66) | copy-start | bytes 248836
  125.3 64.2 %all-to-all-start.2 = ((bf16[32,136,128]{2,1,0:T(8,128)(2,1)}), bf16[32,136,128]{2,1,0:T(8,128)(2,1)S(1)}, u32[]{:S(2)}, u32[]{:S(2)}) async-start(bf16[32,136,128]{2,1,0:T(8,128)(2,1)} %weight_join.1), calls=%async_computation.2 | async-start | bytes 2228224 | tf_op jit(solution)/shard_map/all_to_all | solution.py:544
  133.0 12.6 %collective-permute-start.6 = (bf16[2,2,36,288]{3,2,1,0:T(8,128)(2,1)S(1)}, bf16[2,2,36,288]{3,2,1,0:T(8,128)(2,1)S(1)}, u32[]{:S(2)}, u32[]{:S(2)}) collective-permute-start(bf16[2,2,36,288]{3,2,1,0:T(8,128)(2,1)S(1)} %copy-done.10), channel_id=1, source_target_pairs={{0,2},{2,0},{4,6},{6,4},{1,3},{3,1},{5,7},{7,5},{8,10},{10,8},{12,... | collective-permute-start | bytes 248840 | tf_op jit(solution)/shard_map/ppermute | solution.py:503
  145.7 11.4 %collective-permute-start.7 = (bf16[2,2,2,36,288]{4,3,2,1,0:T(8,128)(2,1)S(1)}, bf16[2,2,2,36,288]{4,3,2,1,0:T(8,128)(2,1)S(1)}, u32[]{:S(2)}, u32[]{:S(2)}) collective-permute-start(bf16[2,2,2,36,288]{4,3,2,1,0:T(8,128)(2,1)S(1)} %pad_maximum_fusion.1), channel_id=1, source_target_pairs={{0,4},{2,6},{4,0},{6,2},{1,5},{3,7},{5,1},{7,3},{8,12},{10,14},{12... | collective-permute-start | bytes 497672 | tf_op jit(solution)/shard_map/ppermute | solution.py:503
  157.3 5.9 %collective-permute-start.8 = (bf16[2,2,2,2,36,288]{5,4,3,2,1,0:T(8,128)(2,1)S(1)}, bf16[2,2,2,2,36,288]{5,4,3,2,1,0:T(8,128)(2,1)S(1)}, u32[]{:S(2)}, u32[]{:S(2)}) collective-permute-start(bf16[2,2,2,2,36,288]{5,4,3,2,1,0:T(8,128)(2,1)S(1)} %pad_maximum_fusion), channel_id=1, source_target_pairs={{0,1},{1,0},{2,3},{3,2},{4,5},{5,4},{6,7},{7,6},{8,9},{9,8},{10,11... | collective-permute-start | bytes 995336 | tf_op jit(solution)/shard_map/ppermute | solution.py:503
  170.8 11.1 %collective-permute-start.10 = (bf16[288,384]{1,0:T(8,128)(2,1)}, bf16[288,384]{1,0:T(8,128)(2,1)S(1)}, u32[]{:S(2)}, u32[]{:S(2)}) collective-permute-start(bf16[288,384]{1,0:T(8,128)(2,1)} %get-tuple-element.69), channel_id=1, source_target_pairs={{0,64},{32,96},{64,0},{96,32},{1,65},{33,97},{65,1},{97,33},{2,66}... | collective-permute-start | bytes 663560 | tf_op jit(solution)/shard_map/ppermute | solution.py:548
  175.5 10.8 %collective-permute-start.11 = (bf16[288,384]{1,0:T(8,128)(2,1)}, bf16[288,384]{1,0:T(8,128)(2,1)S(1)}, u32[]{:S(2)}, u32[]{:S(2)}) collective-permute-start(bf16[288,384]{1,0:T(8,128)(2,1)} %get-tuple-element.70), channel_id=1, source_target_pairs={{0,32},{32,64},{64,96},{96,0},{1,33},{33,65},{65,97},{97,1},{2,34}... | collective-permute-start | bytes 663560 | tf_op jit(solution)/shard_map/ppermute | solution.py:548
  177.7 8.6 %collective-permute-start.9 = (bf16[288,384]{1,0:T(8,128)(2,1)}, bf16[288,384]{1,0:T(8,128)(2,1)S(1)}, u32[]{:S(2)}, u32[]{:S(2)}) collective-permute-start(bf16[288,384]{1,0:T(8,128)(2,1)} %get-tuple-element.68), channel_id=1, source_target_pairs={{0,96},{32,0},{64,32},{96,64},{1,97},{33,1},{65,33},{97,65},{2,98}... | collective-permute-start | bytes 663560 | tf_op jit(solution)/shard_map/ppermute | solution.py:548
  182.0 4.3 %copy-start.7 = (bf16[288,384]{1,0:T(8,128)(2,1)}, bf16[288,384]{1,0:T(8,128)(2,1)S(1)}, u32[]{:S(2)}) copy-start(bf16[288,384]{1,0:T(8,128)(2,1)S(1)} %collective-permute-done.10.in2) | copy-start | bytes 663556
  186.3 0.7 copy-start.8
  186.3 0.8 copy-start.9
  189.5 1.0 copy-start
Sparse Core Ops, SparseCore 0:
  24.9 32.3 all-gather.1

commit v4 on v3

--- a/solution.py
+++ b/solution.py
@@ -187,14 +187,10 @@
     dv_ref[0] = both[:HALF]
     dv_ref[1] = both[HALF:]
     for s in range(2 * HEADS):
-        block = in_ref[s, HDIM + FOLD :].astype(F32)
-        start = 144 * (s % 2) + 8 * (s // 2)
-        for tile in range(3):
-            at = slice(tile * LANES, (tile + 1) * LANES)
-            full[start : start + 8, at] = block[tile * 8 : tile * 8 + 8]
-        start = 144 * (s % 2) + 128 + s // 2
-        for r in range(3):
-            full[start : start + 1, 96 * r : 96 * r + 96] = block[16 + r : 17 + r, 32:]
+        half = 144 * (s % 2)
+        unfold(
+            in_ref[s].astype(F32)[HDIM + FOLD :], full, half + 8 * (s // 2), half + 128 + s // 2
+        )
     dw_ref[...] = full[...].T[:288]
 
 
@@ -215,8 +211,15 @@
     return pltpu.roll(block, HALF, 1)
 
 
-def send_pack_kernel(me_ref, q_ref, k_ref, v_ref, w_ref, out0, out1, out2, out3, slice_ref, held):
-    slice_ref[...] = w_ref[me_ref[1]]
+def fold_tail(rest, r):
+    return jnp.concatenate(
+        [jnp.zeros((rest.shape[0], 32), F32), rest[:, 96 * r : 96 * r + 96]], axis=1
+    )
+
+
+def send_pack_kernel(
+    me_ref, q_ref, k_ref, v_ref, w_ref, out0, out1, out2, out3, piece_ref, held, halves
+):
     for part, ref in enumerate((q_ref, k_ref, v_ref)):
         rows = jnp.concatenate([ref[0], ref[1]], axis=0).astype(F32)
         columns = rows.T.astype(BF16)
@@ -229,16 +232,36 @@
     for shift, out in enumerate((out0, out1, out2, out3)):
         out[...] = held[lax.rem(me + shift, 4)]
 
+    halves[...] = jnp.zeros_like(halves)
+    w = w_ref[...].astype(F32)
+    halves[0, :, :288] = w[:144]
+    halves[1, :, :288] = w[144:]
+    core, place = me_ref[2], me_ref[1]
+    block = halves[core, pl.ds(pl.multiple_of(8 * place, 8), 8)]
+    rest = halves[core, 128:144]
+    here = lax.broadcasted_iota(jnp.int32, rest.shape, 0) == place
+    rest = jnp.sum(jnp.where(here, rest, 0.0), axis=0, keepdims=True)
+    row = lax.broadcasted_iota(jnp.int32, (8, LANES), 0)
+    last = block[:, 2 * LANES :]
+    for r in range(3):
+        last = last + jnp.where(row == r, fold_tail(rest, r), 0.0)
+    piece_ref[...] = jnp.concatenate(
+        [block[:, :LANES], block[:, LANES : 2 * LANES], last], axis=0
+    ).astype(BF16)
+
 
 def send_pack(me, q, k, v, w):
     shape = jax.ShapeDtypeStruct((288, 3 * LANES), BF16)
-    part = jax.ShapeDtypeStruct((36, 288), BF16)
+    piece = jax.ShapeDtypeStruct((24, LANES), BF16)
     return pl.pallas_call(
         send_pack_kernel,
-        out_shape=(shape,) * 4 + (part,),
+        out_shape=(shape,) * 4 + (piece,),
         in_specs=[pl.BlockSpec(memory_space=pltpu.SMEM)] + vmem_specs(4),
         out_specs=tuple(vmem_specs(5)),
-        scratch_shapes=[pltpu.VMEM((4, 288, 3 * LANES), BF16)],
+        scratch_shapes=[
+            pltpu.VMEM((4, 288, 3 * LANES), BF16),
+            pltpu.VMEM((2, 144, 3 * LANES), F32),
+        ],
         compiler_params=pltpu.CompilerParams(vmem_limit_bytes=LIMIT),
         name="temporal_pack",
     )(me, q, k, v, w)
@@ -272,13 +295,7 @@
     return out
 
 
-def pair_up(bit, own_ref, got_ref, out_ref):
-    out_ref[bit] = own_ref[...]
-    out_ref[1 - bit] = got_ref[...]
-
-
-def tout_kernel(me_ref, in0, in1, in2, in3, own_ref, got_ref, out_ref, w_ref, wide, total):
-    pair_up(lax.rem(me_ref[2], 2), own_ref, got_ref, w_ref)
+def tout_kernel(me_ref, in0, in1, in2, in3, out_ref, wide, total):
     for shift, ref in enumerate((in0, in1, in2, in3)):
         wide[shift] = ref[...].astype(F32)
 
@@ -300,59 +317,53 @@
         out_ref[lax.rem(me + 4 - shift, 4)] = total[shift].astype(BF16)
 
 
-def temporal_out(me, pieces, own, got):
+def temporal_out(me, pieces):
     return pl.pallas_call(
         tout_kernel,
-        out_shape=(
-            jax.ShapeDtypeStruct((4, 288, LANES), BF16),
-            jax.ShapeDtypeStruct((2, 36, 288), BF16),
-        ),
-        in_specs=[pl.BlockSpec(memory_space=pltpu.SMEM)] + vmem_specs(6),
-        out_specs=tuple(vmem_specs(2)),
+        out_shape=jax.ShapeDtypeStruct((4, 288, LANES), BF16),
+        in_specs=[pl.BlockSpec(memory_space=pltpu.SMEM)] + vmem_specs(4),
+        out_specs=pl.BlockSpec(memory_space=pltpu.VMEM),
         scratch_shapes=[
             pltpu.VMEM((4, 288, 3 * LANES), F32),
             pltpu.VMEM((4, 288, LANES), F32),
         ],
         compiler_params=pltpu.CompilerParams(vmem_limit_bytes=LIMIT),
         name="temporal_tout",
-    )(me, *pieces, own, got)
-
-
-def partial_kernel(
-    me_ref, tout_ref, grad_ref, own_ref, got_ref, keep_ref, send_ref, w_ref, full, *, scale
-):
-    pair_up(me_ref[2] // 2, own_ref, got_ref, w_ref)
+    )(me, *pieces)
+
+
+def partial_kernel(me_ref, tout_ref, grad_ref, keep_ref, send_ref, full, *, scale):
     total = jnp.dot(tout_ref[0], grad_ref[0], preferred_element_type=F32)
     for a in range(1, 4):
         total = total + jnp.dot(tout_ref[a], grad_ref[a], preferred_element_type=F32)
     total = total * scale
     full[0] = total[:144]
     full[1] = total[144:]
-    core = me_ref[3]
+    core = me_ref[2]
     keep_ref[...] = full[core]
     send_ref[...] = full[1 - core].astype(BF16)
 
 
-def weight_partial(me, tout, grads, own, got, scale):
+def weight_partial(me, tout, grads, scale):
     return pl.pallas_call(
         functools.partial(partial_kernel, scale=scale),
         out_shape=(
             jax.ShapeDtypeStruct((144, 1152), F32),
             jax.ShapeDtypeStruct((144, 1152), BF16),
-            jax.ShapeDtypeStruct((2, 2, 36, 288), BF16),
         ),
-        in_specs=[pl.BlockSpec(memory_space=pltpu.SMEM)] + vmem_specs(4),
-        out_specs=tuple(vmem_specs(3)),
+        in_specs=[pl.BlockSpec(memory_space=pltpu.SMEM)] + vmem_specs(2),
+        out_specs=tuple(vmem_specs(2)),
         scratch_shapes=[pltpu.VMEM((2, 144, 1152), F32)],
         compiler_params=pltpu.CompilerParams(vmem_limit_bytes=LIMIT),
         name="weight_partial",
-    )(me, tout, grads, own, got)
-
-
-def weight_split_kernel(keep_ref, got_ref, out_ref, full, part):
+    )(me, tout, grads)
+
+
+def weight_split_kernel(keep_ref, got_ref, piece_ref, out_ref, full, part):
     full[...] = keep_ref[...] + got_ref[...].astype(F32)
     part[...] = jnp.zeros_like(part)
     row = lax.broadcasted_iota(jnp.int32, (16, 8, LANES), 1)
+    copies = jnp.broadcast_to(piece_ref[...].astype(F32)[None], (16, 24, LANES))
     for d in range(4):
         part[:, :288] = full[:, d * 288 : (d + 1) * 288]
         tiles = [
@@ -361,54 +372,73 @@
         ]
         rest = part[128:144, :]
         for r in range(3):
-            moved = jnp.concatenate(
-                [jnp.zeros((16, 32), F32), rest[:, 96 * r : 96 * r + 96]], axis=1
-            )
-            tiles[2] = tiles[2] + jnp.where(row == r, moved[:, None, :], 0.0)
-        out_ref[d * 16 : (d + 1) * 16] = jnp.concatenate(tiles, axis=1).astype(BF16)
-
-
-def weight_split(keep, got):
+            tiles[2] = tiles[2] + jnp.where(row == r, fold_tail(rest, r)[:, None, :], 0.0)
+        out_ref[d * 16 : (d + 1) * 16] = jnp.concatenate(tiles + [copies], axis=1).astype(BF16)
+
+
+def weight_split(keep, got, piece):
     return pl.pallas_call(
         weight_split_kernel,
-        out_shape=jax.ShapeDtypeStruct((64, 24, LANES), BF16),
-        in_specs=vmem_specs(2),
+        out_shape=jax.ShapeDtypeStruct((64, 48, LANES), BF16),
+        in_specs=vmem_specs(3),
         out_specs=pl.BlockSpec(memory_space=pltpu.VMEM),
         scratch_shapes=[pltpu.VMEM((144, 1152), F32), pltpu.VMEM((144, 3 * LANES), F32)],
         compiler_params=pltpu.CompilerParams(vmem_limit_bytes=LIMIT),
         name="weight_split",
-    )(keep, got)
-
-
-def weight_join_kernel(spatial_ref, in_ref, out_ref):
-    total = in_ref[0].astype(F32)
-    for s in range(1, 64):
-        total = total + in_ref[s].astype(F32)
+    )(keep, got, piece)
+
+
+def unfold(block, full, start, last):
+    for tile in range(3):
+        at = slice(tile * LANES, (tile + 1) * LANES)
+        full[start : start + 8, at] = block[tile * 8 : tile * 8 + 8]
+    for r in range(3):
+        full[last : last + 1, 96 * r : 96 * r + 96] = block[16 + r : 17 + r, 32:]
+
+
+def weight_join_kernel(spatial_ref, in_ref, out_ref, w_ref, full):
+    total = None
+    for s in range(64):
+        block = in_ref[s].astype(F32)
+        total = block[:24] if total is None else total + block[:24]
+        d, j = s // 16, s % 16
+        unfold(block[24:], full, d * 144 + 8 * j, d * 144 + 128 + j)
     copy = total.astype(BF16)
     for s in range(32):
         out_ref[s, : HDIM + FOLD] = spatial_ref[s]
         out_ref[s, HDIM + FOLD :] = copy
+    for d in range(4):
+        w_ref[d] = full[d * 144 : (d + 1) * 144, :288].astype(BF16)
 
 
 def weight_join(spatial, received):
     return pl.pallas_call(
         weight_join_kernel,
-        out_shape=jax.ShapeDtypeStruct((32, HDIM + FOLD + 24, LANES), BF16),
+        out_shape=(
+            jax.ShapeDtypeStruct((32, HDIM + FOLD + 24, LANES), BF16),
+            jax.ShapeDtypeStruct((4, 144, 288), BF16),
+        ),
         in_specs=vmem_specs(2),
-        out_specs=pl.BlockSpec(memory_space=pltpu.VMEM),
+        out_specs=tuple(vmem_specs(2)),
+        scratch_shapes=[pltpu.VMEM((576, 3 * LANES), F32)],
         compiler_params=pltpu.CompilerParams(vmem_limit_bytes=LIMIT),
         name="weight_join",
     )(spatial, received)
 
 
 def temporal_kernel(
-    me_ref, in0, in1, in2, in3, grad_ref, w_ref, out0, out1, out2, out3, wide, back
+    me_ref, in0, in1, in2, in3, grad_ref, own_ref, other_ref,
+    out0, out1, out2, out3, wide, back, halves,
 ):
-    me = me_ref[0]
+    me, core = me_ref[0], me_ref[2]
+    for d in range(4):
+        halves[2 * d + core] = own_ref[d]
+        halves[2 * d + 1 - core] = other_ref[d]
+    w = halves[...].reshape(1152, 288)
     for shift, ref in enumerate((in0, in1, in2, in3)):
         wide[shift, :, : 3 * LANES] = ref[...].astype(F32)
         grads = grad_ref[lax.rem(me + 4 - shift, 4)]
-        tgrad = rounded(jnp.dot(grads, w_ref[...], preferred_element_type=F32))
+        tgrad = rounded(jnp.dot(grads, w, preferred_element_type=F32))
         wide[shift, :, 3 * LANES :] = tgrad.T
     scale = 1.0 / math.sqrt(HDIM)
 
@@ -450,20 +480,21 @@
         out[...] = back[shift].astype(BF16)
 
 
-def temporal_back(me, pieces, grads, w):
+def temporal_back(me, pieces, grads, own, other):
     shape = jax.ShapeDtypeStruct((288, 3 * LANES), BF16)
     return pl.pallas_call(
         temporal_kernel,
         out_shape=(shape,) * 4,
-        in_specs=[pl.BlockSpec(memory_space=pltpu.SMEM)] + vmem_specs(6),
+        in_specs=[pl.BlockSpec(memory_space=pltpu.SMEM)] + vmem_specs(7),
         out_specs=tuple(vmem_specs(4)),
         scratch_shapes=[
             pltpu.VMEM((4, 288, 4 * LANES), F32),
             pltpu.VMEM((4, 288, 3 * LANES), F32),
+            pltpu.VMEM((8, 144, 288), BF16),
         ],
         compiler_params=pltpu.CompilerParams(vmem_limit_bytes=LIMIT),
         name="temporal_back",
-    )(me, *pieces, grads, w)
+    )(me, *pieces, grads, own, other)
 
 
 def receive_kernel(me_ref, in0, in1, in2, in3, dq_ref, dk_ref, dv_ref, held):
@@ -491,18 +522,9 @@
     )(me, *pieces)
 
 
-SWAP = [[(i, i ^ s) for i in range(4)] for s in (1, 2)]
 SWAP_CORE = [(0, 1), (1, 0)]
 RING = [[(i, (i + s) % 4) for i in range(4)] for s in (1, 2, 3)]
 RING_BACK = [[(i, (i - s) % 4) for i in range(4)] for s in (1, 2, 3)]
-
-
-def gather_near(block):
-    y, c = lax.axis_index("y"), lax.axis_index("c")
-    for bit, move, axis in ((lax.rem(y, 2), SWAP[0], "y"), (y // 2, SWAP[1], "y"), (c, SWAP_CORE, "c")):
-        got = lax.ppermute(block, axis, move)
-        block = jnp.stack([jnp.where(bit == 0, block, got), jnp.where(bit == 0, got, block)])
-    return block.transpose(3, 4, 0, 1, 2, 5, 6).reshape(1152, 288)
 
 
 def shards(
@@ -516,34 +538,31 @@
     grad_out,
     w_tout,
 ):
-    y, c = lax.axis_index("y"), lax.axis_index("c")
-    me = jnp.stack([lax.axis_index("tm"), 4 * c + y, lax.axis_index("dp"), c])
+    me = jnp.stack(
+        [lax.axis_index("tm"), 4 * lax.axis_index("z") + lax.axis_index("y"), lax.axis_index("c")]
+    )
     space = ("z", "y", "c")
     grads = lax.all_gather(grad_out, "tm", axis=1, tiled=True).reshape(4, LANES, 1152)
     packed = pack(q_spatial[0], k_spatial[0], v_spatial[0], grad_spatial[0])
-    packed, q, k, v, w = lax.optimization_barrier(
-        (packed, q_temporal[0], k_temporal[0], v_temporal[0], w_tout.reshape(8, 36, 288))
+    packed, q, k, v = lax.optimization_barrier(
+        (packed, q_temporal[0], k_temporal[0], v_temporal[0])
     )
     received = lax.all_to_all(packed, space, split_axis=0, concat_axis=0, tiled=True)
 
-    *sends, own = send_pack(me, q, k, v, w)
-    got = lax.ppermute(own, "dp", SWAP[0])
+    *sends, piece = send_pack(me, q, k, v, w_tout)
     pieces = (sends[0],) + tuple(
         lax.ppermute(sends[shift], "tm", RING[shift - 1]) for shift in (1, 2, 3)
     )
-    tout, own = temporal_out(me, pieces, own, got)
-    got = lax.ppermute(own, "dp", SWAP[1])
-    keep, send, weight = weight_partial(me, tout, grads, own, got, 1.0 / math.sqrt(65536))
-    blocks = weight_split(keep, lax.ppermute(send, "c", SWAP_CORE))
+    tout = temporal_out(me, pieces)
+    keep, send = weight_partial(me, tout, grads, 1.0 / math.sqrt(65536))
+    blocks = weight_split(keep, lax.ppermute(send, "c", SWAP_CORE), piece)
 
     received, blocks = lax.optimization_barrier((received, blocks))
     blocks = lax.all_to_all(blocks, ("dp", "z", "y"), split_axis=0, concat_axis=0, tiled=True)
-    results = attend(received)
-    results, weight, *pieces = lax.optimization_barrier((results, weight) + pieces)
-    results = weight_join(results, blocks)
+    results, own = weight_join(attend(received), blocks)
     returned = lax.all_to_all(results, space, split_axis=0, concat_axis=0, tiled=True)
 
-    backs = temporal_back(me, pieces, grads, gather_near(weight))
+    backs = temporal_back(me, pieces, grads, own, lax.ppermute(own, "c", SWAP_CORE))
     homes = (backs[0],) + tuple(
         lax.ppermute(backs[shift], "tm", RING_BACK[shift - 1]) for shift in (1, 2, 3)
     )

time: 202 us -> 179 us (0.89)
  starting transfers between devices: 96.2 us -> 59 us
  waiting for transfers between devices: 29.9 us -> 48.7 us
  local copies, waits for them, and re-layouts: 7.77 us -> 4.75 us
    ppermute x6 -> x2, starting transfers between devices: 37.1 us -> 5.68 us  [the longest x1 3.53 us: shards(): blocks = weight_split(keep, lax.ppermute(send, 'c', SWAP_CORE), piece)]
    ppermute x6 -> x2, waiting for transfers between devices: 23.5 us -> 2.98 us  [the longest x1 1.53 us: shards(): lax.ppermute(own, 'c', SWAP_CORE)]
    all_to_all x1, waiting for transfers between devices: 1.46 us -> 17.5 us  [shards(): lax.all_to_all(blocks, ('dp', 'z', 'y'), split_axis=0, concat_axis=0, til...]
    all_gather x1, waiting for transfers between devices: 0.01 us -> 10.6 us  [shards(): lax.all_gather(grad_out, 'tm', axis=1, tiled=True).reshape(4, LANES, 1152)]
    ppermute x3, waiting for transfers between devices: 0.01 us -> 6.58 us  [shards(): lax.ppermute(sends[shift], 'tm', RING[shift - 1])]
    ppermute x3, waiting for transfers between devices: 4.26 us -> 10.3 us  [shards(): lax.ppermute(backs[shift], 'tm', RING_BACK[shift - 1])]
    all_to_all x1, starting transfers between devices: 19.5 us -> 15.5 us  [shards(): lax.all_to_all(blocks, ('dp', 'z', 'y'), split_axis=0, concat_axis=0, til...]
    reshape x2 -> x0, local copies, waits for them, and re-layouts: 3 us -> none  [the longest x1 1.68 us: shards(): w_tout.reshape(8, 36, 288)]
  transfers between devices with their start and end apart: 16 -> 12, of which waited for: 8 -> 9; matrix products, arithmetic and copies ran while one was open for 1% -> 0% of each run, Pallas kernels for 21% -> 24%
where the time goes in v4:
time: 179 us
  starting transfers between devices  59 us (33%)
  Pallas kernels  51.3 us (29%)
  waiting for transfers between devices  48.7 us (27%)
  between operations  14.2 us (8%)
  local copies, waits for them, and re-layouts  4.75 us (3%)
    pallas_call x1, Pallas kernels, attend(): pl.pallas_call(functools.partial(attend_kernel, step=step), out_shape=jax...  23.4 us
    all_to_all x1, waiting for transfers between devices, shards(): lax.all_to_all(blocks, ('dp', 'z', 'y'), split_axis=0, concat_axis=0, til...  17.5 us
    all_to_all x1, starting transfers between devices, shards(): lax.all_to_all(blocks, ('dp', 'z', 'y'), split_axis=0, concat_axis=0, til...  15.5 us
    all_gather x1, waiting for transfers between devices, shards(): lax.all_gather(grad_out, 'tm', axis=1, tiled=True).reshape(4, LANES, 1152)  10.6 us
    all_to_all x1, starting transfers between devices, shards(): lax.all_to_all(packed, space, split_axis=0, concat_axis=0, tiled=True)  10.5 us
    ppermute x3, waiting for transfers between devices, shards(): lax.ppermute(backs[shift], 'tm', RING_BACK[shift - 1])  10.3 us
    ppermute x3, starting transfers between devices, shards(): lax.ppermute(sends[shift], 'tm', RING[shift - 1])  10.3 us
    ppermute x3, starting transfers between devices, shards(): lax.ppermute(backs[shift], 'tm', RING_BACK[shift - 1])  8.6 us
  transfers between devices with their start and end apart: 12, of which 9 were waited for; matrix products, arithmetic and copies ran while one was open for 0% of the time, Pallas kernels for 24%

profile of v4, /device:TPU:1, one launch (start us, length us, event | category | flops | bytes accessed | tf_op | source)
XLA Modules:
  0.0 178.6 jit_solution(7487175207130336569)
XLA Ops:
  7.2 2.6 %spatial_pack.1 = bf16[32,2,72,128]{3,2,1,0:T(8,128)(2,1)} custom-call(bf16[2,64,1152]{2,1,0:T(8,128)(2,1)} %bitcast.20, bf16[2,64,1152]{2,1,0:T(8,128)(2,1)} %bitcast.21, bf16[2,64,1152]{2,1,0:T(8,128)(2,1)} %bitcast.22, bf16[2,64,1152]{2,1,0:T(8,128)(2,1)} %bitcast.23), custom_call_target="tpu_custom_call" | custom-call | tf_op jit(solution)/shard_map/spatial_pack/pallas_call | solution.py:45
  9.8 10.5 %all-to-all-start = ((bf16[32,2,72,128]{3,2,1,0:T(8,128)(2,1)}), bf16[32,2,72,128]{3,2,1,0:T(8,128)(2,1)S(1)}, u32[]{:S(2)}, u32[]{:S(2)}) async-start(bf16[32,2,72,128]{3,2,1,0:T(8,128)(2,1)} %spatial_pack.1), calls=%async_computation | async-start | bytes 2359296 | tf_op jit(solution)/shard_map/all_to_all | solution.py:550
  20.3 0.0 all-gather.2.cloned.1.call-start
  20.3 0.7 all-gather.2.cloned.1.call-update
  21.0 0.6 pad_add_fusion.me_ref
  21.7 2.6 %temporal_pack.1 = (bf16[288,384]{1,0:T(8,128)(2,1)}, bf16[288,384]{1,0:T(8,128)(2,1)}, bf16[288,384]{1,0:T(8,128)(2,1)}, bf16[288,384]{1,0:T(8,128)(2,1)}, bf16[24,128]{1,0:T(8,128)(2,1)}) custom-call(s32[3]{0:T(128)} %pad_add_fusion.me_ref, bf16[2,64,1152]{2,1,0:T(8,128)(2,1)} %bitcast.25, bf16[2,64,1152]{2,1,0:T(8,128)(2,1)} %bitcast.26, ...), custom_call_target="tpu_custom_call" | custom-call | tf_op jit(solution)/shard_map/temporal_pack/pallas_call | solution.py:256
  24.3 2.8 %collective-permute-start = (bf16[288,384]{1,0:T(8,128)(2,1)}, bf16[288,384]{1,0:T(8,128)(2,1)S(1)}, u32[]{:S(2)}, u32[]{:S(2)}) collective-permute-start(bf16[288,384]{1,0:T(8,128)(2,1)} %get-tuple-element.38), channel_id=1, source_target_pairs={{0,32},{32,64},{64,96},{96,0},{1,33},{33,65},{65,97},{97,1},{2,34}... | collective-permute-start | bytes 663560 | tf_op jit(solution)/shard_map/ppermute | solution.py:554
  27.1 4.4 %collective-permute-start.1 = (bf16[288,384]{1,0:T(8,128)(2,1)}, bf16[288,384]{1,0:T(8,128)(2,1)S(1)}, u32[]{:S(2)}, u32[]{:S(2)}) collective-permute-start(bf16[288,384]{1,0:T(8,128)(2,1)} %get-tuple-element.39), channel_id=1, source_target_pairs={{0,64},{32,96},{64,0},{96,32},{1,65},{33,97},{65,1},{97,33},{2,66}... | collective-permute-start | bytes 663560 | tf_op jit(solution)/shard_map/ppermute | solution.py:554
  31.5 3.1 %collective-permute-start.2 = (bf16[288,384]{1,0:T(8,128)(2,1)}, bf16[288,384]{1,0:T(8,128)(2,1)S(1)}, u32[]{:S(2)}, u32[]{:S(2)}) collective-permute-start(bf16[288,384]{1,0:T(8,128)(2,1)} %get-tuple-element.40), channel_id=1, source_target_pairs={{0,96},{32,0},{64,32},{96,64},{1,97},{33,1},{65,33},{97,65},{2,98}... | collective-permute-start | bytes 663560 | tf_op jit(solution)/shard_map/ppermute | solution.py:554
  34.6 0.0 collective-permute-done.in1
  34.6 0.0 copy-start.3
  34.6 5.3 %collective-permute-done.1.in2 = bf16[288,384]{1,0:T(8,128)(2,1)S(1)} collective-permute-done((bf16[288,384]{1,0:T(8,128)(2,1)}, bf16[288,384]{1,0:T(8,128)(2,1)S(1)}, u32[]{:S(2)}, u32[]{:S(2)}) %collective-permute-start.1) | collective-permute-done | bytes 221216 | tf_op jit(solution)/shard_map/ppermute | solution.py:554
  39.9 0.0 copy-start.4
  39.9 1.3 collective-permute-done.2.in3
  41.2 0.0 copy-start.5
  41.2 0.0 copy-done.3
  41.2 0.0 copy-done.4
  41.2 0.7 copy-done.5
  41.9 3.1 %temporal_tout.1.tout_ref = bf16[4,288,128]{2,1,0:T(8,128)(2,1)} custom-call(s32[3]{0:T(128)} %pad_add_fusion.me_ref, bf16[288,384]{1,0:T(8,128)(2,1)} %get-tuple-element.37.in0, bf16[288,384]{1,0:T(8,128)(2,1)} %copy-done.3, bf16[288,384]{1,0:T(8,128)(2,1)} %copy-done.4, bf16[288,384]{1,0:T(8,128)(2,1)} %copy-done.5), custom_call_target="tpu_custom_call" | custom-call | tf_op jit(solution)/shard_map/temporal_tout/pallas_call | solution.py:321
  45.0 10.6 %all-gather.2.cloned.1.call-done = bf16[1,8,64,1152]{3,2,0,1:T(8,128)(2,1)} async-done(((bf16[1,2,64,1152]{3,2,0,1:T(8,128)(2,1)}), bf16[1,8,64,1152]{3,2,0,1:T(8,128)(2,1)}) %all-gather.2.cloned.1.call-update) | async-done | bytes 1179664 | tf_op jit(solution)/shard_map/all_gather | solution.py:545
  55.6 3.2 %weight_partial.1 = (f32[144,1152]{1,0:T(8,128)}, bf16[144,1152]{1,0:T(8,128)(2,1)}) custom-call(s32[3]{0:T(128)} %pad_add_fusion.me_ref, bf16[4,288,128]{2,1,0:T(8,128)(2,1)} %temporal_tout.1.tout_ref, bf16[4,128,1152]{2,1,0:T(8,128)(2,1)} %bitcast.18), custom_call_target="tpu_custom_call" | custom-call | tf_op jit(solution)/shard_map/weight_partial/pallas_call | solution.py:348
  58.8 3.5 %collective-permute-start.3 = (bf16[144,1152]{1,0:T(8,128)(2,1)}, bf16[144,1152]{1,0:T(8,128)(2,1)S(1)}, u32[]{:S(2)}, u32[]{:S(2)}) collective-permute-start(bf16[144,1152]{1,0:T(8,128)(2,1)} %get-tuple-element.42), channel_id=1, source_target_pairs={{0,1},{1,0},{2,3},{3,2},{4,5},{5,4},{6,7},{7,6},{8,9},{9,8},{10,11... | collective-permute-start | bytes 995336 | tf_op jit(solution)/shard_map/ppermute | solution.py:558
  62.3 1.4 collective-permute-done.3.got_ref
  63.8 0.0 copy-start.8
  63.8 0.7 copy-done.8
  64.5 2.5 %weight_split.1 = bf16[64,48,128]{2,1,0:T(8,128)(2,1)} custom-call(f32[144,1152]{1,0:T(8,128)} %get-tuple-element.41.keep_ref, bf16[144,1152]{1,0:T(8,128)(2,1)} %copy-done.8, bf16[24,128]{1,0:T(8,128)(2,1)} %get-tuple-element.43.piece_ref), custom_call_target="tpu_custom_call" | custom-call | tf_op jit(solution)/shard_map/weight_split/pallas_call | solution.py:380
  67.0 0.0 all-to-all-done.in_ref
  67.0 0.0 copy-start.2
  67.0 15.5 %all-to-all-start.1 = ((bf16[64,48,128]{2,1,0:T(8,128)(2,1)}), bf16[64,48,128]{2,1,0:T(8,128)(2,1)S(1)}, u32[]{:S(2)}, u32[]{:S(2)}) async-start(bf16[64,48,128]{2,1,0:T(8,128)(2,1)} %weight_split.1), calls=%async_computation.1 | async-start | bytes 1572864 | tf_op jit(solution)/shard_map/all_to_all | solution.py:561
  82.5 0.0 copy-done.2
  82.6 23.4 %spatial_attention.1.spatial_ref = bf16[32,112,128]{2,1,0:T(8,128)(2,1)} custom-call(bf16[32,2,72,128]{3,2,1,0:T(8,128)(2,1)} %copy-done.2), custom_call_target="tpu_custom_call" | custom-call | flops 10737418240 | bytes 2200000 | tf_op jit(solution)/shard_map/spatial_attention/pallas_call | solution.py:146
  106.0 17.5 %all-to-all-done.1.in_ref = bf16[64,48,128]{2,1,0:T(8,128)(2,1)S(1)} async-done(((bf16[64,48,128]{2,1,0:T(8,128)(2,1)}), bf16[64,48,128]{2,1,0:T(8,128)(2,1)S(1)}, u32[]{:S(2)}, u32[]{:S(2)}) %all-to-all-start.1) | async-done | bytes 786464 | tf_op jit(solution)/shard_map/all_to_all | solution.py:561
  123.5 0.0 copy-start.1
  123.5 0.9 copy-done.1
  124.4 2.8 %weight_join.1 = (bf16[32,136,128]{2,1,0:T(8,128)(2,1)}, bf16[4,144,288]{2,1,0:T(8,128)(2,1)}) custom-call(bf16[32,112,128]{2,1,0:T(8,128)(2,1)} %spatial_attention.1.spatial_ref, bf16[64,48,128]{2,1,0:T(8,128)(2,1)} %copy-done.1), custom_call_target="tpu_custom_call" | custom-call | tf_op jit(solution)/shard_map/weight_join/pallas_call | solution.py:415
  127.2 0.0 copy-start.6
  127.2 8.5 %all-to-all-start.2 = ((bf16[32,136,128]{2,1,0:T(8,128)(2,1)}), bf16[32,136,128]{2,1,0:T(8,128)(2,1)S(1)}, u32[]{:S(2)}, u32[]{:S(2)}) async-start(bf16[32,136,128]{2,1,0:T(8,128)(2,1)} %get-tuple-element.46), calls=%async_computation.2 | async-start | bytes 2228224 | tf_op jit(solution)/shard_map/all_to_all | solution.py:563
  135.7 0.0 copy-done.6
  135.7 2.1 %collective-permute-start.4 = (bf16[4,144,288]{2,1,0:T(8,128)(2,1)S(1)}, bf16[4,144,288]{2,1,0:T(8,128)(2,1)S(1)}, u32[]{:S(2)}, u32[]{:S(2)}) collective-permute-start(bf16[4,144,288]{2,1,0:T(8,128)(2,1)S(1)} %copy-done.6), channel_id=1, source_target_pairs={{0,1},{1,0},{2,3},{3,2},{4,5},{5,4},{6,7},{7,6},{8,9},{9,8},{10,11... | collective-permute-start | bytes 995336 | tf_op jit(solution)/shard_map/ppermute | solution.py:565
  137.8 1.5 collective-permute-done.4.other_ref
  139.4 0.0 copy-start.7
  139.4 0.8 copy-done.7
  140.1 5.8 %temporal_back.1 = (bf16[288,384]{1,0:T(8,128)(2,1)}, bf16[288,384]{1,0:T(8,128)(2,1)}, bf16[288,384]{1,0:T(8,128)(2,1)}, bf16[288,384]{1,0:T(8,128)(2,1)}) custom-call(s32[3]{0:T(128)} %pad_add_fusion.me_ref, bf16[288,384]{1,0:T(8,128)(2,1)} %get-tuple-element.37.in0, bf16[288,384]{1,0:T(8,128)(2,1)} %copy-done.3, bf16[288,384]{1,0:T(8,128)(2,1)} %copy-done.4, ...), custom_call_target="tpu_custom_call" | custom-call | tf_op jit(solution)/shard_map/temporal_back/pallas_call | solution.py:485
  145.9 3.2 %collective-permute-start.5 = (bf16[288,384]{1,0:T(8,128)(2,1)}, bf16[288,384]{1,0:T(8,128)(2,1)S(1)}, u32[]{:S(2)}, u32[]{:S(2)}) collective-permute-start(bf16[288,384]{1,0:T(8,128)(2,1)} %get-tuple-element.52), channel_id=1, source_target_pairs={{0,96},{32,0},{64,32},{96,64},{1,97},{33,1},{65,33},{97,65},{2,98}... | collective-permute-start | bytes 663560 | tf_op jit(solution)/shard_map/ppermute | solution.py:567
  149.2 2.6 %collective-permute-start.6 = (bf16[288,384]{1,0:T(8,128)(2,1)}, bf16[288,384]{1,0:T(8,128)(2,1)S(1)}, u32[]{:S(2)}, u32[]{:S(2)}) collective-permute-start(bf16[288,384]{1,0:T(8,128)(2,1)} %get-tuple-element.53), channel_id=1, source_target_pairs={{0,64},{32,96},{64,0},{96,32},{1,65},{33,97},{65,1},{97,33},{2,66}... | collective-permute-start | bytes 663560 | tf_op jit(solution)/shard_map/ppermute | solution.py:567
  151.8 2.8 %collective-permute-start.7 = (bf16[288,384]{1,0:T(8,128)(2,1)}, bf16[288,384]{1,0:T(8,128)(2,1)S(1)}, u32[]{:S(2)}, u32[]{:S(2)}) collective-permute-start(bf16[288,384]{1,0:T(8,128)(2,1)} %get-tuple-element.54), channel_id=1, source_target_pairs={{0,32},{32,64},{64,96},{96,0},{1,33},{33,65},{65,97},{97,1},{2,34}... | collective-permute-start | bytes 663560 | tf_op jit(solution)/shard_map/ppermute | solution.py:567
  154.5 0.3 collective-permute-done.5.in1
  154.8 0.0 copy-start.9
  154.8 4.4 %collective-permute-done.6.in2 = bf16[288,384]{1,0:T(8,128)(2,1)S(1)} collective-permute-done((bf16[288,384]{1,0:T(8,128)(2,1)}, bf16[288,384]{1,0:T(8,128)(2,1)S(1)}, u32[]{:S(2)}, u32[]{:S(2)}) %collective-permute-start.6) | collective-permute-done | bytes 221216 | tf_op jit(solution)/shard_map/ppermute | solution.py:567
  159.3 0.0 copy-start.10
  159.3 5.6 %collective-permute-done.7.in3 = bf16[288,384]{1,0:T(8,128)(2,1)S(1)} collective-permute-done((bf16[288,384]{1,0:T(8,128)(2,1)}, bf16[288,384]{1,0:T(8,128)(2,1)S(1)}, u32[]{:S(2)}, u32[]{:S(2)}) %collective-permute-start.7) | collective-permute-done | bytes 221216 | tf_op jit(solution)/shard_map/ppermute | solution.py:567
  164.9 0.0 copy-start.11
  164.9 0.0 copy-done.9
  164.9 0.0 copy-done.10
  164.9 0.7 copy-done.11
  165.6 2.5 %temporal_unpack.1 = (bf16[2,64,1152]{2,1,0:T(8,128)(2,1)}, bf16[2,64,1152]{2,1,0:T(8,128)(2,1)}, bf16[2,64,1152]{2,1,0:T(8,128)(2,1)}) custom-call(s32[3]{0:T(128)} %pad_add_fusion.me_ref, bf16[288,384]{1,0:T(8,128)(2,1)} %get-tuple-element.51.in0, bf16[288,384]{1,0:T(8,128)(2,1)} %copy-done.9, bf16[288,384]{1,0:T(8,128)(2,1)} %copy-done.10, ...), custom_call_target="tpu_custom_call" | custom-call | tf_op jit(solution)/shard_map/temporal_unpack/pallas_call | solution.py:514
  168.0 0.0 all-to-all-done.2.in_ref
  168.0 0.0 copy-start
  168.0 1.0 copy-done
  169.0 2.7 %spatial_unpack.1 = (bf16[2,64,1152]{2,1,0:T(8,128)(2,1)}, bf16[2,64,1152]{2,1,0:T(8,128)(2,1)}, bf16[2,64,1152]{2,1,0:T(8,128)(2,1)}, f32[288,288]{1,0:T(8,128)}) custom-call(bf16[32,136,128]{2,1,0:T(8,128)(2,1)} %copy-done), custom_call_target="tpu_custom_call" | custom-call | tf_op jit(solution)/shard_map/spatial_unpack/pallas_call | solution.py:199
Async XLA Ops:
  9.8 57.2 %all-to-all-start = ((bf16[32,2,72,128]{3,2,1,0:T(8,128)(2,1)}), bf16[32,2,72,128]{3,2,1,0:T(8,128)(2,1)S(1)}, u32[]{:S(2)}, u32[]{:S(2)}) async-start(bf16[32,2,72,128]{3,2,1,0:T(8,128)(2,1)} %spatial_pack.1), calls=%async_computation | async-start | bytes 2359296 | tf_op jit(solution)/shard_map/all_to_all | solution.py:550
  20.3 35.3 %all-gather.2.cloned.1.call-start = ((), (), s32[]{:S(2)}) async-start(), calls=%async_computation.3 | async-start | bytes 1474560 | tf_op jit(solution)/shard_map/all_gather | solution.py:545
  24.3 10.3 %collective-permute-start = (bf16[288,384]{1,0:T(8,128)(2,1)}, bf16[288,384]{1,0:T(8,128)(2,1)S(1)}, u32[]{:S(2)}, u32[]{:S(2)}) collective-permute-start(bf16[288,384]{1,0:T(8,128)(2,1)} %get-tuple-element.38), channel_id=1, source_target_pairs={{0,32},{32,64},{64,96},{96,0},{1,33},{33,65},{65,97},{97,1},{2,34}... | collective-permute-start | bytes 663560 | tf_op jit(solution)/shard_map/ppermute | solution.py:554
  27.1 12.7 %collective-permute-start.1 = (bf16[288,384]{1,0:T(8,128)(2,1)}, bf16[288,384]{1,0:T(8,128)(2,1)S(1)}, u32[]{:S(2)}, u32[]{:S(2)}) collective-permute-start(bf16[288,384]{1,0:T(8,128)(2,1)} %get-tuple-element.39), channel_id=1, source_target_pairs={{0,64},{32,96},{64,0},{96,32},{1,65},{33,97},{65,1},{97,33},{2,66}... | collective-permute-start | bytes 663560 | tf_op jit(solution)/shard_map/ppermute | solution.py:554
  31.5 9.7 %collective-permute-start.2 = (bf16[288,384]{1,0:T(8,128)(2,1)}, bf16[288,384]{1,0:T(8,128)(2,1)S(1)}, u32[]{:S(2)}, u32[]{:S(2)}) collective-permute-start(bf16[288,384]{1,0:T(8,128)(2,1)} %get-tuple-element.40), channel_id=1, source_target_pairs={{0,96},{32,0},{64,32},{96,64},{1,97},{33,1},{65,33},{97,65},{2,98}... | collective-permute-start | bytes 663560 | tf_op jit(solution)/shard_map/ppermute | solution.py:554
  34.6 6.6 %copy-start.3 = (bf16[288,384]{1,0:T(8,128)(2,1)}, bf16[288,384]{1,0:T(8,128)(2,1)S(1)}, u32[]{:S(2)}) copy-start(bf16[288,384]{1,0:T(8,128)(2,1)S(1)} %collective-permute-done.in1) | copy-start | bytes 663556
  39.9 1.3 copy-start.4
  41.2 0.7 copy-start.5
  58.8 5.0 %collective-permute-start.3 = (bf16[144,1152]{1,0:T(8,128)(2,1)}, bf16[144,1152]{1,0:T(8,128)(2,1)S(1)}, u32[]{:S(2)}, u32[]{:S(2)}) collective-permute-start(bf16[144,1152]{1,0:T(8,128)(2,1)} %get-tuple-element.42), channel_id=1, source_target_pairs={{0,1},{1,0},{2,3},{3,2},{4,5},{5,4},{6,7},{7,6},{8,9},{9,8},{10,11... | collective-permute-start | bytes 995336 | tf_op jit(solution)/shard_map/ppermute | solution.py:558
  63.8 0.7 copy-start.8
  67.0 15.6 %copy-start.2 = (bf16[32,2,72,128]{3,2,1,0:T(8,128)(2,1)}, bf16[32,2,72,128]{3,2,1,0:T(8,128)(2,1)S(1)}, u32[]{:S(2)}) copy-start(bf16[32,2,72,128]{3,2,1,0:T(8,128)(2,1)S(1)} %all-to-all-done.in_ref) | copy-start | bytes 3538948
  67.0 56.5 %all-to-all-start.1 = ((bf16[64,48,128]{2,1,0:T(8,128)(2,1)}), bf16[64,48,128]{2,1,0:T(8,128)(2,1)S(1)}, u32[]{:S(2)}, u32[]{:S(2)}) async-start(bf16[64,48,128]{2,1,0:T(8,128)(2,1)} %weight_split.1), calls=%async_computation.1 | async-start | bytes 1572864 | tf_op jit(solution)/shard_map/all_to_all | solution.py:561
  123.5 0.9 copy-start.1
  127.2 8.5 %copy-start.6 = (bf16[4,144,288]{2,1,0:T(8,128)(2,1)S(1)}, bf16[4,144,288]{2,1,0:T(8,128)(2,1)}, u32[]{:S(2)}) copy-start(bf16[4,144,288]{2,1,0:T(8,128)(2,1)} %get-tuple-element.50.own_ref) | copy-start | bytes 995332
  127.2 40.8 %all-to-all-start.2 = ((bf16[32,136,128]{2,1,0:T(8,128)(2,1)}), bf16[32,136,128]{2,1,0:T(8,128)(2,1)S(1)}, u32[]{:S(2)}, u32[]{:S(2)}) async-start(bf16[32,136,128]{2,1,0:T(8,128)(2,1)} %get-tuple-element.46), calls=%async_computation.2 | async-start | bytes 2228224 | tf_op jit(solution)/shard_map/all_to_all | solution.py:563
  135.7 3.7 %collective-permute-start.4 = (bf16[4,144,288]{2,1,0:T(8,128)(2,1)S(1)}, bf16[4,144,288]{2,1,0:T(8,128)(2,1)S(1)}, u32[]{:S(2)}, u32[]{:S(2)}) collective-permute-start(bf16[4,144,288]{2,1,0:T(8,128)(2,1)S(1)} %copy-done.6), channel_id=1, source_target_pairs={{0,1},{1,0},{2,3},{3,2},{4,5},{5,4},{6,7},{7,6},{8,9},{9,8},{10,11... | collective-permute-start | bytes 995336 | tf_op jit(solution)/shard_map/ppermute | solution.py:565
  139.4 0.8 copy-start.7
  145.9 8.9 %collective-permute-start.5 = (bf16[288,384]{1,0:T(8,128)(2,1)}, bf16[288,384]{1,0:T(8,128)(2,1)S(1)}, u32[]{:S(2)}, u32[]{:S(2)}) collective-permute-start(bf16[288,384]{1,0:T(8,128)(2,1)} %get-tuple-element.52), channel_id=1, source_target_pairs={{0,96},{32,0},{64,32},{96,64},{1,97},{33,1},{65,33},{97,65},{2,98}... | collective-permute-start | bytes 663560 | tf_op jit(solution)/shard_map/ppermute | solution.py:567
  149.2 10.1 %collective-permute-start.6 = (bf16[288,384]{1,0:T(8,128)(2,1)}, bf16[288,384]{1,0:T(8,128)(2,1)S(1)}, u32[]{:S(2)}, u32[]{:S(2)}) collective-permute-start(bf16[288,384]{1,0:T(8,128)(2,1)} %get-tuple-element.53), channel_id=1, source_target_pairs={{0,64},{32,96},{64,0},{96,32},{1,65},{33,97},{65,1},{97,33},{2,66}... | collective-permute-start | bytes 663560 | tf_op jit(solution)/shard_map/ppermute | solution.py:567
  151.8 13.1 %collective-permute-start.7 = (bf16[288,384]{1,0:T(8,128)(2,1)}, bf16[288,384]{1,0:T(8,128)(2,1)S(1)}, u32[]{:S(2)}, u32[]{:S(2)}) collective-permute-start(bf16[288,384]{1,0:T(8,128)(2,1)} %get-tuple-element.54), channel_id=1, source_target_pairs={{0,32},{32,64},{64,96},{96,0},{1,33},{33,65},{65,97},{97,1},{2,34}... | collective-permute-start | bytes 663560 | tf_op jit(solution)/shard_map/ppermute | solution.py:567
  154.8 10.1 %copy-start.9 = (bf16[288,384]{1,0:T(8,128)(2,1)}, bf16[288,384]{1,0:T(8,128)(2,1)S(1)}, u32[]{:S(2)}) copy-start(bf16[288,384]{1,0:T(8,128)(2,1)S(1)} %collective-permute-done.5.in1) | copy-start | bytes 663556
  159.3 5.6 %copy-start.10 = (bf16[288,384]{1,0:T(8,128)(2,1)}, bf16[288,384]{1,0:T(8,128)(2,1)S(1)}, u32[]{:S(2)}) copy-start(bf16[288,384]{1,0:T(8,128)(2,1)S(1)} %collective-permute-done.6.in2) | copy-start | bytes 663556
  164.9 0.7 copy-start.11
  168.0 1.0 copy-start
Sparse Core Ops, SparseCore 0:
  23.2 32.3 all-gather.1

commit v5 on v3

--- a/solution.py
+++ b/solution.py
@@ -15,7 +15,7 @@
 F32 = jnp.float32
 BF16 = jnp.bfloat16
 LIMIT = 56 * 1024 * 1024
-LAST = (((1,), (1,)), ((), ()))
+SMALL = pl.CostEstimate(flops=1000, bytes_accessed=1000, transcendentals=0)
 
 
 def vmem_specs(count):
@@ -48,6 +48,7 @@
         in_specs=vmem_specs(4),
         out_specs=pl.BlockSpec(memory_space=pltpu.VMEM),
         compiler_params=pltpu.CompilerParams(vmem_limit_bytes=LIMIT),
+        cost_estimate=SMALL,
         name="spatial_pack",
     )(q, k, v, g)
 
@@ -187,14 +188,10 @@
     dv_ref[0] = both[:HALF]
     dv_ref[1] = both[HALF:]
     for s in range(2 * HEADS):
-        block = in_ref[s, HDIM + FOLD :].astype(F32)
-        start = 144 * (s % 2) + 8 * (s // 2)
-        for tile in range(3):
-            at = slice(tile * LANES, (tile + 1) * LANES)
-            full[start : start + 8, at] = block[tile * 8 : tile * 8 + 8]
-        start = 144 * (s % 2) + 128 + s // 2
-        for r in range(3):
-            full[start : start + 1, 96 * r : 96 * r + 96] = block[16 + r : 17 + r, 32:]
+        half = 144 * (s % 2)
+        unfold(
+            in_ref[s].astype(F32)[HDIM + FOLD :], full, half + 8 * (s // 2), half + 128 + s // 2
+        )
     dw_ref[...] = full[...].T[:288]
 
 
@@ -215,8 +212,13 @@
     return pltpu.roll(block, HALF, 1)
 
 
-def send_pack_kernel(me_ref, q_ref, k_ref, v_ref, w_ref, out0, out1, out2, out3, slice_ref, held):
-    slice_ref[...] = w_ref[me_ref[1]]
+def fold_tail(rest, r):
+    return jnp.concatenate(
+        [jnp.zeros((rest.shape[0], 32), F32), rest[:, 96 * r : 96 * r + 96]], axis=1
+    )
+
+
+def send_pack_kernel(me_ref, q_ref, k_ref, v_ref, out0, out1, out2, out3, held):
     for part, ref in enumerate((q_ref, k_ref, v_ref)):
         rows = jnp.concatenate([ref[0], ref[1]], axis=0).astype(F32)
         columns = rows.T.astype(BF16)
@@ -230,18 +232,18 @@
         out[...] = held[lax.rem(me + shift, 4)]
 
 
-def send_pack(me, q, k, v, w):
+def send_pack(me, q, k, v):
     shape = jax.ShapeDtypeStruct((288, 3 * LANES), BF16)
-    part = jax.ShapeDtypeStruct((36, 288), BF16)
     return pl.pallas_call(
         send_pack_kernel,
-        out_shape=(shape,) * 4 + (part,),
-        in_specs=[pl.BlockSpec(memory_space=pltpu.SMEM)] + vmem_specs(4),
-        out_specs=tuple(vmem_specs(5)),
+        out_shape=(shape,) * 4,
+        in_specs=[pl.BlockSpec(memory_space=pltpu.SMEM)] + vmem_specs(3),
+        out_specs=tuple(vmem_specs(4)),
         scratch_shapes=[pltpu.VMEM((4, 288, 3 * LANES), BF16)],
         compiler_params=pltpu.CompilerParams(vmem_limit_bytes=LIMIT),
+        cost_estimate=SMALL,
         name="temporal_pack",
-    )(me, q, k, v, w)
+    )(me, q, k, v)
 
 
 def rows_of(values):
@@ -272,13 +274,7 @@
     return out
 
 
-def pair_up(bit, own_ref, got_ref, out_ref):
-    out_ref[bit] = own_ref[...]
-    out_ref[1 - bit] = got_ref[...]
-
-
-def tout_kernel(me_ref, in0, in1, in2, in3, own_ref, got_ref, out_ref, w_ref, wide, total):
-    pair_up(lax.rem(me_ref[2], 2), own_ref, got_ref, w_ref)
+def tout_kernel(me_ref, in0, in1, in2, in3, out_ref, wide, total):
     for shift, ref in enumerate((in0, in1, in2, in3)):
         wide[shift] = ref[...].astype(F32)
 
@@ -300,53 +296,66 @@
         out_ref[lax.rem(me + 4 - shift, 4)] = total[shift].astype(BF16)
 
 
-def temporal_out(me, pieces, own, got):
+def temporal_out(me, pieces):
     return pl.pallas_call(
         tout_kernel,
-        out_shape=(
-            jax.ShapeDtypeStruct((4, 288, LANES), BF16),
-            jax.ShapeDtypeStruct((2, 36, 288), BF16),
-        ),
-        in_specs=[pl.BlockSpec(memory_space=pltpu.SMEM)] + vmem_specs(6),
-        out_specs=tuple(vmem_specs(2)),
+        out_shape=jax.ShapeDtypeStruct((4, 288, LANES), BF16),
+        in_specs=[pl.BlockSpec(memory_space=pltpu.SMEM)] + vmem_specs(4),
+        out_specs=pl.BlockSpec(memory_space=pltpu.VMEM),
         scratch_shapes=[
             pltpu.VMEM((4, 288, 3 * LANES), F32),
             pltpu.VMEM((4, 288, LANES), F32),
         ],
         compiler_params=pltpu.CompilerParams(vmem_limit_bytes=LIMIT),
+        cost_estimate=SMALL,
         name="temporal_tout",
-    )(me, *pieces, own, got)
+    )(me, *pieces)
 
 
 def partial_kernel(
-    me_ref, tout_ref, grad_ref, own_ref, got_ref, keep_ref, send_ref, w_ref, full, *, scale
+    me_ref, tout_ref, grad_ref, w_ref, keep_ref, send_ref, slice_ref, full, stage, rows, *, scale
 ):
-    pair_up(me_ref[2] // 2, own_ref, got_ref, w_ref)
     total = jnp.dot(tout_ref[0], grad_ref[0], preferred_element_type=F32)
     for a in range(1, 4):
         total = total + jnp.dot(tout_ref[a], grad_ref[a], preferred_element_type=F32)
     total = total * scale
     full[0] = total[:144]
     full[1] = total[144:]
-    core = me_ref[3]
+    core, eighth = me_ref[2], me_ref[1]
     keep_ref[...] = full[core]
     send_ref[...] = full[1 - core].astype(BF16)
 
-
-def weight_partial(me, tout, grads, own, got, scale):
+    rows[...] = w_ref[...].astype(F32)
+    stage[...] = jnp.zeros_like(stage)
+    tail = rows[256:288]
+    index = lax.broadcasted_iota(jnp.int32, tail.shape, 0)
+    for k in range(4):
+        at = slice(288 * k, 288 * (k + 1))
+        stage[0:8, at] = rows[pl.ds(pl.multiple_of(32 * eighth + 8 * k, 8), 8)]
+        stage[8:9, at] = jnp.sum(
+            jnp.where(index == 4 * eighth + k, tail, 0.0), axis=0, keepdims=True
+        )
+    slice_ref[...] = stage[...].astype(BF16)
+
+
+def weight_partial(me, tout, grads, w, scale):
     return pl.pallas_call(
         functools.partial(partial_kernel, scale=scale),
         out_shape=(
             jax.ShapeDtypeStruct((144, 1152), F32),
             jax.ShapeDtypeStruct((144, 1152), BF16),
-            jax.ShapeDtypeStruct((2, 2, 36, 288), BF16),
+            jax.ShapeDtypeStruct((16, 1152), BF16),
         ),
-        in_specs=[pl.BlockSpec(memory_space=pltpu.SMEM)] + vmem_specs(4),
+        in_specs=[pl.BlockSpec(memory_space=pltpu.SMEM)] + vmem_specs(3),
         out_specs=tuple(vmem_specs(3)),
-        scratch_shapes=[pltpu.VMEM((2, 144, 1152), F32)],
+        scratch_shapes=[
+            pltpu.VMEM((2, 144, 1152), F32),
+            pltpu.VMEM((16, 1152), F32),
+            pltpu.VMEM((288, 288), F32),
+        ],
         compiler_params=pltpu.CompilerParams(vmem_limit_bytes=LIMIT),
         name="weight_partial",
-    )(me, tout, grads, own, got)
+    )(me, tout, grads, w)
 
 
 def weight_split_kernel(keep_ref, got_ref, out_ref, full, part):
@@ -361,11 +370,14 @@
         ]
         rest = part[128:144, :]
         for r in range(3):
-            moved = jnp.concatenate(
-                [jnp.zeros((16, 32), F32), rest[:, 96 * r : 96 * r + 96]], axis=1
-            )
-            tiles[2] = tiles[2] + jnp.where(row == r, moved[:, None, :], 0.0)
+            tiles[2] = tiles[2] + jnp.where(row == r, fold_tail(rest, r)[:, None, :], 0.0)
         out_ref[d * 16 : (d + 1) * 16] = jnp.concatenate(tiles, axis=1).astype(BF16)
+
+
+def fold_tail(rest, r):
+    return jnp.concatenate(
+        [jnp.zeros((rest.shape[0], 32), F32), rest[:, 96 * r : 96 * r + 96]], axis=1
+    )
 
 
 def weight_split(keep, got):
@@ -378,6 +390,14 @@
         compiler_params=pltpu.CompilerParams(vmem_limit_bytes=LIMIT),
         name="weight_split",
     )(keep, got)
+
+
+def unfold(block, full, start, last):
+    for tile in range(3):
+        at = slice(tile * LANES, (tile + 1) * LANES)
+        full[start : start + 8, at] = block[tile * 8 : tile * 8 + 8]
+    for r in range(3):
+        full[last : last + 1, 96 * r : 96 * r + 96] = block[16 + r : 17 + r, 32:]
 
 
 def weight_join_kernel(spatial_ref, in_ref, out_ref):
@@ -402,13 +422,25 @@
 
 
 def temporal_kernel(
-    me_ref, in0, in1, in2, in3, grad_ref, w_ref, out0, out1, out2, out3, wide, back
+    me_ref, in0, in1, in2, in3, grad_ref, w_ref, out0, out1, out2, out3, wide, back, full
 ):
     me = me_ref[0]
+    for d in range(4):
+        for y in range(4):
+            for c in range(2):
+                block = w_ref[d * 8 + y * 2 + c].astype(F32)
+                eighth = 4 * c + y
+                for k in range(4):
+                    at = slice(288 * k, 288 * (k + 1))
+                    start = d * 288 + 32 * eighth + 8 * k
+                    full[start : start + 8] = block[0:8, at]
+                    start = d * 288 + 256 + 4 * eighth + k
+                    full[start : start + 1] = block[8:9, at]
+    w = full[...].astype(BF16)
     for shift, ref in enumerate((in0, in1, in2, in3)):
         wide[shift, :, : 3 * LANES] = ref[...].astype(F32)
         grads = grad_ref[lax.rem(me + 4 - shift, 4)]
-        tgrad = rounded(jnp.dot(grads, w_ref[...], preferred_element_type=F32))
+        tgrad = rounded(jnp.dot(grads, w, preferred_element_type=F32))
         wide[shift, :, 3 * LANES :] = tgrad.T
     scale = 1.0 / math.sqrt(HDIM)
 
@@ -460,6 +492,7 @@
         scratch_shapes=[
             pltpu.VMEM((4, 288, 4 * LANES), F32),
             pltpu.VMEM((4, 288, 3 * LANES), F32),
+            pltpu.VMEM((1152, 288), F32),
         ],
         compiler_params=pltpu.CompilerParams(vmem_limit_bytes=LIMIT),
         name="temporal_back",
@@ -491,18 +524,9 @@
     )(me, *pieces)
 
 
-SWAP = [[(i, i ^ s) for i in range(4)] for s in (1, 2)]
 SWAP_CORE = [(0, 1), (1, 0)]
 RING = [[(i, (i + s) % 4) for i in range(4)] for s in (1, 2, 3)]
 RING_BACK = [[(i, (i - s) % 4) for i in range(4)] for s in (1, 2, 3)]
-
-
-def gather_near(block):
-    y, c = lax.axis_index("y"), lax.axis_index("c")
-    for bit, move, axis in ((lax.rem(y, 2), SWAP[0], "y"), (y // 2, SWAP[1], "y"), (c, SWAP_CORE, "c")):
-        got = lax.ppermute(block, axis, move)
-        block = jnp.stack([jnp.where(bit == 0, block, got), jnp.where(bit == 0, got, block)])
-    return block.transpose(3, 4, 0, 1, 2, 5, 6).reshape(1152, 288)
 
 
 def shards(
@@ -516,34 +540,32 @@
     grad_out,
     w_tout,
 ):
-    y, c = lax.axis_index("y"), lax.axis_index("c")
-    me = jnp.stack([lax.axis_index("tm"), 4 * c + y, lax.axis_index("dp"), c])
+    core = lax.axis_index("c")
+    me = jnp.stack([lax.axis_index("tm"), 4 * core + lax.axis_index("y"), core])
     space = ("z", "y", "c")
     grads = lax.all_gather(grad_out, "tm", axis=1, tiled=True).reshape(4, LANES, 1152)
     packed = pack(q_spatial[0], k_spatial[0], v_spatial[0], grad_spatial[0])
-    packed, q, k, v, w = lax.optimization_barrier(
-        (packed, q_temporal[0], k_temporal[0], v_temporal[0], w_tout.reshape(8, 36, 288))
+    packed, q, k, v = lax.optimization_barrier(
+        (packed, q_temporal[0], k_temporal[0], v_temporal[0])
     )
     received = lax.all_to_all(packed, space, split_axis=0, concat_axis=0, tiled=True)
 
-    *sends, own = send_pack(me, q, k, v, w)
-    got = lax.ppermute(own, "dp", SWAP[0])
+    sends = send_pack(me, q, k, v)
     pieces = (sends[0],) + tuple(
         lax.ppermute(sends[shift], "tm", RING[shift - 1]) for shift in (1, 2, 3)
     )
-    tout, own = temporal_out(me, pieces, own, got)
-    got = lax.ppermute(own, "dp", SWAP[1])
-    keep, send, weight = weight_partial(me, tout, grads, own, got, 1.0 / math.sqrt(65536))
+    tout = temporal_out(me, pieces)
+    keep, send, eighth = weight_partial(me, tout, grads, w_tout, 1.0 / math.sqrt(65536))
+    weight = lax.all_gather(eighth, ("dp", "y", "c"), axis=0, tiled=True).reshape(32, 16, 1152)
     blocks = weight_split(keep, lax.ppermute(send, "c", SWAP_CORE))
 
     received, blocks = lax.optimization_barrier((received, blocks))
     blocks = lax.all_to_all(blocks, ("dp", "z", "y"), split_axis=0, concat_axis=0, tiled=True)
-    results = attend(received)
-    results, weight, *pieces = lax.optimization_barrier((results, weight) + pieces)
-    results = weight_join(results, blocks)
+    results = weight_join(attend(received), blocks)
+    results, *pieces = lax.optimization_barrier((results,) + pieces)
     returned = lax.all_to_all(results, space, split_axis=0, concat_axis=0, tiled=True)
 
-    backs = temporal_back(me, pieces, grads, gather_near(weight))
+    backs = temporal_back(me, pieces, grads, weight)
     homes = (backs[0],) + tuple(
         lax.ppermute(backs[shift], "tm", RING_BACK[shift - 1]) for shift in (1, 2, 3)
     )

time: 202 us -> 233 us (1.15)
  waiting for transfers between devices: 29.9 us -> 106 us
  starting transfers between devices: 96.2 us -> 56.9 us
  local copies, waits for them, and re-layouts: 7.77 us -> 3.84 us
    all_gather x0 -> x1, waiting for transfers between devices: none -> 73.7 us  [shards(): lax.all_gather(eighth, ('dp', 'y', 'c'), axis=0, tiled=True)]
    ppermute x5 -> x0, starting transfers between devices: 32.3 us -> none  [the longest x3 12.4 us: gather_near(): got = lax.ppermute(block, axis, move)]
    ppermute x5 -> x0, waiting for transfers between devices: 22 us -> none  [the longest x3 17.5 us: gather_near(): got = lax.ppermute(block, axis, move)]
    all_gather x1, waiting for transfers between devices: 0.01 us -> 10.7 us  [shards(): lax.all_gather(grad_out, 'tm', axis=1, tiled=True).reshape(4, LANES, 1152)]
    ppermute x3, waiting for transfers between devices: 0.01 us -> 6.59 us  [shards(): lax.ppermute(sends[shift], 'tm', RING[shift - 1])]
    ppermute x3, waiting for transfers between devices: 4.26 us -> 10.5 us  [shards(): lax.ppermute(backs[shift], 'tm', RING_BACK[shift - 1])]
    all_to_all x1, starting transfers between devices: 19.5 us -> 15.5 us  [shards(): lax.all_to_all(blocks, ('dp', 'z', 'y'), split_axis=0, concat_axis=0, til...]
    reshape x2 -> x0, local copies, waits for them, and re-layouts: 3 us -> none  [the longest x1 1.68 us: shards(): w_tout.reshape(8, 36, 288)]
  transfers between devices with their start and end apart: 16 -> 12, of which waited for: 8 -> 9; matrix products, arithmetic and copies ran while one was open for 1% -> 0% of each run, Pallas kernels for 21% -> 19%
where the time goes in v5:
time: 233 us; the launch traced here: 232 us
  waiting for transfers between devices  106 us (45%)
  starting transfers between devices  56.9 us (24%)
  Pallas kernels  51.1 us (22%)
  between operations  14.2 us (6%)
  local copies, waits for them, and re-layouts  3.84 us (2%)
    all_gather x1, waiting for transfers between devices, shards(): lax.all_gather(eighth, ('dp', 'y', 'c'), axis=0, tiled=True)  73.7 us
    pallas_call x1, Pallas kernels, attend(): pl.pallas_call(functools.partial(attend_kernel, step=step), out_shape=jax...  23.5 us
    all_to_all x1, starting transfers between devices, shards(): lax.all_to_all(blocks, ('dp', 'z', 'y'), split_axis=0, concat_axis=0, til...  15.5 us
    all_gather x1, waiting for transfers between devices, shards(): lax.all_gather(grad_out, 'tm', axis=1, tiled=True).reshape(4, LANES, 1152)  10.7 us
    ppermute x3, waiting for transfers between devices, shards(): lax.ppermute(backs[shift], 'tm', RING_BACK[shift - 1])  10.5 us
    all_to_all x1, starting transfers between devices, shards(): lax.all_to_all(packed, space, split_axis=0, concat_axis=0, tiled=True)  10.5 us
    ppermute x3, starting transfers between devices, shards(): lax.ppermute(sends[shift], 'tm', RING[shift - 1])  10.2 us
    ppermute x3, starting transfers between devices, shards(): lax.ppermute(backs[shift], 'tm', RING_BACK[shift - 1])  9.48 us
  transfers between devices with their start and end apart: 12, of which 9 were waited for; matrix products, arithmetic and copies ran while one was open for 0% of the time, Pallas kernels for 19%

profile of v5, /device:TPU:1, one launch (start us, length us, event | category | flops | bytes accessed | tf_op | source)
XLA Modules:
  0.0 232.5 jit_solution(5664020439316970235)
XLA Ops:
  7.2 2.6 %spatial_pack.1 = bf16[32,2,72,128]{3,2,1,0:T(8,128)(2,1)} custom-call(bf16[2,64,1152]{2,1,0:T(8,128)(2,1)} %bitcast.22, bf16[2,64,1152]{2,1,0:T(8,128)(2,1)} %bitcast.23, bf16[2,64,1152]{2,1,0:T(8,128)(2,1)} %bitcast.24, bf16[2,64,1152]{2,1,0:T(8,128)(2,1)} %bitcast.25), custom_call_target="tpu_custom_call" | custom-call | flops 1000 | bytes 1000 | tf_op jit(solution)/shard_map/spatial_pack/pallas_call | solution.py:45
  9.8 10.5 %all-to-all-start = ((bf16[32,2,72,128]{3,2,1,0:T(8,128)(2,1)}), bf16[32,2,72,128]{3,2,1,0:T(8,128)(2,1)S(1)}, u32[]{:S(2)}, u32[]{:S(2)}) async-start(bf16[32,2,72,128]{3,2,1,0:T(8,128)(2,1)} %spatial_pack.1), calls=%async_computation | async-start | bytes 2359296 | tf_op jit(solution)/shard_map/all_to_all | solution.py:551
  20.3 0.0 all-gather.3.cloned.1.call-start
  20.3 0.7 all-gather.3.cloned.1.call-update
  21.0 0.6 pad_add_fusion.me_ref
  21.6 2.5 %temporal_pack.1 = (bf16[288,384]{1,0:T(8,128)(2,1)}, bf16[288,384]{1,0:T(8,128)(2,1)}, bf16[288,384]{1,0:T(8,128)(2,1)}, bf16[288,384]{1,0:T(8,128)(2,1)}) custom-call(s32[3]{0:T(128)} %pad_add_fusion.me_ref, bf16[2,64,1152]{2,1,0:T(8,128)(2,1)} %bitcast.26, bf16[2,64,1152]{2,1,0:T(8,128)(2,1)} %bitcast.27, bf16[2,64,1152]{2,1,0:T(8,128)(2,1)} %bitcast.28), custom_call_target="tpu_custom_call" | custom-call | flops 1000 | bytes 1000 | tf_op jit(solution)/shard_map/temporal_pack/pallas_call | solution.py:237
  24.2 2.8 %collective-permute-start = (bf16[288,384]{1,0:T(8,128)(2,1)}, bf16[288,384]{1,0:T(8,128)(2,1)S(1)}, u32[]{:S(2)}, u32[]{:S(2)}) collective-permute-start(bf16[288,384]{1,0:T(8,128)(2,1)} %get-tuple-element.41), channel_id=1, source_target_pairs={{0,32},{32,64},{64,96},{96,0},{1,33},{33,65},{65,97},{97,1},{2,34}... | collective-permute-start | bytes 663560 | tf_op jit(solution)/shard_map/ppermute | solution.py:555
  27.0 4.4 %collective-permute-start.1 = (bf16[288,384]{1,0:T(8,128)(2,1)}, bf16[288,384]{1,0:T(8,128)(2,1)S(1)}, u32[]{:S(2)}, u32[]{:S(2)}) collective-permute-start(bf16[288,384]{1,0:T(8,128)(2,1)} %get-tuple-element.42), channel_id=1, source_target_pairs={{0,64},{32,96},{64,0},{96,32},{1,65},{33,97},{65,1},{97,33},{2,66}... | collective-permute-start | bytes 663560 | tf_op jit(solution)/shard_map/ppermute | solution.py:555
  31.4 3.1 %collective-permute-start.2 = (bf16[288,384]{1,0:T(8,128)(2,1)}, bf16[288,384]{1,0:T(8,128)(2,1)S(1)}, u32[]{:S(2)}, u32[]{:S(2)}) collective-permute-start(bf16[288,384]{1,0:T(8,128)(2,1)} %get-tuple-element.43), channel_id=1, source_target_pairs={{0,96},{32,0},{64,32},{96,64},{1,97},{33,1},{65,33},{97,65},{2,98}... | collective-permute-start | bytes 663560 | tf_op jit(solution)/shard_map/ppermute | solution.py:555
  34.5 0.0 collective-permute-done.in1
  34.5 0.0 copy-start.3
  34.5 5.2 %collective-permute-done.1.in2 = bf16[288,384]{1,0:T(8,128)(2,1)S(1)} collective-permute-done((bf16[288,384]{1,0:T(8,128)(2,1)}, bf16[288,384]{1,0:T(8,128)(2,1)S(1)}, u32[]{:S(2)}, u32[]{:S(2)}) %collective-permute-start.1) | collective-permute-done | bytes 221216 | tf_op jit(solution)/shard_map/ppermute | solution.py:555
  39.7 0.0 copy-start.4
  39.7 1.3 collective-permute-done.2.in3
  41.1 0.0 copy-start.5
  41.1 0.0 copy-done.3
  41.1 0.0 copy-done.4
  41.1 0.7 copy-done.5
  41.8 3.1 %temporal_tout.1.tout_ref = bf16[4,288,128]{2,1,0:T(8,128)(2,1)} custom-call(s32[3]{0:T(128)} %pad_add_fusion.me_ref, bf16[288,384]{1,0:T(8,128)(2,1)} %get-tuple-element.52.in0, bf16[288,384]{1,0:T(8,128)(2,1)} %copy-done.3, bf16[288,384]{1,0:T(8,128)(2,1)} %copy-done.4, bf16[288,384]{1,0:T(8,128)(2,1)} %copy-done.5), custom_call_target="tpu_custom_call" | custom-call | flops 1000 | bytes 1000 | tf_op jit(solution)/shard_map/temporal_tout/pallas_call | solution.py:300
  44.9 10.7 %all-gather.3.cloned.1.call-done = bf16[1,8,64,1152]{3,2,0,1:T(8,128)(2,1)} async-done(((bf16[1,2,64,1152]{3,2,0,1:T(8,128)(2,1)}), bf16[1,8,64,1152]{3,2,0,1:T(8,128)(2,1)}) %all-gather.3.cloned.1.call-update) | async-done | bytes 1179664 | tf_op jit(solution)/shard_map/all_gather | solution.py:546
  55.6 3.2 %weight_partial.1 = (f32[144,1152]{1,0:T(8,128)}, bf16[144,1152]{1,0:T(8,128)(2,1)}, bf16[16,1152]{1,0:T(8,128)(2,1)}) custom-call(s32[3]{0:T(128)} %pad_add_fusion.me_ref, bf16[4,288,128]{2,1,0:T(8,128)(2,1)} %temporal_tout.1.tout_ref, bf16[4,128,1152]{2,1,0:T(8,128)(2,1)} %bitcast.19, bf16[288,288]{1,0:T(8,128)(2,1)} %w_ref.1), custom_call_target="tpu_custom_call" | custom-call | tf_op jit(solution)/shard_map/weight_partial/pallas_call | solution.py:342
  58.8 3.5 %collective-permute-start.3 = (bf16[144,1152]{1,0:T(8,128)(2,1)}, bf16[144,1152]{1,0:T(8,128)(2,1)S(1)}, u32[]{:S(2)}, u32[]{:S(2)}) collective-permute-start(bf16[144,1152]{1,0:T(8,128)(2,1)} %get-tuple-element.45), channel_id=1, source_target_pairs={{0,1},{1,0},{2,3},{3,2},{4,5},{5,4},{6,7},{7,6},{8,9},{9,8},{10,11... | collective-permute-start | bytes 995336 | tf_op jit(solution)/shard_map/ppermute | solution.py:560
  62.4 1.4 collective-permute-done.3.got_ref
  63.8 0.0 copy-start.6
  63.8 0.7 copy-done.6
  64.5 2.4 %weight_split.1 = bf16[64,24,128]{2,1,0:T(8,128)(2,1)} custom-call(f32[144,1152]{1,0:T(8,128)} %get-tuple-element.44.keep_ref, bf16[144,1152]{1,0:T(8,128)(2,1)} %copy-done.6), custom_call_target="tpu_custom_call" | custom-call | tf_op jit(solution)/shard_map/weight_split/pallas_call | solution.py:384
  66.9 0.0 all-to-all-done.in_ref
  66.9 0.0 copy-start.2
  66.9 15.5 %all-to-all-start.1 = ((bf16[64,24,128]{2,1,0:T(8,128)(2,1)}), bf16[64,24,128]{2,1,0:T(8,128)(2,1)S(1)}, u32[]{:S(2)}, u32[]{:S(2)}) async-start(bf16[64,24,128]{2,1,0:T(8,128)(2,1)} %weight_split.1), calls=%async_computation.1 | async-start | bytes 786432 | tf_op jit(solution)/shard_map/all_to_all | solution.py:563
  82.4 0.0 copy-done.2
  82.5 23.5 %spatial_attention.1.spatial_ref = bf16[32,112,128]{2,1,0:T(8,128)(2,1)} custom-call(bf16[32,2,72,128]{3,2,1,0:T(8,128)(2,1)} %copy-done.2), custom_call_target="tpu_custom_call" | custom-call | flops 10737418240 | bytes 2200000 | tf_op jit(solution)/shard_map/spatial_attention/pallas_call | solution.py:147
  105.9 1.4 all-to-all-done.1.in_ref
  107.4 0.0 copy-start.1
  107.4 0.7 copy-done.1
  108.1 2.4 %weight_join.1 = bf16[32,136,128]{2,1,0:T(8,128)(2,1)} custom-call(bf16[32,112,128]{2,1,0:T(8,128)(2,1)} %spatial_attention.1.spatial_ref, bf16[64,24,128]{2,1,0:T(8,128)(2,1)} %copy-done.1), custom_call_target="tpu_custom_call" | custom-call | tf_op jit(solution)/shard_map/weight_join/pallas_call | solution.py:414
  110.5 7.6 %all-to-all-start.2 = ((bf16[32,136,128]{2,1,0:T(8,128)(2,1)}), bf16[32,136,128]{2,1,0:T(8,128)(2,1)S(1)}, u32[]{:S(2)}, u32[]{:S(2)}) async-start(bf16[32,136,128]{2,1,0:T(8,128)(2,1)} %weight_join.1), calls=%async_computation.2 | async-start | bytes 2228224 | tf_op jit(solution)/shard_map/all_to_all | solution.py:566
  118.0 0.0 all-gather.5.cloned.1.call-start
  118.1 0.7 all-gather.5.cloned.1.call-update
  118.8 73.7 %all-gather.5.cloned.1.call-done = bf16[512,1152]{1,0:T(8,128)(2,1)} async-done(((bf16[16,1152]{1,0:T(8,128)(2,1)}), bf16[512,1152]{1,0:T(8,128)(2,1)}) %all-gather.5.cloned.1.call-update) | async-done | bytes 1179664 | tf_op jit(solution)/shard_map/all_gather | solution.py:559
  192.5 6.2 %temporal_back.1 = (bf16[288,384]{1,0:T(8,128)(2,1)}, bf16[288,384]{1,0:T(8,128)(2,1)}, bf16[288,384]{1,0:T(8,128)(2,1)}, bf16[288,384]{1,0:T(8,128)(2,1)}) custom-call(s32[3]{0:T(128)} %pad_add_fusion.me_ref, bf16[288,384]{1,0:T(8,128)(2,1)} %get-tuple-element.52.in0, bf16[288,384]{1,0:T(8,128)(2,1)} %copy-done.3, bf16[288,384]{1,0:T(8,128)(2,1)} %copy-done.4, ...), custom_call_target="tpu_custom_call" | custom-call | tf_op jit(solution)/shard_map/temporal_back/pallas_call | solution.py:487
  198.7 4.3 %collective-permute-start.4 = (bf16[288,384]{1,0:T(8,128)(2,1)}, bf16[288,384]{1,0:T(8,128)(2,1)S(1)}, u32[]{:S(2)}, u32[]{:S(2)}) collective-permute-start(bf16[288,384]{1,0:T(8,128)(2,1)} %get-tuple-element.58), channel_id=1, source_target_pairs={{0,96},{32,0},{64,32},{96,64},{1,97},{33,1},{65,33},{97,65},{2,98}... | collective-permute-start | bytes 663560 | tf_op jit(solution)/shard_map/ppermute | solution.py:570
  203.0 2.7 %collective-permute-start.5 = (bf16[288,384]{1,0:T(8,128)(2,1)}, bf16[288,384]{1,0:T(8,128)(2,1)S(1)}, u32[]{:S(2)}, u32[]{:S(2)}) collective-permute-start(bf16[288,384]{1,0:T(8,128)(2,1)} %get-tuple-element.59), channel_id=1, source_target_pairs={{0,64},{32,96},{64,0},{96,32},{1,65},{33,97},{65,1},{97,33},{2,66}... | collective-permute-start | bytes 663560 | tf_op jit(solution)/shard_map/ppermute | solution.py:570
  205.7 2.5 %collective-permute-start.6 = (bf16[288,384]{1,0:T(8,128)(2,1)}, bf16[288,384]{1,0:T(8,128)(2,1)S(1)}, u32[]{:S(2)}, u32[]{:S(2)}) collective-permute-start(bf16[288,384]{1,0:T(8,128)(2,1)} %get-tuple-element.60), channel_id=1, source_target_pairs={{0,32},{32,64},{64,96},{96,0},{1,33},{33,65},{65,97},{97,1},{2,34}... | collective-permute-start | bytes 663560 | tf_op jit(solution)/shard_map/ppermute | solution.py:570
  208.2 4.3 %collective-permute-done.4.in1 = bf16[288,384]{1,0:T(8,128)(2,1)S(1)} collective-permute-done((bf16[288,384]{1,0:T(8,128)(2,1)}, bf16[288,384]{1,0:T(8,128)(2,1)S(1)}, u32[]{:S(2)}, u32[]{:S(2)}) %collective-permute-start.4) | collective-permute-done | bytes 221216 | tf_op jit(solution)/shard_map/ppermute | solution.py:570
  212.5 0.0 copy-start.7
  212.5 0.6 collective-permute-done.5.in2
  213.1 0.0 copy-start.8
  213.1 5.6 %collective-permute-done.6.in3 = bf16[288,384]{1,0:T(8,128)(2,1)S(1)} collective-permute-done((bf16[288,384]{1,0:T(8,128)(2,1)}, bf16[288,384]{1,0:T(8,128)(2,1)S(1)}, u32[]{:S(2)}, u32[]{:S(2)}) %collective-permute-start.6) | collective-permute-done | bytes 221216 | tf_op jit(solution)/shard_map/ppermute | solution.py:570
  218.7 0.0 copy-start.9
  218.7 0.0 copy-done.7
  218.7 0.0 copy-done.8
  218.8 0.7 copy-done.9
  219.4 2.5 %temporal_unpack.1 = (bf16[2,64,1152]{2,1,0:T(8,128)(2,1)}, bf16[2,64,1152]{2,1,0:T(8,128)(2,1)}, bf16[2,64,1152]{2,1,0:T(8,128)(2,1)}) custom-call(s32[3]{0:T(128)} %pad_add_fusion.me_ref, bf16[288,384]{1,0:T(8,128)(2,1)} %get-tuple-element.57.in0, bf16[288,384]{1,0:T(8,128)(2,1)} %copy-done.7, bf16[288,384]{1,0:T(8,128)(2,1)} %copy-done.8, ...), custom_call_target="tpu_custom_call" | custom-call | tf_op jit(solution)/shard_map/temporal_unpack/pallas_call | solution.py:516
  221.9 0.0 all-to-all-done.2.in_ref
  221.9 0.0 copy-start
  221.9 1.0 copy-done
  222.9 2.7 %spatial_unpack.1 = (bf16[2,64,1152]{2,1,0:T(8,128)(2,1)}, bf16[2,64,1152]{2,1,0:T(8,128)(2,1)}, bf16[2,64,1152]{2,1,0:T(8,128)(2,1)}, f32[288,288]{1,0:T(8,128)}) custom-call(bf16[32,136,128]{2,1,0:T(8,128)(2,1)} %copy-done), custom_call_target="tpu_custom_call" | custom-call | tf_op jit(solution)/shard_map/spatial_unpack/pallas_call | solution.py:200
Async XLA Ops:
  9.8 57.1 %all-to-all-start = ((bf16[32,2,72,128]{3,2,1,0:T(8,128)(2,1)}), bf16[32,2,72,128]{3,2,1,0:T(8,128)(2,1)S(1)}, u32[]{:S(2)}, u32[]{:S(2)}) async-start(bf16[32,2,72,128]{3,2,1,0:T(8,128)(2,1)} %spatial_pack.1), calls=%async_computation | async-start | bytes 2359296 | tf_op jit(solution)/shard_map/all_to_all | solution.py:551
  20.3 35.3 %all-gather.3.cloned.1.call-start = ((), (), s32[]{:S(2)}) async-start(), calls=%async_computation.3 | async-start | bytes 1474560 | tf_op jit(solution)/shard_map/all_gather | solution.py:546
  24.2 10.3 %collective-permute-start = (bf16[288,384]{1,0:T(8,128)(2,1)}, bf16[288,384]{1,0:T(8,128)(2,1)S(1)}, u32[]{:S(2)}, u32[]{:S(2)}) collective-permute-start(bf16[288,384]{1,0:T(8,128)(2,1)} %get-tuple-element.41), channel_id=1, source_target_pairs={{0,32},{32,64},{64,96},{96,0},{1,33},{33,65},{65,97},{97,1},{2,34}... | collective-permute-start | bytes 663560 | tf_op jit(solution)/shard_map/ppermute | solution.py:555
  27.0 12.7 %collective-permute-start.1 = (bf16[288,384]{1,0:T(8,128)(2,1)}, bf16[288,384]{1,0:T(8,128)(2,1)S(1)}, u32[]{:S(2)}, u32[]{:S(2)}) collective-permute-start(bf16[288,384]{1,0:T(8,128)(2,1)} %get-tuple-element.42), channel_id=1, source_target_pairs={{0,64},{32,96},{64,0},{96,32},{1,65},{33,97},{65,1},{97,33},{2,66}... | collective-permute-start | bytes 663560 | tf_op jit(solution)/shard_map/ppermute | solution.py:555
  31.4 9.7 %collective-permute-start.2 = (bf16[288,384]{1,0:T(8,128)(2,1)}, bf16[288,384]{1,0:T(8,128)(2,1)S(1)}, u32[]{:S(2)}, u32[]{:S(2)}) collective-permute-start(bf16[288,384]{1,0:T(8,128)(2,1)} %get-tuple-element.43), channel_id=1, source_target_pairs={{0,96},{32,0},{64,32},{96,64},{1,97},{33,1},{65,33},{97,65},{2,98}... | collective-permute-start | bytes 663560 | tf_op jit(solution)/shard_map/ppermute | solution.py:555
  34.5 6.6 %copy-start.3 = (bf16[288,384]{1,0:T(8,128)(2,1)}, bf16[288,384]{1,0:T(8,128)(2,1)S(1)}, u32[]{:S(2)}) copy-start(bf16[288,384]{1,0:T(8,128)(2,1)S(1)} %collective-permute-done.in1) | copy-start | bytes 663556
  39.7 1.3 copy-start.4
  41.1 0.7 copy-start.5
  58.8 5.0 %collective-permute-start.3 = (bf16[144,1152]{1,0:T(8,128)(2,1)}, bf16[144,1152]{1,0:T(8,128)(2,1)S(1)}, u32[]{:S(2)}, u32[]{:S(2)}) collective-permute-start(bf16[144,1152]{1,0:T(8,128)(2,1)} %get-tuple-element.45), channel_id=1, source_target_pairs={{0,1},{1,0},{2,3},{3,2},{4,5},{5,4},{6,7},{7,6},{8,9},{9,8},{10,11... | collective-permute-start | bytes 995336 | tf_op jit(solution)/shard_map/ppermute | solution.py:560
  63.8 0.7 copy-start.6
  66.9 15.6 %copy-start.2 = (bf16[32,2,72,128]{3,2,1,0:T(8,128)(2,1)}, bf16[32,2,72,128]{3,2,1,0:T(8,128)(2,1)S(1)}, u32[]{:S(2)}) copy-start(bf16[32,2,72,128]{3,2,1,0:T(8,128)(2,1)S(1)} %all-to-all-done.in_ref) | copy-start | bytes 3538948
  66.9 40.5 %all-to-all-start.1 = ((bf16[64,24,128]{2,1,0:T(8,128)(2,1)}), bf16[64,24,128]{2,1,0:T(8,128)(2,1)S(1)}, u32[]{:S(2)}, u32[]{:S(2)}) async-start(bf16[64,24,128]{2,1,0:T(8,128)(2,1)} %weight_split.1), calls=%async_computation.1 | async-start | bytes 786432 | tf_op jit(solution)/shard_map/all_to_all | solution.py:563
  107.4 0.7 copy-start.1
  110.5 111.4 %all-to-all-start.2 = ((bf16[32,136,128]{2,1,0:T(8,128)(2,1)}), bf16[32,136,128]{2,1,0:T(8,128)(2,1)S(1)}, u32[]{:S(2)}, u32[]{:S(2)}) async-start(bf16[32,136,128]{2,1,0:T(8,128)(2,1)} %weight_join.1), calls=%async_computation.2 | async-start | bytes 2228224 | tf_op jit(solution)/shard_map/all_to_all | solution.py:566
  118.0 74.5 %all-gather.5.cloned.1.call-start = ((), (), s32[]{:S(2)}) async-start(), calls=%async_computation.4 | async-start | bytes 1216512 | tf_op jit(solution)/shard_map/all_gather | solution.py:559
  198.7 13.8 %collective-permute-start.4 = (bf16[288,384]{1,0:T(8,128)(2,1)}, bf16[288,384]{1,0:T(8,128)(2,1)S(1)}, u32[]{:S(2)}, u32[]{:S(2)}) collective-permute-start(bf16[288,384]{1,0:T(8,128)(2,1)} %get-tuple-element.58), channel_id=1, source_target_pairs={{0,96},{32,0},{64,32},{96,64},{1,97},{33,1},{65,33},{97,65},{2,98}... | collective-permute-start | bytes 663560 | tf_op jit(solution)/shard_map/ppermute | solution.py:570
  203.0 10.1 %collective-permute-start.5 = (bf16[288,384]{1,0:T(8,128)(2,1)}, bf16[288,384]{1,0:T(8,128)(2,1)S(1)}, u32[]{:S(2)}, u32[]{:S(2)}) collective-permute-start(bf16[288,384]{1,0:T(8,128)(2,1)} %get-tuple-element.59), channel_id=1, source_target_pairs={{0,64},{32,96},{64,0},{96,32},{1,65},{33,97},{65,1},{97,33},{2,66}... | collective-permute-start | bytes 663560 | tf_op jit(solution)/shard_map/ppermute | solution.py:570
  205.7 13.0 %collective-permute-start.6 = (bf16[288,384]{1,0:T(8,128)(2,1)}, bf16[288,384]{1,0:T(8,128)(2,1)S(1)}, u32[]{:S(2)}, u32[]{:S(2)}) collective-permute-start(bf16[288,384]{1,0:T(8,128)(2,1)} %get-tuple-element.60), channel_id=1, source_target_pairs={{0,32},{32,64},{64,96},{96,0},{1,33},{33,65},{65,97},{97,1},{2,34}... | collective-permute-start | bytes 663560 | tf_op jit(solution)/shard_map/ppermute | solution.py:570
  212.5 6.2 %copy-start.7 = (bf16[288,384]{1,0:T(8,128)(2,1)}, bf16[288,384]{1,0:T(8,128)(2,1)S(1)}, u32[]{:S(2)}) copy-start(bf16[288,384]{1,0:T(8,128)(2,1)S(1)} %collective-permute-done.4.in1) | copy-start | bytes 663556
  213.1 5.6 %copy-start.8 = (bf16[288,384]{1,0:T(8,128)(2,1)}, bf16[288,384]{1,0:T(8,128)(2,1)S(1)}, u32[]{:S(2)}) copy-start(bf16[288,384]{1,0:T(8,128)(2,1)S(1)} %collective-permute-done.5.in2) | copy-start | bytes 663556
  218.7 0.7 copy-start.9
  221.9 1.0 copy-start
Sparse Core Ops, SparseCore 0:
  23.2 32.3 all-gather.2
  122.7 69.8 all-gather.4

commit v6 on v5

--- a/solution.py
+++ b/solution.py
@@ -16,6 +16,7 @@
 BF16 = jnp.bfloat16
 LIMIT = 56 * 1024 * 1024
 SMALL = pl.CostEstimate(flops=1000, bytes_accessed=1000, transcendentals=0)
+LARGE = pl.CostEstimate(flops=10**12, bytes_accessed=10**8, transcendentals=0)
 
 
 def vmem_specs(count):
@@ -241,7 +242,7 @@
         out_specs=tuple(vmem_specs(4)),
         scratch_shapes=[pltpu.VMEM((4, 288, 3 * LANES), BF16)],
         compiler_params=pltpu.CompilerParams(vmem_limit_bytes=LIMIT),
-        cost_estimate=SMALL,
+        cost_estimate=LARGE,
         name="temporal_pack",
     )(me, q, k, v)
 
@@ -354,6 +355,7 @@
             pltpu.VMEM((288, 288), F32),
         ],
         compiler_params=pltpu.CompilerParams(vmem_limit_bytes=LIMIT),
+        cost_estimate=SMALL,
         name="weight_partial",
     )(me, tout, grads, w)
 
@@ -388,6 +390,7 @@
         out_specs=pl.BlockSpec(memory_space=pltpu.VMEM),
         scratch_shapes=[pltpu.VMEM((144, 1152), F32), pltpu.VMEM((144, 3 * LANES), F32)],
         compiler_params=pltpu.CompilerParams(vmem_limit_bytes=LIMIT),
+        cost_estimate=SMALL,
         name="weight_split",
     )(keep, got)
 
@@ -417,6 +420,7 @@
         in_specs=vmem_specs(2),
         out_specs=pl.BlockSpec(memory_space=pltpu.VMEM),
         compiler_params=pltpu.CompilerParams(vmem_limit_bytes=LIMIT),
+        cost_estimate=SMALL,
         name="weight_join",
     )(spatial, received)
 
@@ -495,6 +499,7 @@
             pltpu.VMEM((1152, 288), F32),
         ],
         compiler_params=pltpu.CompilerParams(vmem_limit_bytes=LIMIT),
+        cost_estimate=LARGE,
         name="temporal_back",
     )(me, *pieces, grads, w)
 

time: 233 us -> 177 us (0.76)
  waiting for transfers between devices: 106 us -> 52.1 us
    all_gather x1, waiting for transfers between devices: 73.7 us -> 19.3 us  [shards(): lax.all_gather(eighth, ('dp', 'y', 'c'), axis=0, tiled=True)]
    all_gather x1, waiting for transfers between devices: 10.7 us -> 2.4 us  [shards(): lax.all_gather(grad_out, 'tm', axis=1, tiled=True).reshape(4, LANES, 1152)]
    ppermute x3, waiting for transfers between devices: 6.59 us -> 12.6 us  [shards(): lax.ppermute(sends[shift], 'tm', RING[shift - 1])]
    all_to_all x1, waiting for transfers between devices: 1.44 us -> 5.02 us  [shards(): lax.all_to_all(blocks, ('dp', 'z', 'y'), split_axis=0, concat_axis=0, til...]
  transfers between devices with their start and end apart: 12 -> 12, of which waited for: 9 -> 10; matrix products, arithmetic and copies ran while one was open for 0% -> 0% of each run, Pallas kernels for 19% -> 27%
where the time goes in v6:
time: 177 us; the launch traced here: 176 us
  starting transfers between devices  55.4 us (31%)
  waiting for transfers between devices  52.1 us (29%)
  Pallas kernels  51.1 us (29%)
  between operations  14.1 us (8%)
  local copies, waits for them, and re-layouts  2.86 us (2%)
    pallas_call x1, Pallas kernels, attend(): pl.pallas_call(functools.partial(attend_kernel, step=step), out_shape=jax...  23.5 us
    all_gather x1, waiting for transfers between devices, shards(): lax.all_gather(eighth, ('dp', 'y', 'c'), axis=0, tiled=True)  19.3 us
    all_to_all x1, starting transfers between devices, shards(): lax.all_to_all(blocks, ('dp', 'z', 'y'), split_axis=0, concat_axis=0, til...  15.4 us
    ppermute x3, waiting for transfers between devices, shards(): lax.ppermute(sends[shift], 'tm', RING[shift - 1])  12.6 us
    all_to_all x1, starting transfers between devices, shards(): lax.all_to_all(packed, space, split_axis=0, concat_axis=0, tiled=True)  11.1 us
    ppermute x3, waiting for transfers between devices, shards(): lax.ppermute(backs[shift], 'tm', RING_BACK[shift - 1])  10.6 us
    ppermute x3, starting transfers between devices, shards(): lax.ppermute(backs[shift], 'tm', RING_BACK[shift - 1])  9.79 us
    ppermute x3, starting transfers between devices, shards(): lax.ppermute(sends[shift], 'tm', RING[shift - 1])  9.64 us
  transfers between devices with their start and end apart: 12, of which 10 were waited for; matrix products, arithmetic and copies ran while one was open for 0% of the time, Pallas kernels for 27%

profile of v6, /device:TPU:1, one launch (start us, length us, event | category | flops | bytes accessed | tf_op | source)
XLA Modules:
  0.0 176.2 jit_solution(11566743611934253202)
XLA Ops:
  7.2 0.0 all-gather.3.cloned.1.call-start
  7.2 0.7 all-gather.3.cloned.1.call-update
  7.9 2.6 %spatial_pack.1 = bf16[32,2,72,128]{3,2,1,0:T(8,128)(2,1)} custom-call(bf16[2,64,1152]{2,1,0:T(8,128)(2,1)} %bitcast.21, bf16[2,64,1152]{2,1,0:T(8,128)(2,1)} %bitcast.22, bf16[2,64,1152]{2,1,0:T(8,128)(2,1)} %bitcast.23, bf16[2,64,1152]{2,1,0:T(8,128)(2,1)} %bitcast.24), custom_call_target="tpu_custom_call" | custom-call | flops 1000 | bytes 1000 | tf_op jit(solution)/shard_map/spatial_pack/pallas_call | solution.py:46
  10.5 11.1 %all-to-all-start = ((bf16[32,2,72,128]{3,2,1,0:T(8,128)(2,1)}), bf16[32,2,72,128]{3,2,1,0:T(8,128)(2,1)}, u32[]{:S(2)}, u32[]{:S(2)}) async-start(bf16[32,2,72,128]{3,2,1,0:T(8,128)(2,1)} %spatial_pack.1), calls=%async_computation | async-start | bytes 2359296 | tf_op jit(solution)/shard_map/all_to_all | solution.py:556
  21.7 0.0 all-gather.5.cloned.1.call-start
  21.7 0.6 pad_add_fusion.me_ref
  22.3 2.5 %temporal_pack.1 = (bf16[288,384]{1,0:T(8,128)(2,1)}, bf16[288,384]{1,0:T(8,128)(2,1)}, bf16[288,384]{1,0:T(8,128)(2,1)}, bf16[288,384]{1,0:T(8,128)(2,1)}) custom-call(s32[3]{0:T(128)} %pad_add_fusion.me_ref, bf16[2,64,1152]{2,1,0:T(8,128)(2,1)} %bitcast.27, bf16[2,64,1152]{2,1,0:T(8,128)(2,1)} %bitcast.28, bf16[2,64,1152]{2,1,0:T(8,128)(2,1)} %bitcast.29), custom_call_target="tpu_custom_call" | custom-call | flops 999999995904 | bytes 100000000 | tf_op jit(solution)/shard_map/temporal_pack/pallas_call | solution.py:238
  24.9 2.2 %collective-permute-start = (bf16[288,384]{1,0:T(8,128)(2,1)}, bf16[288,384]{1,0:T(8,128)(2,1)S(1)}, u32[]{:S(2)}, u32[]{:S(2)}) collective-permute-start(bf16[288,384]{1,0:T(8,128)(2,1)} %get-tuple-element.41), channel_id=1, source_target_pairs={{0,32},{32,64},{64,96},{96,0},{1,33},{33,65},{65,97},{97,1},{2,34}... | collective-permute-start | bytes 663560 | tf_op jit(solution)/shard_map/ppermute | solution.py:560
  27.1 4.4 %collective-permute-start.1 = (bf16[288,384]{1,0:T(8,128)(2,1)}, bf16[288,384]{1,0:T(8,128)(2,1)S(1)}, u32[]{:S(2)}, u32[]{:S(2)}) collective-permute-start(bf16[288,384]{1,0:T(8,128)(2,1)} %get-tuple-element.42), channel_id=1, source_target_pairs={{0,64},{32,96},{64,0},{96,32},{1,65},{33,97},{65,1},{97,33},{2,66}... | collective-permute-start | bytes 663560 | tf_op jit(solution)/shard_map/ppermute | solution.py:560
  31.5 3.1 %collective-permute-start.2 = (bf16[288,384]{1,0:T(8,128)(2,1)}, bf16[288,384]{1,0:T(8,128)(2,1)S(1)}, u32[]{:S(2)}, u32[]{:S(2)}) collective-permute-start(bf16[288,384]{1,0:T(8,128)(2,1)} %get-tuple-element.43), channel_id=1, source_target_pairs={{0,96},{32,0},{64,32},{96,64},{1,97},{33,1},{65,33},{97,65},{2,98}... | collective-permute-start | bytes 663560 | tf_op jit(solution)/shard_map/ppermute | solution.py:560
  34.5 0.3 collective-permute-done.in1
  34.9 0.0 copy-start.5
  34.9 7.5 %collective-permute-done.1.in2 = bf16[288,384]{1,0:T(8,128)(2,1)S(1)} collective-permute-done((bf16[288,384]{1,0:T(8,128)(2,1)}, bf16[288,384]{1,0:T(8,128)(2,1)S(1)}, u32[]{:S(2)}, u32[]{:S(2)}) %collective-permute-start.1) | collective-permute-done | bytes 221216 | tf_op jit(solution)/shard_map/ppermute | solution.py:560
  42.4 0.0 copy-start.6
  42.4 4.7 %collective-permute-done.2.in3 = bf16[288,384]{1,0:T(8,128)(2,1)S(1)} collective-permute-done((bf16[288,384]{1,0:T(8,128)(2,1)}, bf16[288,384]{1,0:T(8,128)(2,1)S(1)}, u32[]{:S(2)}, u32[]{:S(2)}) %collective-permute-start.2) | collective-permute-done | bytes 221216 | tf_op jit(solution)/shard_map/ppermute | solution.py:560
  47.1 0.0 copy-start.7
  47.1 0.0 copy-done.5
  47.1 0.0 copy-done.6
  47.1 0.7 copy-done.7
  47.8 3.1 %temporal_tout.1.tout_ref = bf16[4,288,128]{2,1,0:T(8,128)(2,1)} custom-call(s32[3]{0:T(128)} %pad_add_fusion.me_ref, bf16[288,384]{1,0:T(8,128)(2,1)} %get-tuple-element.52.in0, bf16[288,384]{1,0:T(8,128)(2,1)} %copy-done.5, bf16[288,384]{1,0:T(8,128)(2,1)} %copy-done.6, bf16[288,384]{1,0:T(8,128)(2,1)} %copy-done.7), custom_call_target="tpu_custom_call" | custom-call | flops 1000 | bytes 1000 | tf_op jit(solution)/shard_map/temporal_tout/pallas_call | solution.py:301
  50.9 2.4 %all-gather.3.cloned.1.call-done = bf16[1,8,64,1152]{3,2,0,1:T(8,128)(2,1)} async-done(((bf16[1,2,64,1152]{3,2,0,1:T(8,128)(2,1)}), bf16[1,8,64,1152]{3,2,0,1:T(8,128)(2,1)}) %all-gather.3.cloned.1.call-update) | async-done | bytes 1179664 | tf_op jit(solution)/shard_map/all_gather | solution.py:551
  53.3 3.3 %weight_partial.1 = (f32[144,1152]{1,0:T(8,128)}, bf16[144,1152]{1,0:T(8,128)(2,1)}, bf16[16,1152]{1,0:T(8,128)(2,1)}) custom-call(s32[3]{0:T(128)} %pad_add_fusion.me_ref, bf16[4,288,128]{2,1,0:T(8,128)(2,1)} %temporal_tout.1.tout_ref, bf16[4,128,1152]{2,1,0:T(8,128)(2,1)} %bitcast.19, bf16[288,288]{1,0:T(8,128)(2,1)} %w_ref.1), custom_call_target="tpu_custom_call" | custom-call | flops 1000 | bytes 1000 | tf_op jit(solution)/shard_map/weight_partial/pallas_call | solution.py:343
  56.6 0.0 all-gather.5.cloned.1.call-update
  56.6 2.9 %collective-permute-start.3 = (bf16[144,1152]{1,0:T(8,128)(2,1)}, bf16[144,1152]{1,0:T(8,128)(2,1)S(1)}, u32[]{:S(2)}, u32[]{:S(2)}) collective-permute-start(bf16[144,1152]{1,0:T(8,128)(2,1)} %get-tuple-element.45), channel_id=1, source_target_pairs={{0,1},{1,0},{2,3},{3,2},{4,5},{5,4},{6,7},{7,6},{8,9},{9,8},{10,11... | collective-permute-start | bytes 995336 | tf_op jit(solution)/shard_map/ppermute | solution.py:565
  59.5 1.4 collective-permute-done.3.got_ref
  61.0 0.0 copy-start.1
  61.0 0.7 copy-done.1
  61.7 2.4 %weight_split.1 = bf16[64,24,128]{2,1,0:T(8,128)(2,1)} custom-call(f32[144,1152]{1,0:T(8,128)} %get-tuple-element.44.keep_ref, bf16[144,1152]{1,0:T(8,128)(2,1)} %copy-done.1), custom_call_target="tpu_custom_call" | custom-call | flops 1000 | bytes 1000 | tf_op jit(solution)/shard_map/weight_split/pallas_call | solution.py:386
  64.1 0.0 all-to-all-done.in_ref
  64.1 15.4 %all-to-all-start.1 = ((bf16[64,24,128]{2,1,0:T(8,128)(2,1)}), bf16[64,24,128]{2,1,0:T(8,128)(2,1)S(1)}, u32[]{:S(2)}, u32[]{:S(2)}) async-start(bf16[64,24,128]{2,1,0:T(8,128)(2,1)} %weight_split.1), calls=%async_computation.1 | async-start | bytes 786432 | tf_op jit(solution)/shard_map/all_to_all | solution.py:568
  79.5 23.5 %spatial_attention.1.spatial_ref = bf16[32,112,128]{2,1,0:T(8,128)(2,1)} custom-call(bf16[32,2,72,128]{3,2,1,0:T(8,128)(2,1)} %all-to-all-done.in_ref), custom_call_target="tpu_custom_call" | custom-call | flops 10737418240 | bytes 2200000 | tf_op jit(solution)/shard_map/spatial_attention/pallas_call | solution.py:148
  103.0 5.0 %all-to-all-done.1.in_ref = bf16[64,24,128]{2,1,0:T(8,128)(2,1)S(1)} async-done(((bf16[64,24,128]{2,1,0:T(8,128)(2,1)}), bf16[64,24,128]{2,1,0:T(8,128)(2,1)S(1)}, u32[]{:S(2)}, u32[]{:S(2)}) %all-to-all-start.1) | async-done | bytes 393248 | tf_op jit(solution)/shard_map/all_to_all | solution.py:568
  108.0 0.0 copy-start
  108.0 0.7 copy-done
  108.7 2.4 %weight_join.1 = bf16[32,136,128]{2,1,0:T(8,128)(2,1)} custom-call(bf16[32,112,128]{2,1,0:T(8,128)(2,1)} %spatial_attention.1.spatial_ref, bf16[64,24,128]{2,1,0:T(8,128)(2,1)} %copy-done), custom_call_target="tpu_custom_call" | custom-call | flops 1000 | bytes 1000 | tf_op jit(solution)/shard_map/weight_join/pallas_call | solution.py:417
  111.1 6.4 %all-to-all-start.2 = ((bf16[32,136,128]{2,1,0:T(8,128)(2,1)}), bf16[32,136,128]{2,1,0:T(8,128)(2,1)}, u32[]{:S(2)}, u32[]{:S(2)}) async-start(bf16[32,136,128]{2,1,0:T(8,128)(2,1)} %weight_join.1), calls=%async_computation.2 | async-start | bytes 2228224 | tf_op jit(solution)/shard_map/all_to_all | solution.py:571
  117.5 19.3 %all-gather.5.cloned.1.call-done = bf16[512,1152]{1,0:T(8,128)(2,1)} async-done(((bf16[16,1152]{1,0:T(8,128)(2,1)}), bf16[512,1152]{1,0:T(8,128)(2,1)}) %all-gather.5.cloned.1.call-update) | async-done | bytes 1179664 | tf_op jit(solution)/shard_map/all_gather | solution.py:564
  136.9 6.2 %temporal_back.1 = (bf16[288,384]{1,0:T(8,128)(2,1)}, bf16[288,384]{1,0:T(8,128)(2,1)}, bf16[288,384]{1,0:T(8,128)(2,1)}, bf16[288,384]{1,0:T(8,128)(2,1)}) custom-call(s32[3]{0:T(128)} %pad_add_fusion.me_ref, bf16[288,384]{1,0:T(8,128)(2,1)} %get-tuple-element.52.in0, bf16[288,384]{1,0:T(8,128)(2,1)} %copy-done.5, bf16[288,384]{1,0:T(8,128)(2,1)} %copy-done.6, ...), custom_call_target="tpu_custom_call" | custom-call | flops 999999995904 | bytes 100000000 | tf_op jit(solution)/shard_map/temporal_back/pallas_call | solution.py:491
  143.1 4.7 %collective-permute-start.4 = (bf16[288,384]{1,0:T(8,128)(2,1)}, bf16[288,384]{1,0:T(8,128)(2,1)S(1)}, u32[]{:S(2)}, u32[]{:S(2)}) collective-permute-start(bf16[288,384]{1,0:T(8,128)(2,1)} %get-tuple-element.58), channel_id=1, source_target_pairs={{0,96},{32,0},{64,32},{96,64},{1,97},{33,1},{65,33},{97,65},{2,98}... | collective-permute-start | bytes 663560 | tf_op jit(solution)/shard_map/ppermute | solution.py:575
  147.8 2.3 %collective-permute-start.5 = (bf16[288,384]{1,0:T(8,128)(2,1)}, bf16[288,384]{1,0:T(8,128)(2,1)S(1)}, u32[]{:S(2)}, u32[]{:S(2)}) collective-permute-start(bf16[288,384]{1,0:T(8,128)(2,1)} %get-tuple-element.59), channel_id=1, source_target_pairs={{0,64},{32,96},{64,0},{96,32},{1,65},{33,97},{65,1},{97,33},{2,66}... | collective-permute-start | bytes 663560 | tf_op jit(solution)/shard_map/ppermute | solution.py:575
  150.1 2.8 %collective-permute-start.6 = (bf16[288,384]{1,0:T(8,128)(2,1)}, bf16[288,384]{1,0:T(8,128)(2,1)S(1)}, u32[]{:S(2)}, u32[]{:S(2)}) collective-permute-start(bf16[288,384]{1,0:T(8,128)(2,1)} %get-tuple-element.60), channel_id=1, source_target_pairs={{0,32},{32,64},{64,96},{96,0},{1,33},{33,65},{65,97},{97,1},{2,34}... | collective-permute-start | bytes 663560 | tf_op jit(solution)/shard_map/ppermute | solution.py:575
  152.9 4.4 %collective-permute-done.4.in1 = bf16[288,384]{1,0:T(8,128)(2,1)S(1)} collective-permute-done((bf16[288,384]{1,0:T(8,128)(2,1)}, bf16[288,384]{1,0:T(8,128)(2,1)S(1)}, u32[]{:S(2)}, u32[]{:S(2)}) %collective-permute-start.4) | collective-permute-done | bytes 221216 | tf_op jit(solution)/shard_map/ppermute | solution.py:575
  157.2 0.0 copy-start.2
  157.3 0.6 collective-permute-done.5.in2
  157.9 0.0 copy-start.3
  157.9 5.6 %collective-permute-done.6.in3 = bf16[288,384]{1,0:T(8,128)(2,1)S(1)} collective-permute-done((bf16[288,384]{1,0:T(8,128)(2,1)}, bf16[288,384]{1,0:T(8,128)(2,1)S(1)}, u32[]{:S(2)}, u32[]{:S(2)}) %collective-permute-start.6) | collective-permute-done | bytes 221216 | tf_op jit(solution)/shard_map/ppermute | solution.py:575
  163.5 0.0 copy-start.4
  163.5 0.0 copy-done.2
  163.5 0.0 copy-done.3
  163.5 0.7 copy-done.4
  164.2 2.5 %temporal_unpack.1 = (bf16[2,64,1152]{2,1,0:T(8,128)(2,1)}, bf16[2,64,1152]{2,1,0:T(8,128)(2,1)}, bf16[2,64,1152]{2,1,0:T(8,128)(2,1)}) custom-call(s32[3]{0:T(128)} %pad_add_fusion.me_ref, bf16[288,384]{1,0:T(8,128)(2,1)} %get-tuple-element.57.in0, bf16[288,384]{1,0:T(8,128)(2,1)} %copy-done.2, bf16[288,384]{1,0:T(8,128)(2,1)} %copy-done.3, ...), custom_call_target="tpu_custom_call" | custom-call | tf_op jit(solution)/shard_map/temporal_unpack/pallas_call | solution.py:521
  166.6 0.0 all-to-all-done.2.in_ref
  166.6 2.7 %spatial_unpack.1 = (bf16[2,64,1152]{2,1,0:T(8,128)(2,1)}, bf16[2,64,1152]{2,1,0:T(8,128)(2,1)}, bf16[2,64,1152]{2,1,0:T(8,128)(2,1)}, f32[288,288]{1,0:T(8,128)}) custom-call(bf16[32,136,128]{2,1,0:T(8,128)(2,1)} %all-to-all-done.2.in_ref), custom_call_target="tpu_custom_call" | custom-call | tf_op jit(solution)/shard_map/spatial_unpack/pallas_call | solution.py:201
Async XLA Ops:
  7.2 46.1 %all-gather.3.cloned.1.call-start = ((), (), s32[]{:S(2)}) async-start(), calls=%async_computation.3 | async-start | bytes 1474560 | tf_op jit(solution)/shard_map/all_gather | solution.py:551
  10.5 53.6 %all-to-all-start = ((bf16[32,2,72,128]{3,2,1,0:T(8,128)(2,1)}), bf16[32,2,72,128]{3,2,1,0:T(8,128)(2,1)}, u32[]{:S(2)}, u32[]{:S(2)}) async-start(bf16[32,2,72,128]{3,2,1,0:T(8,128)(2,1)} %spatial_pack.1), calls=%async_computation | async-start | bytes 2359296 | tf_op jit(solution)/shard_map/all_to_all | solution.py:556
  21.7 115.2 %all-gather.5.cloned.1.call-start = ((), (), s32[]{:S(2)}) async-start(), calls=%async_computation.4 | async-start | bytes 1216512 | tf_op jit(solution)/shard_map/all_gather | solution.py:564
  24.9 10.0 %collective-permute-start = (bf16[288,384]{1,0:T(8,128)(2,1)}, bf16[288,384]{1,0:T(8,128)(2,1)S(1)}, u32[]{:S(2)}, u32[]{:S(2)}) collective-permute-start(bf16[288,384]{1,0:T(8,128)(2,1)} %get-tuple-element.41), channel_id=1, source_target_pairs={{0,32},{32,64},{64,96},{96,0},{1,33},{33,65},{65,97},{97,1},{2,34}... | collective-permute-start | bytes 663560 | tf_op jit(solution)/shard_map/ppermute | solution.py:560
  27.1 15.3 %collective-permute-start.1 = (bf16[288,384]{1,0:T(8,128)(2,1)}, bf16[288,384]{1,0:T(8,128)(2,1)S(1)}, u32[]{:S(2)}, u32[]{:S(2)}) collective-permute-start(bf16[288,384]{1,0:T(8,128)(2,1)} %get-tuple-element.42), channel_id=1, source_target_pairs={{0,64},{32,96},{64,0},{96,32},{1,65},{33,97},{65,1},{97,33},{2,66}... | collective-permute-start | bytes 663560 | tf_op jit(solution)/shard_map/ppermute | solution.py:560
  31.5 15.6 %collective-permute-start.2 = (bf16[288,384]{1,0:T(8,128)(2,1)}, bf16[288,384]{1,0:T(8,128)(2,1)S(1)}, u32[]{:S(2)}, u32[]{:S(2)}) collective-permute-start(bf16[288,384]{1,0:T(8,128)(2,1)} %get-tuple-element.43), channel_id=1, source_target_pairs={{0,96},{32,0},{64,32},{96,64},{1,97},{33,1},{65,33},{97,65},{2,98}... | collective-permute-start | bytes 663560 | tf_op jit(solution)/shard_map/ppermute | solution.py:560
  34.9 12.2 %copy-start.5 = (bf16[288,384]{1,0:T(8,128)(2,1)}, bf16[288,384]{1,0:T(8,128)(2,1)S(1)}, u32[]{:S(2)}) copy-start(bf16[288,384]{1,0:T(8,128)(2,1)S(1)} %collective-permute-done.in1) | copy-start | bytes 663556
  42.4 4.7 %copy-start.6 = (bf16[288,384]{1,0:T(8,128)(2,1)}, bf16[288,384]{1,0:T(8,128)(2,1)S(1)}, u32[]{:S(2)}) copy-start(bf16[288,384]{1,0:T(8,128)(2,1)S(1)} %collective-permute-done.1.in2) | copy-start | bytes 663556
  47.1 0.7 copy-start.7
  56.6 4.4 %collective-permute-start.3 = (bf16[144,1152]{1,0:T(8,128)(2,1)}, bf16[144,1152]{1,0:T(8,128)(2,1)S(1)}, u32[]{:S(2)}, u32[]{:S(2)}) collective-permute-start(bf16[144,1152]{1,0:T(8,128)(2,1)} %get-tuple-element.45), channel_id=1, source_target_pairs={{0,1},{1,0},{2,3},{3,2},{4,5},{5,4},{6,7},{7,6},{8,9},{9,8},{10,11... | collective-permute-start | bytes 995336 | tf_op jit(solution)/shard_map/ppermute | solution.py:565
  61.0 0.7 copy-start.1
  64.1 43.9 %all-to-all-start.1 = ((bf16[64,24,128]{2,1,0:T(8,128)(2,1)}), bf16[64,24,128]{2,1,0:T(8,128)(2,1)S(1)}, u32[]{:S(2)}, u32[]{:S(2)}) async-start(bf16[64,24,128]{2,1,0:T(8,128)(2,1)} %weight_split.1), calls=%async_computation.1 | async-start | bytes 786432 | tf_op jit(solution)/shard_map/all_to_all | solution.py:568
  108.0 0.7 copy-start
  111.1 55.5 %all-to-all-start.2 = ((bf16[32,136,128]{2,1,0:T(8,128)(2,1)}), bf16[32,136,128]{2,1,0:T(8,128)(2,1)}, u32[]{:S(2)}, u32[]{:S(2)}) async-start(bf16[32,136,128]{2,1,0:T(8,128)(2,1)} %weight_join.1), calls=%async_computation.2 | async-start | bytes 2228224 | tf_op jit(solution)/shard_map/all_to_all | solution.py:571
  143.1 14.2 %collective-permute-start.4 = (bf16[288,384]{1,0:T(8,128)(2,1)}, bf16[288,384]{1,0:T(8,128)(2,1)S(1)}, u32[]{:S(2)}, u32[]{:S(2)}) collective-permute-start(bf16[288,384]{1,0:T(8,128)(2,1)} %get-tuple-element.58), channel_id=1, source_target_pairs={{0,96},{32,0},{64,32},{96,64},{1,97},{33,1},{65,33},{97,65},{2,98}... | collective-permute-start | bytes 663560 | tf_op jit(solution)/shard_map/ppermute | solution.py:575
  147.8 10.1 %collective-permute-start.5 = (bf16[288,384]{1,0:T(8,128)(2,1)}, bf16[288,384]{1,0:T(8,128)(2,1)S(1)}, u32[]{:S(2)}, u32[]{:S(2)}) collective-permute-start(bf16[288,384]{1,0:T(8,128)(2,1)} %get-tuple-element.59), channel_id=1, source_target_pairs={{0,64},{32,96},{64,0},{96,32},{1,65},{33,97},{65,1},{97,33},{2,66}... | collective-permute-start | bytes 663560 | tf_op jit(solution)/shard_map/ppermute | solution.py:575
  150.1 13.4 %collective-permute-start.6 = (bf16[288,384]{1,0:T(8,128)(2,1)}, bf16[288,384]{1,0:T(8,128)(2,1)S(1)}, u32[]{:S(2)}, u32[]{:S(2)}) collective-permute-start(bf16[288,384]{1,0:T(8,128)(2,1)} %get-tuple-element.60), channel_id=1, source_target_pairs={{0,32},{32,64},{64,96},{96,0},{1,33},{33,65},{65,97},{97,1},{2,34}... | collective-permute-start | bytes 663560 | tf_op jit(solution)/shard_map/ppermute | solution.py:575
  157.2 6.2 %copy-start.2 = (bf16[288,384]{1,0:T(8,128)(2,1)}, bf16[288,384]{1,0:T(8,128)(2,1)S(1)}, u32[]{:S(2)}) copy-start(bf16[288,384]{1,0:T(8,128)(2,1)S(1)} %collective-permute-done.4.in1) | copy-start | bytes 663556
  157.9 5.6 %copy-start.3 = (bf16[288,384]{1,0:T(8,128)(2,1)}, bf16[288,384]{1,0:T(8,128)(2,1)S(1)}, u32[]{:S(2)}) copy-start(bf16[288,384]{1,0:T(8,128)(2,1)S(1)} %collective-permute-done.5.in2) | copy-start | bytes 663556
  163.5 0.7 copy-start.4
Sparse Core Ops, SparseCore 0:
  10.1 43.1 all-gather.2
  57.1 79.7 all-gather.4

commit v7 on v6

--- a/solution.py
+++ b/solution.py
@@ -31,27 +31,44 @@
     return pltpu.roll(block, HALF, 1)
 
 
-def pack_kernel(q_ref, k_ref, v_ref, g_ref, out_ref):
+def pack_kernel(me_ref, q_ref, k_ref, v_ref, g_ref, w_ref, out_ref, slice_ref, stage, rows):
     for frame in range(2):
         for pair, (first, second) in enumerate(((q_ref, k_ref), (v_ref, g_ref))):
-            rows = jnp.concatenate([first[frame], second[frame]], axis=0).astype(F32)
-            columns = rows.T
+            both = jnp.concatenate([first[frame], second[frame]], axis=0).astype(F32)
+            columns = both.T
             for head in range(HEADS):
                 out_ref[frame * HEADS + head, pair] = columns[
                     head * HDIM : (head + 1) * HDIM
                 ].astype(BF16)
 
-
-def pack(q, k, v, g):
+    eighth = me_ref[1]
+    rows[...] = w_ref[...].astype(F32)
+    stage[...] = jnp.zeros_like(stage)
+    tail = rows[256:288]
+    index = lax.broadcasted_iota(jnp.int32, tail.shape, 0)
+    for k in range(4):
+        at = slice(288 * k, 288 * (k + 1))
+        stage[0:8, at] = rows[pl.ds(pl.multiple_of(32 * eighth + 8 * k, 8), 8)]
+        stage[8:9, at] = jnp.sum(
+            jnp.where(index == 4 * eighth + k, tail, 0.0), axis=0, keepdims=True
+        )
+    slice_ref[...] = stage[...].astype(BF16)
+
+
+def pack(me, q, k, v, g, w):
     return pl.pallas_call(
         pack_kernel,
-        out_shape=jax.ShapeDtypeStruct((2 * HEADS, 2, HDIM, LANES), BF16),
-        in_specs=vmem_specs(4),
-        out_specs=pl.BlockSpec(memory_space=pltpu.VMEM),
+        out_shape=(
+            jax.ShapeDtypeStruct((2 * HEADS, 2, HDIM, LANES), BF16),
+            jax.ShapeDtypeStruct((16, 1152), BF16),
+        ),
+        in_specs=[pl.BlockSpec(memory_space=pltpu.SMEM)] + vmem_specs(5),
+        out_specs=tuple(vmem_specs(2)),
+        scratch_shapes=[pltpu.VMEM((16, 1152), F32), pltpu.VMEM((288, 288), F32)],
         compiler_params=pltpu.CompilerParams(vmem_limit_bytes=LIMIT),
         cost_estimate=SMALL,
         name="spatial_pack",
-    )(q, k, v, g)
+    )(me, q, k, v, g, w)
 
 
 def attend_kernel(
@@ -219,7 +236,7 @@
     )
 
 
-def send_pack_kernel(me_ref, q_ref, k_ref, v_ref, out0, out1, out2, out3, held):
+def send_pack_kernel(me_ref, q_ref, k_ref, v_ref, g_ref, out0, out1, out2, out3, held):
     for part, ref in enumerate((q_ref, k_ref, v_ref)):
         rows = jnp.concatenate([ref[0], ref[1]], axis=0).astype(F32)
         columns = rows.T.astype(BF16)
@@ -229,22 +246,33 @@
         held[2, :, at] = columns[576:864]
         held[3, :, at] = columns[864:]
     me = me_ref[0]
+    grads = jnp.concatenate([g_ref[0], g_ref[1]], axis=0)
     for shift, out in enumerate((out0, out1, out2, out3)):
-        out[...] = held[lax.rem(me + shift, 4)]
-
-
-def send_pack(me, q, k, v):
-    shape = jax.ShapeDtypeStruct((288, 3 * LANES), BF16)
+        out[:288] = held[lax.rem(me + shift, 4)]
+        for third in range(3):
+            out[288 + LANES * third : 288 + LANES * (third + 1)] = grads[
+                :, 384 * third : 384 * (third + 1)
+            ]
+
+
+def send_pack(me, q, k, v, g):
+    shape = jax.ShapeDtypeStruct((672, 3 * LANES), BF16)
     return pl.pallas_call(
         send_pack_kernel,
         out_shape=(shape,) * 4,
-        in_specs=[pl.BlockSpec(memory_space=pltpu.SMEM)] + vmem_specs(3),
+        in_specs=[pl.BlockSpec(memory_space=pltpu.SMEM)] + vmem_specs(4),
         out_specs=tuple(vmem_specs(4)),
         scratch_shapes=[pltpu.VMEM((4, 288, 3 * LANES), BF16)],
         compiler_params=pltpu.CompilerParams(vmem_limit_bytes=LIMIT),
         cost_estimate=LARGE,
         name="temporal_pack",
-    )(me, q, k, v)
+    )(me, q, k, v, g)
+
+
+def piece_grads(ref):
+    return jnp.concatenate(
+        [ref[288 + LANES * third : 288 + LANES * (third + 1)] for third in range(3)], axis=1
+    )
 
 
 def rows_of(values):
@@ -275,9 +303,9 @@
     return out
 
 
-def tout_kernel(me_ref, in0, in1, in2, in3, out_ref, wide, total):
+def partial_kernel(me_ref, in0, in1, in2, in3, keep_ref, send_ref, wide, tout, full, *, scale):
     for shift, ref in enumerate((in0, in1, in2, in3)):
-        wide[shift] = ref[...].astype(F32)
+        wide[shift] = ref[:288].astype(F32)
 
     def body(head, _):
         queries = head_rows(wide, head, 0)
@@ -288,76 +316,40 @@
             out = weights[0:1] * values[0]
             for j in range(1, 8):
                 out = out + weights[j : j + 1] * values[j]
-            total[shift, pl.ds(pl.multiple_of(head * HDIM, 8), HDIM)] = out
+            tout[shift, pl.ds(pl.multiple_of(head * HDIM, 8), HDIM)] = out
         return 0
 
     lax.fori_loop(0, 4, body, 0)
-    me = me_ref[0]
-    for shift in range(4):
-        out_ref[lax.rem(me + 4 - shift, 4)] = total[shift].astype(BF16)
-
-
-def temporal_out(me, pieces):
-    return pl.pallas_call(
-        tout_kernel,
-        out_shape=jax.ShapeDtypeStruct((4, 288, LANES), BF16),
-        in_specs=[pl.BlockSpec(memory_space=pltpu.SMEM)] + vmem_specs(4),
-        out_specs=pl.BlockSpec(memory_space=pltpu.VMEM),
-        scratch_shapes=[
-            pltpu.VMEM((4, 288, 3 * LANES), F32),
-            pltpu.VMEM((4, 288, LANES), F32),
-        ],
-        compiler_params=pltpu.CompilerParams(vmem_limit_bytes=LIMIT),
-        cost_estimate=SMALL,
-        name="temporal_tout",
-    )(me, *pieces)
-
-
-def partial_kernel(
-    me_ref, tout_ref, grad_ref, w_ref, keep_ref, send_ref, slice_ref, full, stage, rows, *, scale
-):
-    total = jnp.dot(tout_ref[0], grad_ref[0], preferred_element_type=F32)
-    for a in range(1, 4):
-        total = total + jnp.dot(tout_ref[a], grad_ref[a], preferred_element_type=F32)
+    total = None
+    for shift, ref in enumerate((in0, in1, in2, in3)):
+        term = jnp.dot(tout[shift].astype(BF16), piece_grads(ref), preferred_element_type=F32)
+        total = term if total is None else total + term
     total = total * scale
     full[0] = total[:144]
     full[1] = total[144:]
-    core, eighth = me_ref[2], me_ref[1]
+    core = me_ref[2]
     keep_ref[...] = full[core]
     send_ref[...] = full[1 - core].astype(BF16)
 
-    rows[...] = w_ref[...].astype(F32)
-    stage[...] = jnp.zeros_like(stage)
-    tail = rows[256:288]
-    index = lax.broadcasted_iota(jnp.int32, tail.shape, 0)
-    for k in range(4):
-        at = slice(288 * k, 288 * (k + 1))
-        stage[0:8, at] = rows[pl.ds(pl.multiple_of(32 * eighth + 8 * k, 8), 8)]
-        stage[8:9, at] = jnp.sum(
-            jnp.where(index == 4 * eighth + k, tail, 0.0), axis=0, keepdims=True
-        )
-    slice_ref[...] = stage[...].astype(BF16)
-
-
-def weight_partial(me, tout, grads, w, scale):
+
+def weight_partial(me, pieces, scale):
     return pl.pallas_call(
         functools.partial(partial_kernel, scale=scale),
         out_shape=(
             jax.ShapeDtypeStruct((144, 1152), F32),
             jax.ShapeDtypeStruct((144, 1152), BF16),
-            jax.ShapeDtypeStruct((16, 1152), BF16),
         ),
-        in_specs=[pl.BlockSpec(memory_space=pltpu.SMEM)] + vmem_specs(3),
-        out_specs=tuple(vmem_specs(3)),
+        in_specs=[pl.BlockSpec(memory_space=pltpu.SMEM)] + vmem_specs(4),
+        out_specs=tuple(vmem_specs(2)),
         scratch_shapes=[
+            pltpu.VMEM((4, 288, 3 * LANES), F32),
+            pltpu.VMEM((4, 288, LANES), F32),
             pltpu.VMEM((2, 144, 1152), F32),
-            pltpu.VMEM((16, 1152), F32),
-            pltpu.VMEM((288, 288), F32),
         ],
         compiler_params=pltpu.CompilerParams(vmem_limit_bytes=LIMIT),
         cost_estimate=SMALL,
         name="weight_partial",
-    )(me, tout, grads, w)
+    )(me, *pieces)
 
 
 def weight_split_kernel(keep_ref, got_ref, out_ref, full, part):
@@ -426,9 +418,8 @@
 
 
 def temporal_kernel(
-    me_ref, in0, in1, in2, in3, grad_ref, w_ref, out0, out1, out2, out3, wide, back, full
+    in0, in1, in2, in3, w_ref, out0, out1, out2, out3, wide, back, full
 ):
-    me = me_ref[0]
     for d in range(4):
         for y in range(4):
             for c in range(2):
@@ -442,9 +433,8 @@
                     full[start : start + 1] = block[8:9, at]
     w = full[...].astype(BF16)
     for shift, ref in enumerate((in0, in1, in2, in3)):
-        wide[shift, :, : 3 * LANES] = ref[...].astype(F32)
-        grads = grad_ref[lax.rem(me + 4 - shift, 4)]
-        tgrad = rounded(jnp.dot(grads, w, preferred_element_type=F32))
+        wide[shift, :, : 3 * LANES] = ref[:288].astype(F32)
+        tgrad = rounded(jnp.dot(piece_grads(ref), w, preferred_element_type=F32))
         wide[shift, :, 3 * LANES :] = tgrad.T
     scale = 1.0 / math.sqrt(HDIM)
 
@@ -486,12 +476,12 @@
         out[...] = back[shift].astype(BF16)
 
 
-def temporal_back(me, pieces, grads, w):
+def temporal_back(pieces, w):
     shape = jax.ShapeDtypeStruct((288, 3 * LANES), BF16)
     return pl.pallas_call(
         temporal_kernel,
         out_shape=(shape,) * 4,
-        in_specs=[pl.BlockSpec(memory_space=pltpu.SMEM)] + vmem_specs(6),
+        in_specs=vmem_specs(5),
         out_specs=tuple(vmem_specs(4)),
         scratch_shapes=[
             pltpu.VMEM((4, 288, 4 * LANES), F32),
@@ -501,7 +491,7 @@
         compiler_params=pltpu.CompilerParams(vmem_limit_bytes=LIMIT),
         cost_estimate=LARGE,
         name="temporal_back",
-    )(me, *pieces, grads, w)
+    )(*pieces, w)
 
 
 def receive_kernel(me_ref, in0, in1, in2, in3, dq_ref, dk_ref, dv_ref, held):
@@ -548,20 +538,20 @@
     core = lax.axis_index("c")
     me = jnp.stack([lax.axis_index("tm"), 4 * core + lax.axis_index("y"), core])
     space = ("z", "y", "c")
-    grads = lax.all_gather(grad_out, "tm", axis=1, tiled=True).reshape(4, LANES, 1152)
-    packed = pack(q_spatial[0], k_spatial[0], v_spatial[0], grad_spatial[0])
-    packed, q, k, v = lax.optimization_barrier(
-        (packed, q_temporal[0], k_temporal[0], v_temporal[0])
+    packed, eighth = pack(
+        me, q_spatial[0], k_spatial[0], v_spatial[0], grad_spatial[0], w_tout
+    )
+    weight = lax.all_gather(eighth, ("dp", "y", "c"), axis=0, tiled=True).reshape(32, 16, 1152)
+    packed, q, k, v, g = lax.optimization_barrier(
+        (packed, q_temporal[0], k_temporal[0], v_temporal[0], grad_out[0])
     )
     received = lax.all_to_all(packed, space, split_axis=0, concat_axis=0, tiled=True)
 
-    sends = send_pack(me, q, k, v)
+    sends = send_pack(me, q, k, v, g)
     pieces = (sends[0],) + tuple(
         lax.ppermute(sends[shift], "tm", RING[shift - 1]) for shift in (1, 2, 3)
     )
-    tout = temporal_out(me, pieces)
-    keep, send, eighth = weight_partial(me, tout, grads, w_tout, 1.0 / math.sqrt(65536))
-    weight = lax.all_gather(eighth, ("dp", "y", "c"), axis=0, tiled=True).reshape(32, 16, 1152)
+    keep, send = weight_partial(me, pieces, 1.0 / math.sqrt(65536))
     blocks = weight_split(keep, lax.ppermute(send, "c", SWAP_CORE))
 
     received, blocks = lax.optimization_barrier((received, blocks))
@@ -570,7 +560,7 @@
     results, *pieces = lax.optimization_barrier((results,) + pieces)
     returned = lax.all_to_all(results, space, split_axis=0, concat_axis=0, tiled=True)
 
-    backs = temporal_back(me, pieces, grads, weight)
+    backs = temporal_back(pieces, weight)
     homes = (backs[0],) + tuple(
         lax.ppermute(backs[shift], "tm", RING_BACK[shift - 1]) for shift in (1, 2, 3)
     )

time: 177 us -> 167 us (0.944)
  waiting for transfers between devices: 52.1 us -> 44.3 us
    all_gather x1, waiting for transfers between devices: 19.3 us -> 0.02 us  [shards(): lax.all_gather(eighth, ('dp', 'y', 'c'), axis=0, tiled=True)]
    all_to_all x1, waiting for transfers between devices: 5.02 us -> 12.8 us  [shards(): lax.all_to_all(blocks, ('dp', 'z', 'y'), split_axis=0, concat_axis=0, til...]
    ppermute x3, waiting for transfers between devices: 12.6 us -> 19.9 us  [shards(): lax.ppermute(sends[shift], 'tm', RING[shift - 1])]
    pallas_call x3 -> x2, Pallas kernels: 11.9 us -> 8.83 us  [the longest x1 6.15 us: temporal_back(): pl.pallas_call(temporal_kernel, out_shape=(shape,) * 4, in_specs=vmem_spe...]
    all_gather x1 -> x0, waiting for transfers between devices: 2.4 us -> none  [shards(): lax.all_gather(grad_out, 'tm', axis=1, tiled=True).reshape(4, LANES, 1152)]
  transfers between devices with their start and end apart: 12 -> 11, of which waited for: 10 -> 8; matrix products, arithmetic and copies ran while one was open for 0% -> 0% of each run, Pallas kernels for 27% -> 27%
where the time goes in v7:
time: 167 us; the launch traced here: 166 us
  starting transfers between devices  54.6 us (33%)
  Pallas kernels  49.8 us (30%)
  waiting for transfers between devices  44.3 us (27%)
  between operations  14.1 us (8%)
  local copies, waits for them, and re-layouts  2.96 us (2%)
    pallas_call x1, Pallas kernels, attend(): pl.pallas_call(functools.partial(attend_kernel, step=step), out_shape=jax...  23.4 us
    ppermute x3, waiting for transfers between devices, shards(): lax.ppermute(sends[shift], 'tm', RING[shift - 1])  19.9 us
    all_to_all x1, starting transfers between devices, shards(): lax.all_to_all(blocks, ('dp', 'z', 'y'), split_axis=0, concat_axis=0, til...  15.1 us
    all_to_all x1, waiting for transfers between devices, shards(): lax.all_to_all(blocks, ('dp', 'z', 'y'), split_axis=0, concat_axis=0, til...  12.8 us
    all_to_all x1, starting transfers between devices, shards(): lax.all_to_all(packed, space, split_axis=0, concat_axis=0, tiled=True)  11.1 us
    ppermute x3, waiting for transfers between devices, shards(): lax.ppermute(backs[shift], 'tm', RING_BACK[shift - 1])  10.1 us
    ppermute x3, starting transfers between devices, shards(): lax.ppermute(sends[shift], 'tm', RING[shift - 1])  9.64 us
    ppermute x3, starting transfers between devices, shards(): lax.ppermute(backs[shift], 'tm', RING_BACK[shift - 1])  9.59 us
  transfers between devices with their start and end apart: 11, of which 8 were waited for; matrix products, arithmetic and copies ran while one was open for 0% of the time, Pallas kernels for 27%

profile of v7, /device:TPU:1, one launch (start us, length us, event | category | flops | bytes accessed | tf_op | source)
XLA Modules:
  0.0 166.5 jit_solution(17612984027385137941)
XLA Ops:
  7.2 0.7 pad_add_fusion.me_ref
  7.8 2.7 %spatial_pack.1 = (bf16[32,2,72,128]{3,2,1,0:T(8,128)(2,1)}, bf16[16,1152]{1,0:T(8,128)(2,1)}) custom-call(s32[3]{0:T(128)} %pad_add_fusion.me_ref, bf16[2,64,1152]{2,1,0:T(8,128)(2,1)} %bitcast.18, bf16[2,64,1152]{2,1,0:T(8,128)(2,1)} %bitcast.19, bf16[2,64,1152]{2,1,0:T(8,128)(2,1)} %bitcast.20, bf16[2,64,1152]{2,1,0:T(8,128)(2,1)} %bitcast.21, ...), custom_call_target="tpu_custom_call" | custom-call | flops 1000 | bytes 1000 | tf_op jit(solution)/shard_map/spatial_pack/pallas_call | solution.py:59
  10.5 11.1 %all-to-all-start = ((bf16[32,2,72,128]{3,2,1,0:T(8,128)(2,1)}), bf16[32,2,72,128]{3,2,1,0:T(8,128)(2,1)}, u32[]{:S(2)}, u32[]{:S(2)}) async-start(bf16[32,2,72,128]{3,2,1,0:T(8,128)(2,1)} %get-tuple-element.39), calls=%async_computation | async-start | bytes 2359296 | tf_op jit(solution)/shard_map/all_to_all | solution.py:548
  21.7 0.0 all-gather.2.cloned.1.call-start
  21.7 3.2 %temporal_pack.1 = (bf16[672,384]{1,0:T(8,128)(2,1)}, bf16[672,384]{1,0:T(8,128)(2,1)}, bf16[672,384]{1,0:T(8,128)(2,1)}, bf16[672,384]{1,0:T(8,128)(2,1)}) custom-call(s32[3]{0:T(128)} %pad_add_fusion.me_ref, bf16[2,64,1152]{2,1,0:T(8,128)(2,1)} %bitcast.23, bf16[2,64,1152]{2,1,0:T(8,128)(2,1)} %bitcast.24, bf16[2,64,1152]{2,1,0:T(8,128)(2,1)} %bitcast.25, ...), custom_call_target="tpu_custom_call" | custom-call | flops 999999995904 | bytes 100000000 | tf_op jit(solution)/shard_map/temporal_pack/pallas_call | solution.py:260
  24.9 2.2 %collective-permute-start = (bf16[672,384]{1,0:T(8,128)(2,1)}, bf16[672,384]{1,0:T(8,128)(2,1)S(1)}, u32[]{:S(2)}, u32[]{:S(2)}) collective-permute-start(bf16[672,384]{1,0:T(8,128)(2,1)} %get-tuple-element.45), channel_id=1, source_target_pairs={{0,32},{32,64},{64,96},{96,0},{1,33},{33,65},{65,97},{97,1},{2,34}... | collective-permute-start | bytes 1548296 | tf_op jit(solution)/shard_map/ppermute | solution.py:552
  27.1 4.4 %collective-permute-start.1 = (bf16[672,384]{1,0:T(8,128)(2,1)}, bf16[672,384]{1,0:T(8,128)(2,1)S(1)}, u32[]{:S(2)}, u32[]{:S(2)}) collective-permute-start(bf16[672,384]{1,0:T(8,128)(2,1)} %get-tuple-element.46), channel_id=1, source_target_pairs={{0,64},{32,96},{64,0},{96,32},{1,65},{33,97},{65,1},{97,33},{2,66}... | collective-permute-start | bytes 1548296 | tf_op jit(solution)/shard_map/ppermute | solution.py:552
  31.5 3.1 %collective-permute-start.2 = (bf16[672,384]{1,0:T(8,128)(2,1)}, bf16[672,384]{1,0:T(8,128)(2,1)S(1)}, u32[]{:S(2)}, u32[]{:S(2)}) collective-permute-start(bf16[672,384]{1,0:T(8,128)(2,1)} %get-tuple-element.47), channel_id=1, source_target_pairs={{0,96},{32,0},{64,32},{96,64},{1,97},{33,1},{65,33},{97,65},{2,98}... | collective-permute-start | bytes 1548296 | tf_op jit(solution)/shard_map/ppermute | solution.py:552
  34.5 0.0 all-gather.2.cloned.1.call-update
  34.6 6.6 %collective-permute-done.in1 = bf16[672,384]{1,0:T(8,128)(2,1)S(1)} collective-permute-done((bf16[672,384]{1,0:T(8,128)(2,1)}, bf16[672,384]{1,0:T(8,128)(2,1)S(1)}, u32[]{:S(2)}, u32[]{:S(2)}) %collective-permute-start) | collective-permute-done | bytes 516128 | tf_op jit(solution)/shard_map/ppermute | solution.py:552
  41.2 0.0 copy-start.1
  41.2 11.2 %collective-permute-done.1.in2 = bf16[672,384]{1,0:T(8,128)(2,1)S(1)} collective-permute-done((bf16[672,384]{1,0:T(8,128)(2,1)}, bf16[672,384]{1,0:T(8,128)(2,1)S(1)}, u32[]{:S(2)}, u32[]{:S(2)}) %collective-permute-start.1) | collective-permute-done | bytes 516128 | tf_op jit(solution)/shard_map/ppermute | solution.py:552
  52.4 0.0 copy-start.2
  52.4 2.1 %collective-permute-done.2.in3 = bf16[672,384]{1,0:T(8,128)(2,1)S(1)} collective-permute-done((bf16[672,384]{1,0:T(8,128)(2,1)}, bf16[672,384]{1,0:T(8,128)(2,1)S(1)}, u32[]{:S(2)}, u32[]{:S(2)}) %collective-permute-start.2) | collective-permute-done | bytes 516128 | tf_op jit(solution)/shard_map/ppermute | solution.py:552
  54.5 0.0 copy-start.3
  54.5 0.0 copy-done.1
  54.5 0.0 copy-done.2
  54.5 0.8 copy-done.3
  55.3 4.4 %weight_partial.1 = (f32[144,1152]{1,0:T(8,128)}, bf16[144,1152]{1,0:T(8,128)(2,1)}) custom-call(s32[3]{0:T(128)} %pad_add_fusion.me_ref, bf16[672,384]{1,0:T(8,128)(2,1)} %get-tuple-element.56.in0, bf16[672,384]{1,0:T(8,128)(2,1)} %copy-done.1, bf16[672,384]{1,0:T(8,128)(2,1)} %copy-done.2, bf16[672,384]{1,0:T(8,128)(2,1)} %copy-done.3), custom_call_target="tpu_custom_call" | custom-call | flops 1000 | bytes 1000 | tf_op jit(solution)/shard_map/weight_partial/pallas_call | solution.py:336
  59.7 3.3 %collective-permute-start.3 = (bf16[144,1152]{1,0:T(8,128)(2,1)}, bf16[144,1152]{1,0:T(8,128)(2,1)S(1)}, u32[]{:S(2)}, u32[]{:S(2)}) collective-permute-start(bf16[144,1152]{1,0:T(8,128)(2,1)} %get-tuple-element.49), channel_id=1, source_target_pairs={{0,1},{1,0},{2,3},{3,2},{4,5},{5,4},{6,7},{7,6},{8,9},{9,8},{10,11... | collective-permute-start | bytes 995336 | tf_op jit(solution)/shard_map/ppermute | solution.py:555
  63.0 1.4 collective-permute-done.3.got_ref
  64.5 0.0 copy-start.4
  64.5 0.7 copy-done.4
  65.2 2.4 %weight_split.1 = bf16[64,24,128]{2,1,0:T(8,128)(2,1)} custom-call(f32[144,1152]{1,0:T(8,128)} %get-tuple-element.48.keep_ref, bf16[144,1152]{1,0:T(8,128)(2,1)} %copy-done.4), custom_call_target="tpu_custom_call" | custom-call | flops 1000 | bytes 1000 | tf_op jit(solution)/shard_map/weight_split/pallas_call | solution.py:378
  67.6 0.0 all-to-all-done.in_ref
  67.6 15.1 %all-to-all-start.1 = ((bf16[64,24,128]{2,1,0:T(8,128)(2,1)}), bf16[64,24,128]{2,1,0:T(8,128)(2,1)S(1)}, u32[]{:S(2)}, u32[]{:S(2)}) async-start(bf16[64,24,128]{2,1,0:T(8,128)(2,1)} %weight_split.1), calls=%async_computation.1 | async-start | bytes 786432 | tf_op jit(solution)/shard_map/all_to_all | solution.py:558
  82.7 23.4 %spatial_attention.1.spatial_ref = bf16[32,112,128]{2,1,0:T(8,128)(2,1)} custom-call(bf16[32,2,72,128]{3,2,1,0:T(8,128)(2,1)} %all-to-all-done.in_ref), custom_call_target="tpu_custom_call" | custom-call | flops 10737418240 | bytes 2200000 | tf_op jit(solution)/shard_map/spatial_attention/pallas_call | solution.py:165
  106.1 12.8 %all-to-all-done.1.in_ref = bf16[64,24,128]{2,1,0:T(8,128)(2,1)S(1)} async-done(((bf16[64,24,128]{2,1,0:T(8,128)(2,1)}), bf16[64,24,128]{2,1,0:T(8,128)(2,1)S(1)}, u32[]{:S(2)}, u32[]{:S(2)}) %all-to-all-start.1) | async-done | bytes 393248 | tf_op jit(solution)/shard_map/all_to_all | solution.py:558
  118.9 0.0 copy-start
  118.9 0.7 copy-done
  119.6 2.4 %weight_join.1 = bf16[32,136,128]{2,1,0:T(8,128)(2,1)} custom-call(bf16[32,112,128]{2,1,0:T(8,128)(2,1)} %spatial_attention.1.spatial_ref, bf16[64,24,128]{2,1,0:T(8,128)(2,1)} %copy-done), custom_call_target="tpu_custom_call" | custom-call | flops 1000 | bytes 1000 | tf_op jit(solution)/shard_map/weight_join/pallas_call | solution.py:409
  122.0 5.8 %all-to-all-start.2 = ((bf16[32,136,128]{2,1,0:T(8,128)(2,1)}), bf16[32,136,128]{2,1,0:T(8,128)(2,1)}, u32[]{:S(2)}, u32[]{:S(2)}) async-start(bf16[32,136,128]{2,1,0:T(8,128)(2,1)} %weight_join.1), calls=%async_computation.2 | async-start | bytes 2228224 | tf_op jit(solution)/shard_map/all_to_all | solution.py:561
  127.8 0.0 all-gather.2.cloned.1.call-done
  127.9 6.1 %temporal_back.1 = (bf16[288,384]{1,0:T(8,128)(2,1)}, bf16[288,384]{1,0:T(8,128)(2,1)}, bf16[288,384]{1,0:T(8,128)(2,1)}, bf16[288,384]{1,0:T(8,128)(2,1)}) custom-call(bf16[672,384]{1,0:T(8,128)(2,1)} %get-tuple-element.56.in0, bf16[672,384]{1,0:T(8,128)(2,1)} %copy-done.1, bf16[672,384]{1,0:T(8,128)(2,1)} %copy-done.2, bf16[672,384]{1,0:T(8,128)(2,1)} %copy-done.3, ...), custom_call_target="tpu_custom_call" | custom-call | flops 999999995904 | bytes 100000000 | tf_op jit(solution)/shard_map/temporal_back/pallas_call | solution.py:481
  134.0 4.2 %collective-permute-start.4 = (bf16[288,384]{1,0:T(8,128)(2,1)}, bf16[288,384]{1,0:T(8,128)(2,1)S(1)}, u32[]{:S(2)}, u32[]{:S(2)}) collective-permute-start(bf16[288,384]{1,0:T(8,128)(2,1)} %get-tuple-element.62), channel_id=1, source_target_pairs={{0,96},{32,0},{64,32},{96,64},{1,97},{33,1},{65,33},{97,65},{2,98}... | collective-permute-start | bytes 663560 | tf_op jit(solution)/shard_map/ppermute | solution.py:565
  138.2 3.4 %collective-permute-start.5 = (bf16[288,384]{1,0:T(8,128)(2,1)}, bf16[288,384]{1,0:T(8,128)(2,1)S(1)}, u32[]{:S(2)}, u32[]{:S(2)}) collective-permute-start(bf16[288,384]{1,0:T(8,128)(2,1)} %get-tuple-element.63), channel_id=1, source_target_pairs={{0,64},{32,96},{64,0},{96,32},{1,65},{33,97},{65,1},{97,33},{2,66}... | collective-permute-start | bytes 663560 | tf_op jit(solution)/shard_map/ppermute | solution.py:565
  141.7 1.9 %collective-permute-start.6 = (bf16[288,384]{1,0:T(8,128)(2,1)}, bf16[288,384]{1,0:T(8,128)(2,1)S(1)}, u32[]{:S(2)}, u32[]{:S(2)}) collective-permute-start(bf16[288,384]{1,0:T(8,128)(2,1)} %get-tuple-element.64), channel_id=1, source_target_pairs={{0,32},{32,64},{64,96},{96,0},{1,33},{33,65},{65,97},{97,1},{2,34}... | collective-permute-start | bytes 663560 | tf_op jit(solution)/shard_map/ppermute | solution.py:565
  143.6 0.3 collective-permute-done.4.in1
  143.9 0.0 copy-start.5
  143.9 4.5 %collective-permute-done.5.in2 = bf16[288,384]{1,0:T(8,128)(2,1)S(1)} collective-permute-done((bf16[288,384]{1,0:T(8,128)(2,1)}, bf16[288,384]{1,0:T(8,128)(2,1)S(1)}, u32[]{:S(2)}, u32[]{:S(2)}) %collective-permute-start.5) | collective-permute-done | bytes 221216 | tf_op jit(solution)/shard_map/ppermute | solution.py:565
  148.4 0.0 copy-start.6
  148.4 5.4 %collective-permute-done.6.in3 = bf16[288,384]{1,0:T(8,128)(2,1)S(1)} collective-permute-done((bf16[288,384]{1,0:T(8,128)(2,1)}, bf16[288,384]{1,0:T(8,128)(2,1)S(1)}, u32[]{:S(2)}, u32[]{:S(2)}) %collective-permute-start.6) | collective-permute-done | bytes 221216 | tf_op jit(solution)/shard_map/ppermute | solution.py:565
  153.7 0.0 copy-start.7
  153.7 0.0 copy-done.5
  153.7 0.0 copy-done.6
  153.7 0.7 copy-done.7
  154.4 2.5 %temporal_unpack.1 = (bf16[2,64,1152]{2,1,0:T(8,128)(2,1)}, bf16[2,64,1152]{2,1,0:T(8,128)(2,1)}, bf16[2,64,1152]{2,1,0:T(8,128)(2,1)}) custom-call(s32[3]{0:T(128)} %pad_add_fusion.me_ref, bf16[288,384]{1,0:T(8,128)(2,1)} %get-tuple-element.61.in0, bf16[288,384]{1,0:T(8,128)(2,1)} %copy-done.5, bf16[288,384]{1,0:T(8,128)(2,1)} %copy-done.6, ...), custom_call_target="tpu_custom_call" | custom-call | tf_op jit(solution)/shard_map/temporal_unpack/pallas_call | solution.py:511
  156.9 0.0 all-to-all-done.2.in_ref
  156.9 2.7 %spatial_unpack.1 = (bf16[2,64,1152]{2,1,0:T(8,128)(2,1)}, bf16[2,64,1152]{2,1,0:T(8,128)(2,1)}, bf16[2,64,1152]{2,1,0:T(8,128)(2,1)}, f32[288,288]{1,0:T(8,128)}) custom-call(bf16[32,136,128]{2,1,0:T(8,128)(2,1)} %all-to-all-done.2.in_ref), custom_call_target="tpu_custom_call" | custom-call | tf_op jit(solution)/shard_map/spatial_unpack/pallas_call | solution.py:218
Async XLA Ops:
  10.5 57.1 %all-to-all-start = ((bf16[32,2,72,128]{3,2,1,0:T(8,128)(2,1)}), bf16[32,2,72,128]{3,2,1,0:T(8,128)(2,1)}, u32[]{:S(2)}, u32[]{:S(2)}) async-start(bf16[32,2,72,128]{3,2,1,0:T(8,128)(2,1)} %get-tuple-element.39), calls=%async_computation | async-start | bytes 2359296 | tf_op jit(solution)/shard_map/all_to_all | solution.py:548
  21.7 106.2 %all-gather.2.cloned.1.call-start = ((), (), s32[]{:S(2)}) async-start(), calls=%async_computation.3 | async-start | bytes 1216512 | tf_op jit(solution)/shard_map/all_gather | solution.py:544
  24.9 16.3 %collective-permute-start = (bf16[672,384]{1,0:T(8,128)(2,1)}, bf16[672,384]{1,0:T(8,128)(2,1)S(1)}, u32[]{:S(2)}, u32[]{:S(2)}) collective-permute-start(bf16[672,384]{1,0:T(8,128)(2,1)} %get-tuple-element.45), channel_id=1, source_target_pairs={{0,32},{32,64},{64,96},{96,0},{1,33},{33,65},{65,97},{97,1},{2,34}... | collective-permute-start | bytes 1548296 | tf_op jit(solution)/shard_map/ppermute | solution.py:552
  27.1 25.3 %collective-permute-start.1 = (bf16[672,384]{1,0:T(8,128)(2,1)}, bf16[672,384]{1,0:T(8,128)(2,1)S(1)}, u32[]{:S(2)}, u32[]{:S(2)}) collective-permute-start(bf16[672,384]{1,0:T(8,128)(2,1)} %get-tuple-element.46), channel_id=1, source_target_pairs={{0,64},{32,96},{64,0},{96,32},{1,65},{33,97},{65,1},{97,33},{2,66}... | collective-permute-start | bytes 1548296 | tf_op jit(solution)/shard_map/ppermute | solution.py:552
  31.5 23.0 %collective-permute-start.2 = (bf16[672,384]{1,0:T(8,128)(2,1)}, bf16[672,384]{1,0:T(8,128)(2,1)S(1)}, u32[]{:S(2)}, u32[]{:S(2)}) collective-permute-start(bf16[672,384]{1,0:T(8,128)(2,1)} %get-tuple-element.47), channel_id=1, source_target_pairs={{0,96},{32,0},{64,32},{96,64},{1,97},{33,1},{65,33},{97,65},{2,98}... | collective-permute-start | bytes 1548296 | tf_op jit(solution)/shard_map/ppermute | solution.py:552
  41.2 13.3 %copy-start.1 = (bf16[672,384]{1,0:T(8,128)(2,1)}, bf16[672,384]{1,0:T(8,128)(2,1)S(1)}, u32[]{:S(2)}) copy-start(bf16[672,384]{1,0:T(8,128)(2,1)S(1)} %collective-permute-done.in1) | copy-start | bytes 1548292
  52.4 2.1 %copy-start.2 = (bf16[672,384]{1,0:T(8,128)(2,1)}, bf16[672,384]{1,0:T(8,128)(2,1)S(1)}, u32[]{:S(2)}) copy-start(bf16[672,384]{1,0:T(8,128)(2,1)S(1)} %collective-permute-done.1.in2) | copy-start | bytes 1548292
  54.5 0.8 copy-start.3
  59.7 4.8 %collective-permute-start.3 = (bf16[144,1152]{1,0:T(8,128)(2,1)}, bf16[144,1152]{1,0:T(8,128)(2,1)S(1)}, u32[]{:S(2)}, u32[]{:S(2)}) collective-permute-start(bf16[144,1152]{1,0:T(8,128)(2,1)} %get-tuple-element.49), channel_id=1, source_target_pairs={{0,1},{1,0},{2,3},{3,2},{4,5},{5,4},{6,7},{7,6},{8,9},{9,8},{10,11... | collective-permute-start | bytes 995336 | tf_op jit(solution)/shard_map/ppermute | solution.py:555
  64.5 0.7 copy-start.4
  67.6 51.3 %all-to-all-start.1 = ((bf16[64,24,128]{2,1,0:T(8,128)(2,1)}), bf16[64,24,128]{2,1,0:T(8,128)(2,1)S(1)}, u32[]{:S(2)}, u32[]{:S(2)}) async-start(bf16[64,24,128]{2,1,0:T(8,128)(2,1)} %weight_split.1), calls=%async_computation.1 | async-start | bytes 786432 | tf_op jit(solution)/shard_map/all_to_all | solution.py:558
  118.9 0.7 copy-start
  122.0 34.8 %all-to-all-start.2 = ((bf16[32,136,128]{2,1,0:T(8,128)(2,1)}), bf16[32,136,128]{2,1,0:T(8,128)(2,1)}, u32[]{:S(2)}, u32[]{:S(2)}) async-start(bf16[32,136,128]{2,1,0:T(8,128)(2,1)} %weight_join.1), calls=%async_computation.2 | async-start | bytes 2228224 | tf_op jit(solution)/shard_map/all_to_all | solution.py:561
  134.0 9.9 %collective-permute-start.4 = (bf16[288,384]{1,0:T(8,128)(2,1)}, bf16[288,384]{1,0:T(8,128)(2,1)S(1)}, u32[]{:S(2)}, u32[]{:S(2)}) collective-permute-start(bf16[288,384]{1,0:T(8,128)(2,1)} %get-tuple-element.62), channel_id=1, source_target_pairs={{0,96},{32,0},{64,32},{96,64},{1,97},{33,1},{65,33},{97,65},{2,98}... | collective-permute-start | bytes 663560 | tf_op jit(solution)/shard_map/ppermute | solution.py:565
  138.2 10.1 %collective-permute-start.5 = (bf16[288,384]{1,0:T(8,128)(2,1)}, bf16[288,384]{1,0:T(8,128)(2,1)S(1)}, u32[]{:S(2)}, u32[]{:S(2)}) collective-permute-start(bf16[288,384]{1,0:T(8,128)(2,1)} %get-tuple-element.63), channel_id=1, source_target_pairs={{0,64},{32,96},{64,0},{96,32},{1,65},{33,97},{65,1},{97,33},{2,66}... | collective-permute-start | bytes 663560 | tf_op jit(solution)/shard_map/ppermute | solution.py:565
  141.7 12.0 %collective-permute-start.6 = (bf16[288,384]{1,0:T(8,128)(2,1)}, bf16[288,384]{1,0:T(8,128)(2,1)S(1)}, u32[]{:S(2)}, u32[]{:S(2)}) collective-permute-start(bf16[288,384]{1,0:T(8,128)(2,1)} %get-tuple-element.64), channel_id=1, source_target_pairs={{0,32},{32,64},{64,96},{96,0},{1,33},{33,65},{65,97},{97,1},{2,34}... | collective-permute-start | bytes 663560 | tf_op jit(solution)/shard_map/ppermute | solution.py:565
  143.9 9.9 %copy-start.5 = (bf16[288,384]{1,0:T(8,128)(2,1)}, bf16[288,384]{1,0:T(8,128)(2,1)S(1)}, u32[]{:S(2)}) copy-start(bf16[288,384]{1,0:T(8,128)(2,1)S(1)} %collective-permute-done.4.in1) | copy-start | bytes 663556
  148.4 5.4 %copy-start.6 = (bf16[288,384]{1,0:T(8,128)(2,1)}, bf16[288,384]{1,0:T(8,128)(2,1)S(1)}, u32[]{:S(2)}) copy-start(bf16[288,384]{1,0:T(8,128)(2,1)S(1)} %collective-permute-done.5.in2) | copy-start | bytes 663556
  153.7 0.7 copy-start.7
Sparse Core Ops, SparseCore 0:
  34.7 78.8 all-gather.1

commit v8 on v7

--- a/solution.py
+++ b/solution.py
@@ -11,6 +11,7 @@
 HDIM = 72
 LANES = 128
 HALF = 64
+CUTS = ((0, 40), (40, 80), (80, 112), (112, 144))
 FOLD = 40
 F32 = jnp.float32
 BF16 = jnp.bfloat16
@@ -31,7 +32,7 @@
     return pltpu.roll(block, HALF, 1)
 
 
-def pack_kernel(me_ref, q_ref, k_ref, v_ref, g_ref, w_ref, out_ref, slice_ref, stage, rows):
+def pack_kernel(me_ref, q_ref, k_ref, v_ref, g_ref, w_ref, out_ref, half_ref, stage, rows):
     for frame in range(2):
         for pair, (first, second) in enumerate(((q_ref, k_ref), (v_ref, g_ref))):
             both = jnp.concatenate([first[frame], second[frame]], axis=0).astype(F32)
@@ -41,18 +42,14 @@
                     head * HDIM : (head + 1) * HDIM
                 ].astype(BF16)
 
-    eighth = me_ref[1]
-    rows[...] = w_ref[...].astype(F32)
+    w = w_ref[...].astype(F32)
+    rows[0] = w[:144]
+    rows[1] = w[144:]
+    half = rows[me_ref[2]]
     stage[...] = jnp.zeros_like(stage)
-    tail = rows[256:288]
-    index = lax.broadcasted_iota(jnp.int32, tail.shape, 0)
-    for k in range(4):
-        at = slice(288 * k, 288 * (k + 1))
-        stage[0:8, at] = rows[pl.ds(pl.multiple_of(32 * eighth + 8 * k, 8), 8)]
-        stage[8:9, at] = jnp.sum(
-            jnp.where(index == 4 * eighth + k, tail, 0.0), axis=0, keepdims=True
-        )
-    slice_ref[...] = stage[...].astype(BF16)
+    for k, (start, end) in enumerate(CUTS):
+        stage[: end - start, 288 * k : 288 * (k + 1)] = half[start:end]
+    half_ref[...] = stage[...].astype(BF16)
 
 
 def pack(me, q, k, v, g, w):
@@ -60,11 +57,11 @@
         pack_kernel,
         out_shape=(
             jax.ShapeDtypeStruct((2 * HEADS, 2, HDIM, LANES), BF16),
-            jax.ShapeDtypeStruct((16, 1152), BF16),
+            jax.ShapeDtypeStruct((64, 1152), BF16),
         ),
         in_specs=[pl.BlockSpec(memory_space=pltpu.SMEM)] + vmem_specs(5),
         out_specs=tuple(vmem_specs(2)),
-        scratch_shapes=[pltpu.VMEM((16, 1152), F32), pltpu.VMEM((288, 288), F32)],
+        scratch_shapes=[pltpu.VMEM((64, 1152), F32), pltpu.VMEM((2, 144, 288), F32)],
         compiler_params=pltpu.CompilerParams(vmem_limit_bytes=LIMIT),
         cost_estimate=SMALL,
         name="spatial_pack",
@@ -420,17 +417,12 @@
 def temporal_kernel(
     in0, in1, in2, in3, w_ref, out0, out1, out2, out3, wide, back, full
 ):
-    for d in range(4):
-        for y in range(4):
-            for c in range(2):
-                block = w_ref[d * 8 + y * 2 + c].astype(F32)
-                eighth = 4 * c + y
-                for k in range(4):
-                    at = slice(288 * k, 288 * (k + 1))
-                    start = d * 288 + 32 * eighth + 8 * k
-                    full[start : start + 8] = block[0:8, at]
-                    start = d * 288 + 256 + 4 * eighth + k
-                    full[start : start + 1] = block[8:9, at]
+    for part in range(8):
+        block = w_ref[part].astype(F32)
+        for k, (start, end) in enumerate(CUTS):
+            full[part * 144 + start : part * 144 + end] = block[
+                : end - start, 288 * k : 288 * (k + 1)
+            ]
     w = full[...].astype(BF16)
     for shift, ref in enumerate((in0, in1, in2, in3)):
         wide[shift, :, : 3 * LANES] = ref[:288].astype(F32)
@@ -538,10 +530,10 @@
     core = lax.axis_index("c")
     me = jnp.stack([lax.axis_index("tm"), 4 * core + lax.axis_index("y"), core])
     space = ("z", "y", "c")
-    packed, eighth = pack(
+    packed, half = pack(
         me, q_spatial[0], k_spatial[0], v_spatial[0], grad_spatial[0], w_tout
     )
-    weight = lax.all_gather(eighth, ("dp", "y", "c"), axis=0, tiled=True).reshape(32, 16, 1152)
+    weight = lax.all_gather(half, ("dp", "c"), axis=0, tiled=True).reshape(8, 64, 1152)
     packed, q, k, v, g = lax.optimization_barrier(
         (packed, q_temporal[0], k_temporal[0], v_temporal[0], grad_out[0])
     )

time: 167 us -> 158 us (0.946)
  waiting for transfers between devices: 44.3 us -> 32.9 us
  starting transfers between devices: 54.6 us -> 56.5 us
    all_to_all x1, waiting for transfers between devices: 12.8 us -> 1.45 us  [shards(): lax.all_to_all(blocks, ('dp', 'z', 'y'), split_axis=0, concat_axis=0, til...]
    all_to_all x1, starting transfers between devices: 5.79 us -> 7.61 us  [shards(): lax.all_to_all(results, space, split_axis=0, concat_axis=0, tiled=True)]
  transfers between devices with their start and end apart: 11 -> 11, of which waited for: 8 -> 8; matrix products, arithmetic and copies ran while one was open for 0% -> 0% of each run, Pallas kernels for 27% -> 28%
where the time goes in v8:
time: 158 us; the launch traced here: 157 us
  starting transfers between devices  56.5 us (36%)
  Pallas kernels  49.6 us (31%)
  waiting for transfers between devices  32.9 us (21%)
  between operations  14.1 us (9%)
  local copies, waits for them, and re-layouts  2.96 us (2%)
    pallas_call x1, Pallas kernels, attend(): pl.pallas_call(functools.partial(attend_kernel, step=step), out_shape=jax...  23.5 us
    ppermute x3, waiting for transfers between devices, shards(): lax.ppermute(sends[shift], 'tm', RING[shift - 1])  19.9 us
    all_to_all x1, starting transfers between devices, shards(): lax.all_to_all(blocks, ('dp', 'z', 'y'), split_axis=0, concat_axis=0, til...  15.1 us
    all_to_all x1, starting transfers between devices, shards(): lax.all_to_all(packed, space, split_axis=0, concat_axis=0, tiled=True)  11.1 us
    ppermute x3, waiting for transfers between devices, shards(): lax.ppermute(backs[shift], 'tm', RING_BACK[shift - 1])  10.1 us
    ppermute x3, starting transfers between devices, shards(): lax.ppermute(sends[shift], 'tm', RING[shift - 1])  9.64 us
    ppermute x3, starting transfers between devices, shards(): lax.ppermute(backs[shift], 'tm', RING_BACK[shift - 1])  9.61 us
    all_to_all x1, starting transfers between devices, shards(): lax.all_to_all(results, space, split_axis=0, concat_axis=0, tiled=True)  7.61 us
  transfers between devices with their start and end apart: 11, of which 8 were waited for; matrix products, arithmetic and copies ran while one was open for 0% of the time, Pallas kernels for 28%

profile of v8, /device:TPU:1, one launch (start us, length us, event | category | flops | bytes accessed | tf_op | source)
XLA Modules:
  0.0 156.8 jit_solution(15415435816944676877)
XLA Ops:
  7.2 0.7 pad_add_fusion.me_ref
  7.8 2.7 %spatial_pack.1 = (bf16[32,2,72,128]{3,2,1,0:T(8,128)(2,1)}, bf16[64,1152]{1,0:T(8,128)(2,1)}) custom-call(s32[3]{0:T(128)} %pad_add_fusion.me_ref, bf16[2,64,1152]{2,1,0:T(8,128)(2,1)} %bitcast.18, bf16[2,64,1152]{2,1,0:T(8,128)(2,1)} %bitcast.19, bf16[2,64,1152]{2,1,0:T(8,128)(2,1)} %bitcast.20, bf16[2,64,1152]{2,1,0:T(8,128)(2,1)} %bitcast.21, ...), custom_call_target="tpu_custom_call" | custom-call | flops 1000 | bytes 1000 | tf_op jit(solution)/shard_map/spatial_pack/pallas_call | solution.py:56
  10.6 11.1 %all-to-all-start = ((bf16[32,2,72,128]{3,2,1,0:T(8,128)(2,1)}), bf16[32,2,72,128]{3,2,1,0:T(8,128)(2,1)}, u32[]{:S(2)}, u32[]{:S(2)}) async-start(bf16[32,2,72,128]{3,2,1,0:T(8,128)(2,1)} %get-tuple-element.39), calls=%async_computation | async-start | bytes 2359296 | tf_op jit(solution)/shard_map/all_to_all | solution.py:540
  21.7 0.0 all-gather.2.cloned.1.call-start
  21.8 3.2 %temporal_pack.1 = (bf16[672,384]{1,0:T(8,128)(2,1)}, bf16[672,384]{1,0:T(8,128)(2,1)}, bf16[672,384]{1,0:T(8,128)(2,1)}, bf16[672,384]{1,0:T(8,128)(2,1)}) custom-call(s32[3]{0:T(128)} %pad_add_fusion.me_ref, bf16[2,64,1152]{2,1,0:T(8,128)(2,1)} %bitcast.23, bf16[2,64,1152]{2,1,0:T(8,128)(2,1)} %bitcast.24, bf16[2,64,1152]{2,1,0:T(8,128)(2,1)} %bitcast.25, ...), custom_call_target="tpu_custom_call" | custom-call | flops 999999995904 | bytes 100000000 | tf_op jit(solution)/shard_map/temporal_pack/pallas_call | solution.py:257
  24.9 2.2 %collective-permute-start = (bf16[672,384]{1,0:T(8,128)(2,1)}, bf16[672,384]{1,0:T(8,128)(2,1)S(1)}, u32[]{:S(2)}, u32[]{:S(2)}) collective-permute-start(bf16[672,384]{1,0:T(8,128)(2,1)} %get-tuple-element.45), channel_id=1, source_target_pairs={{0,32},{32,64},{64,96},{96,0},{1,33},{33,65},{65,97},{97,1},{2,34}... | collective-permute-start | bytes 1548296 | tf_op jit(solution)/shard_map/ppermute | solution.py:544
  27.1 4.4 %collective-permute-start.1 = (bf16[672,384]{1,0:T(8,128)(2,1)}, bf16[672,384]{1,0:T(8,128)(2,1)S(1)}, u32[]{:S(2)}, u32[]{:S(2)}) collective-permute-start(bf16[672,384]{1,0:T(8,128)(2,1)} %get-tuple-element.46), channel_id=1, source_target_pairs={{0,64},{32,96},{64,0},{96,32},{1,65},{33,97},{65,1},{97,33},{2,66}... | collective-permute-start | bytes 1548296 | tf_op jit(solution)/shard_map/ppermute | solution.py:544
  31.5 3.1 %collective-permute-start.2 = (bf16[672,384]{1,0:T(8,128)(2,1)}, bf16[672,384]{1,0:T(8,128)(2,1)S(1)}, u32[]{:S(2)}, u32[]{:S(2)}) collective-permute-start(bf16[672,384]{1,0:T(8,128)(2,1)} %get-tuple-element.47), channel_id=1, source_target_pairs={{0,96},{32,0},{64,32},{96,64},{1,97},{33,1},{65,33},{97,65},{2,98}... | collective-permute-start | bytes 1548296 | tf_op jit(solution)/shard_map/ppermute | solution.py:544
  34.6 0.0 all-gather.2.cloned.1.call-update
  34.6 6.6 %collective-permute-done.in1 = bf16[672,384]{1,0:T(8,128)(2,1)S(1)} collective-permute-done((bf16[672,384]{1,0:T(8,128)(2,1)}, bf16[672,384]{1,0:T(8,128)(2,1)S(1)}, u32[]{:S(2)}, u32[]{:S(2)}) %collective-permute-start) | collective-permute-done | bytes 516128 | tf_op jit(solution)/shard_map/ppermute | solution.py:544
  41.2 0.0 copy-start.1
  41.2 11.2 %collective-permute-done.1.in2 = bf16[672,384]{1,0:T(8,128)(2,1)S(1)} collective-permute-done((bf16[672,384]{1,0:T(8,128)(2,1)}, bf16[672,384]{1,0:T(8,128)(2,1)S(1)}, u32[]{:S(2)}, u32[]{:S(2)}) %collective-permute-start.1) | collective-permute-done | bytes 516128 | tf_op jit(solution)/shard_map/ppermute | solution.py:544
  52.4 0.0 copy-start.2
  52.4 2.1 %collective-permute-done.2.in3 = bf16[672,384]{1,0:T(8,128)(2,1)S(1)} collective-permute-done((bf16[672,384]{1,0:T(8,128)(2,1)}, bf16[672,384]{1,0:T(8,128)(2,1)S(1)}, u32[]{:S(2)}, u32[]{:S(2)}) %collective-permute-start.2) | collective-permute-done | bytes 516128 | tf_op jit(solution)/shard_map/ppermute | solution.py:544
  54.5 0.0 copy-start.3
  54.5 0.0 copy-done.1
  54.5 0.0 copy-done.2
  54.5 0.8 copy-done.3
  55.3 4.4 %weight_partial.1 = (f32[144,1152]{1,0:T(8,128)}, bf16[144,1152]{1,0:T(8,128)(2,1)}) custom-call(s32[3]{0:T(128)} %pad_add_fusion.me_ref, bf16[672,384]{1,0:T(8,128)(2,1)} %get-tuple-element.56.in0, bf16[672,384]{1,0:T(8,128)(2,1)} %copy-done.1, bf16[672,384]{1,0:T(8,128)(2,1)} %copy-done.2, bf16[672,384]{1,0:T(8,128)(2,1)} %copy-done.3), custom_call_target="tpu_custom_call" | custom-call | flops 1000 | bytes 1000 | tf_op jit(solution)/shard_map/weight_partial/pallas_call | solution.py:333
  59.7 3.3 %collective-permute-start.3 = (bf16[144,1152]{1,0:T(8,128)(2,1)}, bf16[144,1152]{1,0:T(8,128)(2,1)S(1)}, u32[]{:S(2)}, u32[]{:S(2)}) collective-permute-start(bf16[144,1152]{1,0:T(8,128)(2,1)} %get-tuple-element.49), channel_id=1, source_target_pairs={{0,1},{1,0},{2,3},{3,2},{4,5},{5,4},{6,7},{7,6},{8,9},{9,8},{10,11... | collective-permute-start | bytes 995336 | tf_op jit(solution)/shard_map/ppermute | solution.py:547
  63.1 1.4 collective-permute-done.3.got_ref
  64.5 0.0 copy-start.4
  64.5 0.7 copy-done.4
  65.3 2.4 %weight_split.1 = bf16[64,24,128]{2,1,0:T(8,128)(2,1)} custom-call(f32[144,1152]{1,0:T(8,128)} %get-tuple-element.48.keep_ref, bf16[144,1152]{1,0:T(8,128)(2,1)} %copy-done.4), custom_call_target="tpu_custom_call" | custom-call | flops 1000 | bytes 1000 | tf_op jit(solution)/shard_map/weight_split/pallas_call | solution.py:375
  67.6 0.0 all-to-all-done.in_ref
  67.6 15.1 %all-to-all-start.1 = ((bf16[64,24,128]{2,1,0:T(8,128)(2,1)}), bf16[64,24,128]{2,1,0:T(8,128)(2,1)S(1)}, u32[]{:S(2)}, u32[]{:S(2)}) async-start(bf16[64,24,128]{2,1,0:T(8,128)(2,1)} %weight_split.1), calls=%async_computation.1 | async-start | bytes 786432 | tf_op jit(solution)/shard_map/all_to_all | solution.py:550
  82.7 23.5 %spatial_attention.1.spatial_ref = bf16[32,112,128]{2,1,0:T(8,128)(2,1)} custom-call(bf16[32,2,72,128]{3,2,1,0:T(8,128)(2,1)} %all-to-all-done.in_ref), custom_call_target="tpu_custom_call" | custom-call | flops 10737418240 | bytes 2200000 | tf_op jit(solution)/shard_map/spatial_attention/pallas_call | solution.py:162
  106.2 1.5 all-to-all-done.1.in_ref
  107.6 0.0 copy-start
  107.6 0.7 copy-done
  108.4 2.4 %weight_join.1 = bf16[32,136,128]{2,1,0:T(8,128)(2,1)} custom-call(bf16[32,112,128]{2,1,0:T(8,128)(2,1)} %spatial_attention.1.spatial_ref, bf16[64,24,128]{2,1,0:T(8,128)(2,1)} %copy-done), custom_call_target="tpu_custom_call" | custom-call | flops 1000 | bytes 1000 | tf_op jit(solution)/shard_map/weight_join/pallas_call | solution.py:406
  110.8 7.6 %all-to-all-start.2 = ((bf16[32,136,128]{2,1,0:T(8,128)(2,1)}), bf16[32,136,128]{2,1,0:T(8,128)(2,1)}, u32[]{:S(2)}, u32[]{:S(2)}) async-start(bf16[32,136,128]{2,1,0:T(8,128)(2,1)} %weight_join.1), calls=%async_computation.2 | async-start | bytes 2228224 | tf_op jit(solution)/shard_map/all_to_all | solution.py:553
  118.4 0.0 all-gather.2.cloned.1.call-done
  118.4 5.9 %temporal_back.1 = (bf16[288,384]{1,0:T(8,128)(2,1)}, bf16[288,384]{1,0:T(8,128)(2,1)}, bf16[288,384]{1,0:T(8,128)(2,1)}, bf16[288,384]{1,0:T(8,128)(2,1)}) custom-call(bf16[672,384]{1,0:T(8,128)(2,1)} %get-tuple-element.56.in0, bf16[672,384]{1,0:T(8,128)(2,1)} %copy-done.1, bf16[672,384]{1,0:T(8,128)(2,1)} %copy-done.2, bf16[672,384]{1,0:T(8,128)(2,1)} %copy-done.3, ...), custom_call_target="tpu_custom_call" | custom-call | flops 999999995904 | bytes 100000000 | tf_op jit(solution)/shard_map/temporal_back/pallas_call | solution.py:473
  124.4 4.2 %collective-permute-start.4 = (bf16[288,384]{1,0:T(8,128)(2,1)}, bf16[288,384]{1,0:T(8,128)(2,1)S(1)}, u32[]{:S(2)}, u32[]{:S(2)}) collective-permute-start(bf16[288,384]{1,0:T(8,128)(2,1)} %get-tuple-element.62), channel_id=1, source_target_pairs={{0,96},{32,0},{64,32},{96,64},{1,97},{33,1},{65,33},{97,65},{2,98}... | collective-permute-start | bytes 663560 | tf_op jit(solution)/shard_map/ppermute | solution.py:557
  128.6 3.5 %collective-permute-start.5 = (bf16[288,384]{1,0:T(8,128)(2,1)}, bf16[288,384]{1,0:T(8,128)(2,1)S(1)}, u32[]{:S(2)}, u32[]{:S(2)}) collective-permute-start(bf16[288,384]{1,0:T(8,128)(2,1)} %get-tuple-element.63), channel_id=1, source_target_pairs={{0,64},{32,96},{64,0},{96,32},{1,65},{33,97},{65,1},{97,33},{2,66}... | collective-permute-start | bytes 663560 | tf_op jit(solution)/shard_map/ppermute | solution.py:557
  132.1 1.9 %collective-permute-start.6 = (bf16[288,384]{1,0:T(8,128)(2,1)}, bf16[288,384]{1,0:T(8,128)(2,1)S(1)}, u32[]{:S(2)}, u32[]{:S(2)}) collective-permute-start(bf16[288,384]{1,0:T(8,128)(2,1)} %get-tuple-element.64), channel_id=1, source_target_pairs={{0,32},{32,64},{64,96},{96,0},{1,33},{33,65},{65,97},{97,1},{2,34}... | collective-permute-start | bytes 663560 | tf_op jit(solution)/shard_map/ppermute | solution.py:557
  134.0 0.3 collective-permute-done.4.in1
  134.2 0.0 copy-start.5
  134.2 4.5 %collective-permute-done.5.in2 = bf16[288,384]{1,0:T(8,128)(2,1)S(1)} collective-permute-done((bf16[288,384]{1,0:T(8,128)(2,1)}, bf16[288,384]{1,0:T(8,128)(2,1)S(1)}, u32[]{:S(2)}, u32[]{:S(2)}) %collective-permute-start.5) | collective-permute-done | bytes 221216 | tf_op jit(solution)/shard_map/ppermute | solution.py:557
  138.7 0.0 copy-start.6
  138.7 5.3 %collective-permute-done.6.in3 = bf16[288,384]{1,0:T(8,128)(2,1)S(1)} collective-permute-done((bf16[288,384]{1,0:T(8,128)(2,1)}, bf16[288,384]{1,0:T(8,128)(2,1)S(1)}, u32[]{:S(2)}, u32[]{:S(2)}) %collective-permute-start.6) | collective-permute-done | bytes 221216 | tf_op jit(solution)/shard_map/ppermute | solution.py:557
  144.1 0.0 copy-start.7
  144.1 0.0 copy-done.5
  144.1 0.0 copy-done.6
  144.1 0.7 copy-done.7
  144.8 2.5 %temporal_unpack.1 = (bf16[2,64,1152]{2,1,0:T(8,128)(2,1)}, bf16[2,64,1152]{2,1,0:T(8,128)(2,1)}, bf16[2,64,1152]{2,1,0:T(8,128)(2,1)}) custom-call(s32[3]{0:T(128)} %pad_add_fusion.me_ref, bf16[288,384]{1,0:T(8,128)(2,1)} %get-tuple-element.61.in0, bf16[288,384]{1,0:T(8,128)(2,1)} %copy-done.5, bf16[288,384]{1,0:T(8,128)(2,1)} %copy-done.6, ...), custom_call_target="tpu_custom_call" | custom-call | tf_op jit(solution)/shard_map/temporal_unpack/pallas_call | solution.py:503
  147.2 0.0 all-to-all-done.2.in_ref
  147.2 2.7 %spatial_unpack.1 = (bf16[2,64,1152]{2,1,0:T(8,128)(2,1)}, bf16[2,64,1152]{2,1,0:T(8,128)(2,1)}, bf16[2,64,1152]{2,1,0:T(8,128)(2,1)}, f32[288,288]{1,0:T(8,128)}) custom-call(bf16[32,136,128]{2,1,0:T(8,128)(2,1)} %all-to-all-done.2.in_ref), custom_call_target="tpu_custom_call" | custom-call | tf_op jit(solution)/shard_map/spatial_unpack/pallas_call | solution.py:215
Async XLA Ops:
  10.6 57.1 %all-to-all-start = ((bf16[32,2,72,128]{3,2,1,0:T(8,128)(2,1)}), bf16[32,2,72,128]{3,2,1,0:T(8,128)(2,1)}, u32[]{:S(2)}, u32[]{:S(2)}) async-start(bf16[32,2,72,128]{3,2,1,0:T(8,128)(2,1)} %get-tuple-element.39), calls=%async_computation | async-start | bytes 2359296 | tf_op jit(solution)/shard_map/all_to_all | solution.py:540
  21.7 96.7 %all-gather.2.cloned.1.call-start = ((), (), s32[]{:S(2)}) async-start(), calls=%async_computation.3 | async-start | bytes 1327104 | tf_op jit(solution)/shard_map/all_gather | solution.py:536
  24.9 16.3 %collective-permute-start = (bf16[672,384]{1,0:T(8,128)(2,1)}, bf16[672,384]{1,0:T(8,128)(2,1)S(1)}, u32[]{:S(2)}, u32[]{:S(2)}) collective-permute-start(bf16[672,384]{1,0:T(8,128)(2,1)} %get-tuple-element.45), channel_id=1, source_target_pairs={{0,32},{32,64},{64,96},{96,0},{1,33},{33,65},{65,97},{97,1},{2,34}... | collective-permute-start | bytes 1548296 | tf_op jit(solution)/shard_map/ppermute | solution.py:544
  27.1 25.3 %collective-permute-start.1 = (bf16[672,384]{1,0:T(8,128)(2,1)}, bf16[672,384]{1,0:T(8,128)(2,1)S(1)}, u32[]{:S(2)}, u32[]{:S(2)}) collective-permute-start(bf16[672,384]{1,0:T(8,128)(2,1)} %get-tuple-element.46), channel_id=1, source_target_pairs={{0,64},{32,96},{64,0},{96,32},{1,65},{33,97},{65,1},{97,33},{2,66}... | collective-permute-start | bytes 1548296 | tf_op jit(solution)/shard_map/ppermute | solution.py:544
  31.5 23.0 %collective-permute-start.2 = (bf16[672,384]{1,0:T(8,128)(2,1)}, bf16[672,384]{1,0:T(8,128)(2,1)S(1)}, u32[]{:S(2)}, u32[]{:S(2)}) collective-permute-start(bf16[672,384]{1,0:T(8,128)(2,1)} %get-tuple-element.47), channel_id=1, source_target_pairs={{0,96},{32,0},{64,32},{96,64},{1,97},{33,1},{65,33},{97,65},{2,98}... | collective-permute-start | bytes 1548296 | tf_op jit(solution)/shard_map/ppermute | solution.py:544
  41.2 13.3 %copy-start.1 = (bf16[672,384]{1,0:T(8,128)(2,1)}, bf16[672,384]{1,0:T(8,128)(2,1)S(1)}, u32[]{:S(2)}) copy-start(bf16[672,384]{1,0:T(8,128)(2,1)S(1)} %collective-permute-done.in1) | copy-start | bytes 1548292
  52.4 2.1 %copy-start.2 = (bf16[672,384]{1,0:T(8,128)(2,1)}, bf16[672,384]{1,0:T(8,128)(2,1)S(1)}, u32[]{:S(2)}) copy-start(bf16[672,384]{1,0:T(8,128)(2,1)S(1)} %collective-permute-done.1.in2) | copy-start | bytes 1548292
  54.5 0.8 copy-start.3
  59.7 4.8 %collective-permute-start.3 = (bf16[144,1152]{1,0:T(8,128)(2,1)}, bf16[144,1152]{1,0:T(8,128)(2,1)S(1)}, u32[]{:S(2)}, u32[]{:S(2)}) collective-permute-start(bf16[144,1152]{1,0:T(8,128)(2,1)} %get-tuple-element.49), channel_id=1, source_target_pairs={{0,1},{1,0},{2,3},{3,2},{4,5},{5,4},{6,7},{7,6},{8,9},{9,8},{10,11... | collective-permute-start | bytes 995336 | tf_op jit(solution)/shard_map/ppermute | solution.py:547
  64.5 0.7 copy-start.4
  67.6 40.0 %all-to-all-start.1 = ((bf16[64,24,128]{2,1,0:T(8,128)(2,1)}), bf16[64,24,128]{2,1,0:T(8,128)(2,1)S(1)}, u32[]{:S(2)}, u32[]{:S(2)}) async-start(bf16[64,24,128]{2,1,0:T(8,128)(2,1)} %weight_split.1), calls=%async_computation.1 | async-start | bytes 786432 | tf_op jit(solution)/shard_map/all_to_all | solution.py:550
  107.6 0.7 copy-start
  110.8 36.4 %all-to-all-start.2 = ((bf16[32,136,128]{2,1,0:T(8,128)(2,1)}), bf16[32,136,128]{2,1,0:T(8,128)(2,1)}, u32[]{:S(2)}, u32[]{:S(2)}) async-start(bf16[32,136,128]{2,1,0:T(8,128)(2,1)} %weight_join.1), calls=%async_computation.2 | async-start | bytes 2228224 | tf_op jit(solution)/shard_map/all_to_all | solution.py:553
  124.4 9.9 %collective-permute-start.4 = (bf16[288,384]{1,0:T(8,128)(2,1)}, bf16[288,384]{1,0:T(8,128)(2,1)S(1)}, u32[]{:S(2)}, u32[]{:S(2)}) collective-permute-start(bf16[288,384]{1,0:T(8,128)(2,1)} %get-tuple-element.62), channel_id=1, source_target_pairs={{0,96},{32,0},{64,32},{96,64},{1,97},{33,1},{65,33},{97,65},{2,98}... | collective-permute-start | bytes 663560 | tf_op jit(solution)/shard_map/ppermute | solution.py:557
  128.6 10.1 %collective-permute-start.5 = (bf16[288,384]{1,0:T(8,128)(2,1)}, bf16[288,384]{1,0:T(8,128)(2,1)S(1)}, u32[]{:S(2)}, u32[]{:S(2)}) collective-permute-start(bf16[288,384]{1,0:T(8,128)(2,1)} %get-tuple-element.63), channel_id=1, source_target_pairs={{0,64},{32,96},{64,0},{96,32},{1,65},{33,97},{65,1},{97,33},{2,66}... | collective-permute-start | bytes 663560 | tf_op jit(solution)/shard_map/ppermute | solution.py:557
  132.1 12.0 %collective-permute-start.6 = (bf16[288,384]{1,0:T(8,128)(2,1)}, bf16[288,384]{1,0:T(8,128)(2,1)S(1)}, u32[]{:S(2)}, u32[]{:S(2)}) collective-permute-start(bf16[288,384]{1,0:T(8,128)(2,1)} %get-tuple-element.64), channel_id=1, source_target_pairs={{0,32},{32,64},{64,96},{96,0},{1,33},{33,65},{65,97},{97,1},{2,34}... | collective-permute-start | bytes 663560 | tf_op jit(solution)/shard_map/ppermute | solution.py:557
  134.2 9.8 %copy-start.5 = (bf16[288,384]{1,0:T(8,128)(2,1)}, bf16[288,384]{1,0:T(8,128)(2,1)S(1)}, u32[]{:S(2)}) copy-start(bf16[288,384]{1,0:T(8,128)(2,1)S(1)} %collective-permute-done.4.in1) | copy-start | bytes 663556
  138.7 5.4 %copy-start.6 = (bf16[288,384]{1,0:T(8,128)(2,1)}, bf16[288,384]{1,0:T(8,128)(2,1)S(1)}, u32[]{:S(2)}) copy-start(bf16[288,384]{1,0:T(8,128)(2,1)S(1)} %collective-permute-done.5.in2) | copy-start | bytes 663556
  144.1 0.7 copy-start.7
Sparse Core Ops, SparseCore 0:
  34.7 49.5 all-gather.1
